TPU v7x, 512 devices: a whole 4x4x16 slice. The times are simulated.
512 devices in a mesh: bin: 32 (over y, x, core), pen: 16 (over z).
Axes of the slice: x: 4, y: 4, z: 16, core: 2. Of those that a mesh axis runs over, the one named last changes fastest.
Arguments:
- features: bfloat16 [1048576, 64], P(('bin', 'pen')), may hold values from -6 to 6
- positions: float32 [3, 1048576], P(None, ('bin', 'pen')), may hold values from 0 to 192, as said below
- home_cells: int32 [3, 1048576], P(None, ('bin', 'pen')), may hold values from 0 to 191, as said below
- neighbours: int32 [1048576, 16], P(('bin', 'pen')), may hold values from 0 to 26, as said below
- degrees: int32 [1048576], P(('bin', 'pen')), may hold values from 1 to 16
- lift_input: bfloat16 [64, 64], replicated, may hold values from -0.75 to 0.75
- kernel_first: float32 [3, 64], replicated, may hold values from -4 to 4
- kernel_bias: float32 [64], replicated, may hold values from -1 to 1
- kernel_second: bfloat16 [64, 64], replicated, may hold values from -0.75 to 0.75
- spectral_weights: bfloat16 [32, 32, 32, 64, 128], P(None, 'bin', 'pen'), may hold values from -6 to 6
- skip_weights: float32 [64, 64], replicated, may hold values from -0.75 to 0.75
- skip_bias: float32 [64], replicated, may hold values from -0.5 to 0.5
Outputs:
- latent_out: bfloat16 [128, 128, 192, 64], P('bin', 'pen')
Inputs may be any that keep to these rules, and one draw needn't show every extreme that they name: `neighbours`: each code k names the step (k // 9 - 1, (k // 3) % 3 - 1, k % 3 - 1) of the 3 x 3 x 3 cells around a point's home cell; slot 0 is 13, the home cell itself, and the other slots hold distinct codes other than 13. `home_cells`: row 0 is below 4, row 1 below 8, row 2 below 192. `positions`: each point lies in its home cell: the integer parts of its coordinates are that cell's global coordinates.
All inputs are finite; a program needn't handle non-finite values.
Results may differ from a plain program's by a relative error of at most 0.0037.
Values sent between devices are 32-bit elements; how exact they have to be, the bound alone decides.
No kernel may reach another device: no remote copies, remote signals or barrier semaphores. Data moves between devices by JAX's collectives and lax.ppermute only.
A program may use at most 128 MiB of HBM per device.

v0:
```python
import math

import jax
import jax.numpy as jnp
from jax import lax
from jax.sharding import PartitionSpec as P

NZ = 192
CX = 4
CY = 8


def passed_along(block, axis, distance):
    devices = range(lax.axis_size(axis))
    route = [(i - distance, i) for i in devices if i - distance in devices]
    return lax.ppermute(block, axis, route)


def dft_table(rows, length, count, signed):
    mode = jnp.arange(count, dtype=jnp.int32)
    if signed:
        mode = jnp.where(mode < count // 2, mode, mode - count)
    phase = rows[:, None] * mode[None, :] % length
    angle = phase.astype(jnp.float32) * (2.0 * math.pi / length)
    scale = 1.0 / math.sqrt(length)
    return (jnp.cos(angle) * scale, jnp.sin(angle) * scale)


def pair_messages(
    off_x, off_y, off_z, feat_rows, valid, kernel_first, kernel_bias, kernel_second, lift_input
):
    pre = (
        off_x[..., None] * kernel_first[0]
        + off_y[..., None] * kernel_first[1]
        + off_z[..., None] * kernel_first[2]
        + kernel_bias
    )
    hidden = jax.nn.gelu(pre).astype(jnp.bfloat16)
    count, slots_n, width = hidden.shape
    kernel = jnp.dot(
        hidden.reshape(count * slots_n, width), kernel_second, preferred_element_type=jnp.float32
    )
    kernel = kernel.reshape(count, slots_n, -1)
    values = jnp.dot(feat_rows, lift_input, preferred_element_type=jnp.float32)
    return kernel * values[:, None, :] * valid[..., None]


def invert_along(spec, cos_t, sin_t, form):
    real = spec[:, :, :, 0]
    imag = spec[:, :, :, 1]
    high = lax.Precision.HIGHEST
    out_re = jnp.einsum(form, real, cos_t, precision=high) - jnp.einsum(
        form, imag, sin_t, precision=high
    )
    out_im = jnp.einsum(form, imag, cos_t, precision=high) + jnp.einsum(
        form, real, sin_t, precision=high
    )
    return jnp.stack([out_re, out_im], axis=3)


def forward_along(spec, cos_t, sin_t, form):
    real = spec[:, :, :, 0]
    imag = spec[:, :, :, 1]
    high = lax.Precision.HIGHEST
    out_re = jnp.einsum(form, real, cos_t, precision=high) + jnp.einsum(
        form, imag, sin_t, precision=high
    )
    out_im = jnp.einsum(form, imag, cos_t, precision=high) - jnp.einsum(
        form, real, sin_t, precision=high
    )
    return jnp.stack([out_re, out_im], axis=3)


def per_device(
    features,
    positions,
    home_cells,
    neighbours,
    degrees,
    lift_input,
    kernel_first,
    kernel_bias,
    kernel_second,
    spectral_weights,
    skip_weights,
    skip_bias,
):
    high = lax.Precision.HIGHEST
    bins = lax.axis_size("bin")
    pens = lax.axis_size("pen")
    bin_index = lax.axis_index("bin")
    pen_index = lax.axis_index("pen")
    width_x = CX * bins
    width_y = CY * pens
    channels = lift_input.shape[1]
    modes = spectral_weights.shape[0]
    points = features.shape[0]
    block = min(points, 1024)
    span_x = CX + 2
    span_y = CY + 2
    slots = jnp.arange(neighbours.shape[1], dtype=jnp.int32)[None, :]

    def add_block(step, grid):
        start = (step * block).astype(jnp.int32)
        codes = lax.dynamic_slice_in_dim(neighbours, start, block, 0)
        feat_rows = lax.dynamic_slice_in_dim(features, start, block, 0)
        where = lax.dynamic_slice_in_dim(positions, start, block, 1)
        home = lax.dynamic_slice_in_dim(home_cells, start, block, 1)
        live = lax.dynamic_slice_in_dim(degrees, start, block, 0)
        cell_x = jnp.clip(bin_index * CX + home[0][:, None] + codes // 9 - 1, 0, width_x - 1)
        cell_y = jnp.clip(pen_index * CY + home[1][:, None] + codes // 3 % 3 - 1, 0, width_y - 1)
        cell_z = jnp.clip(home[2][:, None] + codes % 3 - 1, 0, NZ - 1)
        off_x = cell_x.astype(jnp.float32) + 0.5 - where[0][:, None]
        off_y = cell_y.astype(jnp.float32) + 0.5 - where[1][:, None]
        off_z = cell_z.astype(jnp.float32) + 0.5 - where[2][:, None]
        valid = (slots < live[:, None]).astype(jnp.float32)
        message = pair_messages(
            off_x,
            off_y,
            off_z,
            feat_rows,
            valid,
            kernel_first,
            kernel_bias,
            kernel_second,
            lift_input,
        )
        local = (
            (cell_x - bin_index * CX + 1) * span_y + (cell_y - pen_index * CY + 1)
        ) * NZ + cell_z
        return grid.at[local.reshape(-1)].add(message.reshape(-1, channels))

    grid = lax.fori_loop(
        0, points // block, add_block, jnp.zeros((span_x * span_y * NZ, channels), jnp.float32)
    )
    grid = grid.reshape(span_x, span_y, NZ, channels)
    from_below = passed_along(grid[CX + 1], "bin", 1)
    from_above = passed_along(grid[0], "bin", -1)
    inner = grid[1 : CX + 1]
    inner = inner.at[0].add(from_below).at[CX - 1].add(from_above)
    from_left = passed_along(inner[:, CY + 1], "pen", 1)
    from_right = passed_along(inner[:, 0], "pen", -1)
    latent = inner[:, 1 : CY + 1]
    latent = latent.at[:, 0].add(from_left).at[:, CY - 1].add(from_right)
    cos_z, sin_z = dft_table(jnp.arange(NZ, dtype=jnp.int32), NZ, modes, False)
    cos_y, sin_y = dft_table(jnp.arange(width_y, dtype=jnp.int32), width_y, modes, True)
    z_re = jnp.einsum("xyzc,zk->xykc", latent, cos_z, precision=high)
    z_im = -jnp.einsum("xyzc,zk->xykc", latent, sin_z, precision=high)
    z_spec = jnp.stack([z_re, z_im], axis=3)
    y_in = lax.all_to_all(z_spec, "pen", split_axis=2, concat_axis=1, tiled=True)
    y_spec = forward_along(y_in, cos_y, sin_y, "xykc,yj->xjkc")
    x_in = lax.all_to_all(y_spec, "bin", split_axis=1, concat_axis=0, tiled=True)
    cos_x, sin_x = dft_table(jnp.arange(width_x, dtype=jnp.int32), width_x, modes, True)
    x_spec = forward_along(x_in, cos_x, sin_x, "xykc,xj->jykc")
    weights = spectral_weights.astype(jnp.float32)
    real_w = jnp.einsum("abki,abkio->abko", x_spec[:, :, :, 0], weights, precision=high)
    imag_w = jnp.einsum("abki,abkio->abko", x_spec[:, :, :, 1], weights, precision=high)
    mix_re = real_w[..., :channels] - imag_w[..., channels:]
    mix_im = real_w[..., channels:] + imag_w[..., :channels]
    mixed = jnp.stack([mix_re, mix_im], axis=3)
    own_rows = bin_index * CX + jnp.arange(CX, dtype=jnp.int32)
    own_cos, own_sin = dft_table(own_rows, width_x, modes, True)
    y_back = invert_along(
        lax.all_gather(mixed, "bin", axis=1, tiled=True), own_cos, own_sin, "jykc,xj->xykc"
    )
    y_rows = invert_along(y_back, cos_y, sin_y, "xjkc,yj->xykc")
    z_back = lax.all_to_all(y_rows, "pen", split_axis=1, concat_axis=2, tiled=True)
    doubling = jnp.where(jnp.arange(modes) == 0, 1.0, 2.0).astype(jnp.float32)[:, None]
    spectral_part = jnp.einsum(
        "xykc,zk->xyzc", z_back[:, :, :, 0] * doubling, cos_z, precision=high
    ) - jnp.einsum("xykc,zk->xyzc", z_back[:, :, :, 1] * doubling, sin_z, precision=high)
    skip = jnp.einsum("xyzc,cd->xyzd", latent, skip_weights, precision=high)
    return jax.nn.gelu(spectral_part + skip + skip_bias).astype(jnp.bfloat16)


def solution(mesh):
    in_specs = (
        P(("bin", "pen"), None),
        P(None, ("bin", "pen")),
        P(None, ("bin", "pen")),
        P(("bin", "pen"), None),
        P(("bin", "pen")),
        P(),
        P(),
        P(),
        P(),
        P(None, "bin", "pen", None, None),
        P(),
        P(),
    )
    out_specs = P("bin", "pen", None, None)
    return jax.shard_map(
        per_device, mesh=mesh, in_specs=in_specs, out_specs=out_specs, check_vma=False
    )
```

profile of v0, /device:TPU:32, one launch (start us, length us, event | category | flops | bytes accessed | tf_op | source)
XLA Modules:
  0.0 468.3 jit_solution(8501826001774433996)
XLA Ops:
  7.5 2.8 broadcast_in_dim.45
  10.3 199.2 %while.21 = (s32[]{:T(128)}, f32[11520,64]{1,0:T(8,128)}, s32[]{:T(128)}, s32[3,2048]{1,0:T(4,128)}, s32[2048,16]{0,1:T(8,128)S(1)}, /*index=5*/s32[]{:T(128)}, ...) while((s32[]{:T(128)}, f32[11520,64]{1,0:T(8,128)}, ...), condition=%wide.region_2.3_spmd.clone, body=%wide.region_0.2_spmd.clone.sunk | while | flops 162891776 | bytes 27241264 | solution.py:133
  12.7 4.4 multiply_multiply_fusion.4
  17.1 8.1 %copy.187 = f32[1024,16,64]{2,1,0:T(8,128)} copy(f32[1024,16,64]{0,2,1:T(8,128)} %multiply_multiply_fusion.4) | data formatting | bytes 8388608 | tf_op jit(solution)/shard_map/while/body/eval_jaxpr/mul | solution.py:45
  25.9 84.0 %scatter_fusion = f32[11520,64]{1,0:T(8,128)} fusion(f32[11520,64]{1,0:T(8,128)} %get-tuple-element.709, s32[16384]{0:T(1024)S(1)} %bitcast.259, f32[16384,64]{1,0:T(8,128)} %bitcast.253), kind=kCustom, calls=%fused_computation.clone.clone.1 | custom fusion | flops 1048576 | bytes 12648448 | tf_op jit(solution)/shard_map/while/body/eval_jaxpr/scatter-add | solution.py:131
  112.3 4.4 multiply_multiply_fusion.4
  116.7 8.1 %copy.187 = f32[1024,16,64]{2,1,0:T(8,128)} copy(f32[1024,16,64]{0,2,1:T(8,128)} %multiply_multiply_fusion.4) | data formatting | bytes 8388608 | tf_op jit(solution)/shard_map/while/body/eval_jaxpr/mul | solution.py:45
  125.5 84.0 %scatter_fusion = f32[11520,64]{1,0:T(8,128)} fusion(f32[11520,64]{1,0:T(8,128)} %get-tuple-element.709, s32[16384]{0:T(1024)S(1)} %bitcast.259, f32[16384,64]{1,0:T(8,128)} %bitcast.253), kind=kCustom, calls=%fused_computation.clone.clone.1 | custom fusion | flops 1048576 | bytes 12648448 | tf_op jit(solution)/shard_map/while/body/eval_jaxpr/scatter-add | solution.py:131
  209.5 2.9 fusion.244
  212.5 2.4 copy.115
  214.9 2.6 collective-permute-start
  220.0 4.2 slice.269
  224.6 4.9 %copy.117 = f32[4,10,192,64]{2,3,0,1:T(8,128)} copy(f32[4,10,192,64]{3,2,1,0:T(8,128)} %bitcast.254) | data formatting | bytes 3932160 | tf_op jit(solution)/shard_map/slice | solution.py:139
  234.9 3.8 collective-permute-start.2
  240.5 4.6 collective-permute-start.3
  245.1 2.9 collective-permute-done.2
  249.2 2.3 collective-permute-done.3
  251.5 3.1 convolution_bitcast_fusion
  254.6 3.1 fusion.51
  259.3 2.7 reshape.430
  262.0 14.9 %all-to-all-start = ((f32[16,1,8192]{2,1,0:T(1,128)}), f32[16,1,8192]{2,1,0:T(1,128)}, u32[]{:S(2)}, u32[]{:S(2)}) async-start(f32[16,1,8192]{2,1,0:T(1,128)} %reshape.430), calls=%async_computation | async-start | bytes 1048576 | tf_op jit(solution)/shard_map/all_to_all | solution.py:150
  276.9 29.1 %all-to-all-done = f32[16,1,8192]{2,1,0:T(1,128)} async-done(((f32[16,1,8192]{2,1,0:T(1,128)}), f32[16,1,8192]{2,1,0:T(1,128)}, u32[]{:S(2)}, u32[]{:S(2)}) %all-to-all-start) | async-done | bytes 524320 | tf_op jit(solution)/shard_map/all_to_all | solution.py:150
  306.6 3.7 reduce.8
  310.2 2.4 reshape.431
  316.6 14.8 %all_to_all.54 = f32[32,1,1024]{2,1,0:T(1,128)S(1)} all-to-all(f32[32,1,1024]{2,1,0:T(1,128)S(1)} %reshape.432), channel_id=1, replica_groups=mesh['bin'=32,'pen'=16] {'bin'}, dimensions={0} | all-to-all | bytes 262144 | tf_op jit(solution)/shard_map/all_to_all | solution.py:152
  336.5 51.5 %all-gather.2.cloned.1.call-done = f32[32,32,2,2,64]{4,0,2,1,3:T(8,128)} async-done(((f32[32,1,2,2,64]{4,0,2,1,3:T(8,128)}), f32[32,32,2,2,64]{4,0,2,1,3:T(8,128)}) %all-gather.2.cloned.1.call-update) | async-done | bytes 1048592 | tf_op jit(solution)/shard_map/all_gather | solution.py:164
  398.9 3.1 reshape.434
  402.0 13.1 %all-to-all-start.2 = ((f32[16,1,8192]{2,1,0:T(1,128)}), f32[16,1,8192]{2,1,0:T(1,128)}, u32[]{:S(2)}, u32[]{:S(2)}) async-start(f32[16,1,8192]{2,1,0:T(1,128)} %reshape.434), calls=%async_computation.2 | async-start | bytes 1048576 | tf_op jit(solution)/shard_map/all_to_all | solution.py:167
  415.1 29.6 %all-to-all-done.2 = f32[16,1,8192]{2,1,0:T(1,128)} async-done(((f32[16,1,8192]{2,1,0:T(1,128)}), f32[16,1,8192]{2,1,0:T(1,128)}, u32[]{:S(2)}, u32[]{:S(2)}) %all-to-all-start.2) | async-done | bytes 524320 | tf_op jit(solution)/shard_map/all_to_all | solution.py:167
  444.8 3.7 reduce.10
  448.4 2.8 reshape.435
  457.1 3.9 fusion.49
  (101 shorter events, 45.9 us)
Async XLA Ops:
  6.5 327.3 %copy-start = (bf16[32,1,2,64,128]{4,3,2,1,0:T(8,128)(2,1)S(1)}, bf16[32,1,2,64,128]{4,3,2,1,0:T(8,128)(2,1)}, u32[]{:S(2)}) copy-start(bf16[32,1,2,64,128]{4,3,2,1,0:T(8,128)(2,1)} %param.31) | copy-start | bytes 3145732
  7.4 2.8 copy-start.2
  7.4 2.8 copy-start.3
  7.5 2.8 copy-start.4
  7.5 2.8 copy-start.5
  7.5 2.8 copy-start.7
  7.5 2.8 copy-start.9
  214.9 14.7 %collective-permute-start = (f32[10,192,64]{1,2,0:T(8,128)}, f32[10,192,64]{1,2,0:T(8,128)}, u32[]{:S(2)}, u32[]{:S(2)}) collective-permute-start(f32[10,192,64]{1,2,0:T(8,128)} %copy.115), channel_id=1, source_target_pairs={{0,16},{16,32},{32,48},{48,64},{64,80},{80,96},{96,112},{112,128},... | collective-permute-start | bytes 1474568 | tf_op jit(solution)/shard_map/ppermute | solution.py:16
  218.7 12.9 %collective-permute-start.1 = (f32[10,192,64]{1,2,0:T(8,128)}, f32[10,192,64]{1,2,0:T(8,128)}, u32[]{:S(2)}, u32[]{:S(2)}) collective-permute-start(f32[10,192,64]{1,2,0:T(8,128)} %copy.118), channel_id=1, source_target_pairs={{16,0},{32,16},{48,32},{64,48},{80,64},{96,80},{112,96},{128,112},... | collective-permute-start | bytes 1474568 | tf_op jit(solution)/shard_map/ppermute | solution.py:16
  234.9 13.1 %collective-permute-start.2 = (f32[4,192,64]{1,2,0:T(8,128)S(1)}, f32[4,192,64]{1,2,0:T(8,128)S(1)}, u32[]{:S(2)}, u32[]{:S(2)}) collective-permute-start(f32[4,192,64]{1,2,0:T(8,128)S(1)} %get-tuple-element.577), channel_id=1, source_target_pairs={{0,1},{1,2},{2,3},{3,4},{4,5},{5,6},{6,7},{7,8},{8,9},{9,10},{10,1... | collective-permute-start | bytes 589832 | tf_op jit(solution)/shard_map/ppermute | solution.py:16
  240.5 11.0 %collective-permute-start.3 = (f32[4,192,64]{1,2,0:T(8,128)S(1)}, f32[4,192,64]{1,2,0:T(8,128)S(1)}, u32[]{:S(2)}, u32[]{:S(2)}) collective-permute-start(f32[4,192,64]{1,2,0:T(8,128)S(1)} %get-tuple-element.576), channel_id=1, source_target_pairs={{1,0},{2,1},{3,2},{4,3},{5,4},{6,5},{7,6},{8,7},{9,8},{10,9},{11,1... | collective-permute-start | bytes 589832 | tf_op jit(solution)/shard_map/ppermute | solution.py:16
  262.0 44.0 %all-to-all-start = ((f32[16,1,8192]{2,1,0:T(1,128)}), f32[16,1,8192]{2,1,0:T(1,128)}, u32[]{:S(2)}, u32[]{:S(2)}) async-start(f32[16,1,8192]{2,1,0:T(1,128)} %reshape.430), calls=%async_computation | async-start | bytes 1048576 | tf_op jit(solution)/shard_map/all_to_all | solution.py:150
  276.9 111.1 %all-gather.2.cloned.1.call-start = ((), (), s32[]{:S(2)}) async-start(), calls=%async_computation.3 | async-start | bytes 2162688 | tf_op jit(solution)/shard_map/all_gather | solution.py:164
  388.0 4.6 copy-start.1
  402.0 42.7 %all-to-all-start.2 = ((f32[16,1,8192]{2,1,0:T(1,128)}), f32[16,1,8192]{2,1,0:T(1,128)}, u32[]{:S(2)}, u32[]{:S(2)}) async-start(f32[16,1,8192]{2,1,0:T(1,128)} %reshape.434), calls=%async_computation.2 | async-start | bytes 1048576 | tf_op jit(solution)/shard_map/all_to_all | solution.py:167
  453.1 4.0 copy-start.6
  453.1 4.0 copy-start.8
Sparse Core Ops, SparseCore 0:
  336.6 51.3 all-gather.1
where the time goes:
time: 476 us; the launch traced here: 468 us
  other arithmetic  186 us (39%)
  waiting for transfers between devices  115 us (24%)
  local copies, waits for them, and re-layouts  60.7 us (13%)
  starting transfers between devices  40.3 us (8%)
  matrix products  36.4 us (8%)
  blocking collectives  14.8 us (3%)
  between operations  14.3 us (3%)
    scatter-add x2, other arithmetic, add_block(): return grid.at[local.reshape(-1)].add(message.reshape(-1, channels))  168 us
    all_gather x1, waiting for transfers between devices, per_device(): lax.all_gather(mixed, 'bin', axis=1, tiled=True)  51.5 us
    all_to_all x1, waiting for transfers between devices, per_device(): lax.all_to_all(y_rows, 'pen', split_axis=1, concat_axis=2, tiled=True)  29.6 us
    all_to_all x1, waiting for transfers between devices, per_device(): lax.all_to_all(z_spec, 'pen', split_axis=2, concat_axis=1, tiled=True)  29.1 us
    mul x2, local copies, waits for them, and re-layouts, pair_messages(): return kernel * values[:, None, :] * valid[..., None]  16.2 us
    all_to_all x1, starting transfers between devices, per_device(): lax.all_to_all(z_spec, 'pen', split_axis=2, concat_axis=1, tiled=True)  14.9 us
    all_to_all x1, blocking collectives, per_device(): lax.all_to_all(y_spec, 'bin', split_axis=1, concat_axis=0, tiled=True)  14.8 us
    all_to_all x1, starting transfers between devices, per_device(): lax.all_to_all(y_rows, 'pen', split_axis=1, concat_axis=2, tiled=True)  13.1 us
  transfers between devices with their start and end apart: 7, of which 5 were waited for; matrix products, arithmetic and copies ran while one was open for 3% of the time, Pallas kernels for 0%

commit v1 on v0

v1 whole, which is shorter than its diff:
```python
import functools
import math

import jax
import jax.numpy as jnp
import numpy as np
from jax import lax
from jax.experimental import pallas as pl
from jax.experimental.pallas import tpu as pltpu
from jax.sharding import PartitionSpec as P

NZ = 192
CX = 4
CY = 8
PTS = 2048
CH = 64
MODES = 32
CHUNK = 256
SUB = 128
HALVES = 2 * CH

F32 = jnp.float32
BF16 = jnp.bfloat16
HIGH = lax.Precision.HIGHEST
LIMIT = pltpu.CompilerParams(vmem_limit_bytes=48 * 1024 * 1024)

NN = (((1,), (0,)), ((), ()))
NT = (((1,), (1,)), ((), ()))
TN = (((0,), (0,)), ((), ()))


def mm(a, b, dims=NN, precision=None):
    return lax.dot_general(a, b, dims, precision=precision, preferred_element_type=F32)


def gelu(x):
    inner = x * (0.7978845608028654 + 0.035677408136300125 * (x * x))
    half = 0.5 * x
    return half + half * jnp.tanh(inner)


def swap(x):
    return pltpu.roll(x, CH, 1)


def sign_row(shape):
    lane = lax.broadcasted_iota(jnp.int32, shape, 1)
    return jnp.where(lane < CH, 1.0, -1.0).astype(F32)


def tables(length, signed):
    mode = np.arange(MODES)
    if signed:
        mode = np.where(mode < MODES // 2, mode, mode - MODES)
    return mode


def angles(rows, length, signed):
    mode = tables(length, signed)
    phase = (np.asarray(rows)[:, None] * mode[None, :]) % length
    angle = phase * (2.0 * math.pi / length)
    scale = 1.0 / math.sqrt(length)
    return np.cos(angle) * scale, np.sin(angle) * scale


def z_forward_table():
    c, s = angles(np.arange(NZ), NZ, False)
    return np.concatenate([c.T, -s.T], axis=0).astype(np.float32)


def z_inverse_table():
    c, s = angles(np.arange(NZ), NZ, False)
    w = np.where(np.arange(MODES) == 0, 1.0, 2.0)[:, None]
    return np.concatenate([c.T * w, -s.T * w], axis=0).astype(np.float32)


def y_forward_tables(pens):
    length = CY * pens
    c, s = angles(np.arange(length), length, True)
    main = np.concatenate([c.T, s.T], axis=0)
    side = np.zeros((CX, 2, MODES, pens, CX, 2))
    for q in range(pens):
        for h in range(2):
            y = min(max(q * CY - 1 + h * (CY + 1), 0), length - 1)
            for x in range(CX):
                side[x, 0, :, q, x, h] = c[y]
                side[x, 1, :, q, x, h] = s[y]
    side = side.reshape(CX * 2 * MODES, pens * CX * 2)
    return main.astype(np.float32), side.astype(np.float32)


def y_inverse_table(pens):
    length = CY * pens
    c, s = angles(np.arange(length), length, True)
    return np.concatenate([c, s], axis=0).astype(np.float32)


def x_tables(bins):
    length = CX * bins
    c, s = angles(np.arange(length), length, True)
    fwd = np.zeros((2, 2, MODES, bins, 2, CX))
    inv = np.zeros((2, bins, 2, CX, 2, MODES))
    for k in range(2):
        fwd[0, k, :, :, k, :] = c.T.reshape(MODES, bins, CX)
        fwd[1, k, :, :, k, :] = s.T.reshape(MODES, bins, CX)
        inv[0, :, k, :, k, :] = c.reshape(bins, CX, MODES)
        inv[1, :, k, :, k, :] = s.reshape(bins, CX, MODES)
    fwd = fwd.reshape(4 * MODES, bins * 2 * CX)
    inv = inv.reshape(2 * bins * 2 * CX, 2 * MODES)
    return fwd.astype(np.float32), inv.astype(np.float32)


def pieces(x):
    hi = x.astype(BF16).astype(F32)
    rest = x - hi
    mid = rest.astype(BF16).astype(F32)
    return hi, mid, rest - mid


def lift_kernel(last, at, feat, pos, home, nbr, deg, lift, first, bias, second, tabz,
                own, ysides, xsides, spec, edge, grid, rank, data, mess):
    bin_index = at[0]
    pen_index = at[1]
    last_bin, last_pen = last
    hx = home[0:1, :]
    hy = home[1:2, :]
    hz = home[2:3, :]
    col = hx * CY + hy

    ids = lax.broadcasted_iota(jnp.int32, (CX * CY, PTS), 0)
    carry = jnp.sum(jnp.where(col < ids, 1.0, 0.0), axis=1, keepdims=True)
    tri = jnp.where(
        lax.broadcasted_iota(jnp.int32, (CHUNK, CHUNK), 0)
        < lax.broadcasted_iota(jnp.int32, (CHUNK, CHUNK), 1), 1.0, 0.0).astype(BF16)
    for blk in range(PTS // CHUNK):
        part = slice(blk * CHUNK, (blk + 1) * CHUNK)
        hot = jnp.where(col[:, part] == ids[:, part], 1.0, 0.0)
        ahead = mm(hot.astype(BF16), tri) + carry
        rank[0:1, part] = jnp.sum(hot * ahead, axis=0, keepdims=True).astype(jnp.int32)
        carry = carry + jnp.sum(hot, axis=1, keepdims=True)

    slot = lax.broadcasted_iota(jnp.int32, (16, PTS), 0)
    bits = jnp.sum(
        jnp.where(slot < deg[...], jnp.left_shift(1, nbr[...]), 0), axis=0, keepdims=True)
    code = lax.broadcasted_iota(jnp.int32, (32, PTS), 0)
    live = jnp.bitwise_and(jnp.right_shift(bits, code), 1).astype(F32)
    off_x = (hx + bin_index * CX).astype(F32) + 0.5 - pos[0:1, :]
    off_y = (hy + pen_index * CY).astype(F32) + 0.5 - pos[1:2, :]
    off_z = hz.astype(F32) + 0.5 - pos[2:3, :]
    rows = [*pieces(off_x), *pieces(off_y), *pieces(off_z), hz.astype(F32), col.astype(F32),
            jnp.zeros((5, PTS), F32)]
    data[0:64, :] = feat[...]
    data[64:80, :] = jnp.concatenate(rows, axis=0).astype(BF16)
    data[80:112, :] = live.astype(BF16)

    grid[...] = jnp.zeros_like(grid)

    taps = jnp.concatenate([first[...], bias[...], jnp.zeros((4, CH), F32)], axis=0)
    taps = jnp.concatenate([taps, jnp.zeros((8, 128 - CH), F32)], axis=1)
    taps = jnp.transpose(taps)
    k_x, k_y, k_z, k_b = (
        jnp.broadcast_to(taps[0:CH, j:j + 1], (CH, CHUNK)) for j in range(4))
    zero = jnp.zeros((CH, CH), F32)
    sec_t = jnp.transpose(second[...].astype(F32))
    quad = jnp.concatenate(
        [jnp.concatenate([sec_t if i == j else zero for j in range(4)], axis=1)
         for i in range(4)], axis=0).astype(BF16)
    lift_t = jnp.transpose(lift[...].astype(F32)).astype(BF16)
    z_ids = lax.broadcasted_iota(jnp.int32, (NZ, SUB), 0)

    def chunk(step, _):
        base = step * CHUNK
        want = lax.broadcasted_iota(jnp.int32, (CHUNK, PTS), 0) + base
        perm = jnp.where(rank[0:1, :] == want, 1.0, 0.0).astype(BF16)
        t = mm(data[...], perm, NT)
        values = mm(lift_t, t[0:64].astype(BF16))
        ox = t[64:65] + t[65:66] + t[66:67]
        oy = t[67:68] + t[68:69] + t[69:70]
        oz = t[70:71] + t[71:72] + t[72:73]
        hzs = t[73:74].astype(jnp.int32)
        cols = t[74:75].astype(jnp.int32)
        hxs = lax.shift_right_logical(cols, 3) + bin_index * CX
        hys = jnp.bitwise_and(cols, 7) + pen_index * CY

        def ends(g, last):
            return (jnp.where(g > 0, -1.0, 0.0), None, jnp.where(g < last, 1.0, 0.0))

        base_pre = k_x * ox + k_y * oy + k_z * oz + k_b
        ex = ends(hxs, last_bin)
        ey = ends(hys, last_pen)
        ez = ends(hzs, NZ - 1)
        pend = []

        def flush():
            while len(pend) < 4:
                pend.append((None, jnp.zeros((CH, CHUNK), BF16)))
            hid4 = jnp.concatenate([h for _, h in pend], axis=0)
            kern = mm(quad, hid4)
            for j, (where, _) in enumerate(pend):
                if where is None:
                    continue
                dx, dy, dz = where
                k = dx * 9 + dy * 3 + dz
                m = kern[j * CH:(j + 1) * CH] * (values * t[80 + k:81 + k])
                hi = m.astype(BF16)
                lo = (m - hi.astype(F32)).astype(BF16)
                r = (dx * 3 + dy) * CH
                for s in range(CHUNK // SUB):
                    cut = slice(s * SUB, (s + 1) * SUB)
                    mess[s, r:r + CH, dz * SUB:(dz + 1) * SUB] = hi[:, cut]
                    mess[s, r:r + CH, (3 + dz) * SUB:(4 + dz) * SUB] = lo[:, cut]
            pend.clear()

        for dx in range(3):
            pre_x = base_pre if ex[dx] is None else base_pre + ex[dx] * k_x
            for dy in range(3):
                pre_y = pre_x if ey[dy] is None else pre_x + ey[dy] * k_y
                for dz in range(3):
                    pre = pre_y if ez[dz] is None else pre_y + ez[dz] * k_z
                    pend.append(((dx, dy, dz), gelu(pre).astype(BF16)))
                    if len(pend) == 4:
                        flush()
        flush()

        for s in range(CHUNK // SUB):
            cut = slice(s * SUB, (s + 1) * SUB)
            c_row = cols[:, cut]
            h_row = hzs[:, cut]
            zs = (jnp.maximum(h_row - 1, 0), h_row, jnp.minimum(h_row + 1, NZ - 1))

            def column(c, _):
                mine = c_row == c
                hot = jnp.concatenate(
                    [jnp.where(z_ids == jnp.where(mine, z, -1), 1.0, 0.0).astype(BF16)
                     for z in zs], axis=1)
                hot = jnp.concatenate([hot, hot], axis=1)
                acc = mm(mess[s], hot, NT)
                cx = lax.shift_right_logical(c, 3)
                cy = jnp.bitwise_and(c, 7)
                for dx in range(3):
                    for dy in range(3):
                        r = (dx * 3 + dy) * CH
                        grid[cx + dx, cy + dy] += acc[r:r + CH]
                return 0

            lax.fori_loop(jnp.min(c_row), jnp.max(c_row) + 1, column, 0)
        return 0

    lax.fori_loop(0, PTS // CHUNK, chunk, 0)

    lane = lax.broadcasted_iota(jnp.int32, (MODES, HALVES), 1)
    table = tabz[...]
    for xi in range(CX + 2):
        for yp in range((CY + 2) // 2):
            pair = grid[xi, 2 * yp:2 * yp + 2].reshape(2 * CH, NZ)
            d = mm(table, pair, NT, HIGH)
            re, im = d[0:MODES], d[MODES:]
            out = (jnp.where(lane < CH, re, swap(im)), jnp.where(lane < CH, swap(re), im))
            for j in range(2):
                yi = 2 * yp + j
                row = CY if yi == 0 else (CY + 1 if yi == CY + 1 else yi - 1)
                if xi in (0, CX + 1):
                    e = 0 if xi == 0 else 1
                    edge[e, :, row, :] = out[j]
                    xsides[e, row] = grid[xi, yi]
                else:
                    x = xi - 1
                    if row < CY:
                        spec[:, x * CY + row, :] = out[j]
                        own[x * CY + row] = grid[xi, yi]
                    else:
                        spec[:, CX * CY + x * 2 + row - CY, :] = out[j]
                        ysides[row - CY, x] = grid[xi, yi]


def lift_points(at, last, feat, pos, home, nbr, deg, lift, first, bias, second):
    shapes = [
        jax.ShapeDtypeStruct((CX * CY, CH, NZ), F32),
        jax.ShapeDtypeStruct((2, CX, CH, NZ), F32),
        jax.ShapeDtypeStruct((2, CY + 2, CH, NZ), F32),
        jax.ShapeDtypeStruct((MODES, CX * (CY + 2), HALVES), F32),
        jax.ShapeDtypeStruct((2, MODES, CY + 2, HALVES), F32),
    ]
    return pl.pallas_call(
        functools.partial(lift_kernel, last),
        out_shape=shapes,
        in_specs=[pl.BlockSpec(memory_space=pltpu.SMEM)]
        + [pl.BlockSpec(memory_space=pltpu.VMEM)] * 10,
        out_specs=[pl.BlockSpec(memory_space=pltpu.VMEM)] * 5,
        scratch_shapes=[
            pltpu.VMEM((CX + 2, CY + 2, CH, NZ), F32),
            pltpu.VMEM((8, PTS), jnp.int32),
            pltpu.VMEM((112, PTS), BF16),
            pltpu.VMEM((CHUNK // SUB, 9 * CH, 6 * SUB), BF16),
        ],
        compiler_params=LIMIT,
        name="lift",
    )(at, feat, pos, home, nbr, deg, lift, first, bias, second, jnp.asarray(z_forward_table()))


def join_kernel(last, at, spec, edge, below, above, out):
    low = at[0] == 0
    top = at[0] == last
    n = CX * CY
    b = jnp.where(low, edge[0], below[...])
    a = jnp.where(top, edge[1], above[...])
    out[...] = spec[...]
    out[:, 0:CY] += b[:, 0:CY]
    out[:, n - CY:n] += a[:, 0:CY]
    out[:, n:n + 2] += b[:, CY:]
    out[:, n + 2 * CX - 2:n + 2 * CX] += a[:, CY:]


def y_kernel(last, at, r, main, side, ysides, xsides, below, above, out, yedge):
    sgn = sign_row((MODES, HALVES))
    n = CX * CY
    pens = r.shape[0]
    for kz in range(2):
        o = kz * (n + 2 * CX)
        halo = mm(side[...], r[:, o + n:o + n + 2 * CX, :].reshape(pens * 2 * CX, HALVES), NN, HIGH)
        for x in range(CX):
            rows = r[:, o + x * CY:o + (x + 1) * CY, :].reshape(pens * CY, HALVES)
            ab = mm(main[...], rows, NN, HIGH) + halo[x * 2 * MODES:(x + 1) * 2 * MODES]
            out[:, kz * CX + x, :] = ab[:MODES] + swap(ab[MODES:]) * sgn
    low = at[0] == 0
    top = at[0] == last
    yedge[...] = ysides[...]
    for h in range(2):
        yedge[h, 0] += jnp.where(low, xsides[0, CY + h], below[CY + h])
        yedge[h, CX - 1] += jnp.where(top, xsides[1, CY + h], above[CY + h])


def x_kernel(r, fwd, inv, w, out, lhs, res):
    rows = r.shape[0] * r.shape[1]
    modes = 2 * MODES
    sgn = sign_row((modes, HALVES))
    ab = mm(fwd[...], r[...].reshape(rows, HALVES), NN, HIGH)
    x = ab[:modes] + swap(ab[modes:]) * sgn
    parts = [*pieces(x), *pieces(swap(x))]
    lhs[...] = jnp.zeros_like(lhs)
    for j, p in enumerate(parts):
        lhs[:, j, :] = p
    for k in range(2):
        for j in range(MODES):
            m = k * MODES + j
            res[m] = mm(lhs[m][:, 0:CH].astype(BF16), w[j, 0, k])
    re = res[:, 0, :] + res[:, 1, :] + res[:, 2, :]
    im = res[:, 3, :] + res[:, 4, :] + res[:, 5, :]
    mixed = re - swap(im) * sgn
    ab = mm(inv[...], mixed, NN, HIGH)
    a, b = ab[:rows], ab[rows:]
    y = a - swap(b) * sign_row((rows, HALVES))
    out[...] = y.reshape(out.shape)


def y_back_kernel(r, inv, out):
    rows = inv.shape[0] // 2
    sgn = sign_row((rows, HALVES))
    for i in range(2 * CX):
        ab = mm(inv[...], r[:, i, :], NN, HIGH)
        y = ab[:rows] - swap(ab[rows:]) * sgn
        out[:, i * CY:(i + 1) * CY, :] = y.reshape(rows // CY, CY, HALVES)


def final_kernel(last, at, zb, tab, own, xsides, below, above, yedge, left, right, skip, bias, out):
    low = at[0] == 0
    top = at[0] == last[0]
    first_pen = at[1] == 0
    last_pen = at[1] == last[1]
    lane = lax.broadcasted_iota(jnp.int32, (MODES, HALVES), 1)
    zero = jnp.zeros((CH, CH), F32)
    skip_t = jnp.transpose(skip[...])
    pair = jnp.concatenate(
        [jnp.concatenate([skip_t, zero], axis=1), jnp.concatenate([zero, skip_t], axis=1)], axis=0)
    col = jnp.concatenate([bias[...], bias[...]], axis=1)
    col = jnp.transpose(jnp.broadcast_to(col, (8, HALVES)))
    col = jnp.broadcast_to(col[:, 0:1], (HALVES, NZ))
    for x in range(CX):
        for yp in range(CY // 2):
            i = x * CY + 2 * yp
            u = zb[:, i, :]
            v = zb[:, i + 1, :]
            s = jnp.concatenate(
                [jnp.where(lane < CH, u, swap(v)), jnp.where(lane < CH, swap(u), v)], axis=0)
            spectral = mm(s, tab[...], TN, HIGH)
            lat = []
            for j in range(2):
                y = 2 * yp + j
                l = own[i + j]
                if x == 0:
                    l = l + jnp.where(low, xsides[0, y], below[y])
                if x == CX - 1:
                    l = l + jnp.where(top, xsides[1, y], above[y])
                if y == 0:
                    l = l + jnp.where(first_pen, yedge[0, x], left[x])
                if y == CY - 1:
                    l = l + jnp.where(last_pen, yedge[1, x], right[x])
                lat.append(l)
            total = spectral + mm(pair, jnp.concatenate(lat, axis=0), NN, HIGH) + col
            out[x, 2 * yp:2 * yp + 2] = gelu(total).astype(BF16).reshape(2, CH, NZ)


def call(kernel, shapes, args, scratch=(), smem=False, name=None):
    specs = [pl.BlockSpec(memory_space=pltpu.VMEM)] * len(args)
    if smem:
        specs[0] = pl.BlockSpec(memory_space=pltpu.SMEM)
    return pl.pallas_call(
        kernel,
        out_shape=shapes,
        in_specs=specs,
        scratch_shapes=list(scratch),
        compiler_params=LIMIT,
        name=name,
    )(*args)


def shape(*dims):
    return jax.ShapeDtypeStruct(dims, F32)


def exchange(x, axis):
    return lax.all_to_all(x, axis, split_axis=0, concat_axis=0, tiled=True)


def moved(x, axis, step):
    devices = range(lax.axis_size(axis))
    return lax.ppermute(x, axis, [(i - step, i) for i in devices if i - step in devices])


def per_device(features, positions, home_cells, neighbours, degrees, lift_input, kernel_first,
               kernel_bias, kernel_second, spectral_weights, skip_weights, skip_bias):
    bins = lax.axis_size("bin")
    pens = lax.axis_size("pen")
    at = jnp.stack([lax.axis_index("bin"), lax.axis_index("pen")]).astype(jnp.int32)
    own, ysides, xsides, spec, edge = lift_points(
        at, (bins * CX - 1, pens * CY - 1), features.T, positions, home_cells, neighbours.T,
        degrees[None, :], lift_input, kernel_first, kernel_bias[None, :], kernel_second)
    edge_below = moved(edge[1], "bin", 1)
    edge_above = moved(edge[0], "bin", -1)
    below = moved(xsides[1], "bin", 1)
    above = moved(xsides[0], "bin", -1)
    spec = call(functools.partial(join_kernel, bins - 1), shape(*spec.shape),
                (at, spec, edge, edge_below, edge_above), smem=True, name="join")
    rows = 2 * CX * (CY + 2)
    r = exchange(spec.reshape(pens, rows, HALVES), "pen")
    main, side = y_forward_tables(pens)
    r, yedge = call(
        functools.partial(y_kernel, bins - 1),
        [shape(MODES, 2 * CX, HALVES), shape(*ysides.shape)],
        (at, r, jnp.asarray(main), jnp.asarray(side), ysides, xsides, below, above),
        smem=True, name="forward_y")
    left = moved(yedge[1], "pen", 1)
    right = moved(yedge[0], "pen", -1)
    r = exchange(r, "bin")
    fwd, inv = x_tables(bins)
    r = call(x_kernel, shape(MODES, 2 * CX, HALVES),
             (r, jnp.asarray(fwd), jnp.asarray(inv), spectral_weights),
             scratch=[pltpu.VMEM((2 * MODES, 8, HALVES), F32)] * 2, name="mix_x")
    r = exchange(r, "bin")
    r = call(y_back_kernel, shape(pens, 2 * CX * CY, HALVES),
             (r, jnp.asarray(y_inverse_table(pens))), name="inverse_y")
    r = exchange(r, "pen")
    out = call(
        functools.partial(final_kernel, (bins - 1, pens - 1)),
        jax.ShapeDtypeStruct((CX, CY, CH, NZ), BF16),
        (at, r.reshape(MODES, CX * CY, HALVES), jnp.asarray(z_inverse_table()), own, xsides,
         below, above, yedge, left, right, skip_weights, skip_bias[None, :]),
        smem=True, name="finish")
    return out.transpose(0, 1, 3, 2)


def solution(mesh):
    in_specs = (
        P(("bin", "pen"), None),
        P(None, ("bin", "pen")),
        P(None, ("bin", "pen")),
        P(("bin", "pen"), None),
        P(("bin", "pen")),
        P(),
        P(),
        P(),
        P(),
        P(None, "bin", "pen", None, None),
        P(),
        P(),
    )
    out_specs = P("bin", "pen", None, None)
    return jax.shard_map(
        per_device, mesh=mesh, in_specs=in_specs, out_specs=out_specs, check_vma=False
    )
```

time: 476 us -> 192 us (0.40)
  the two profiles are of different devices: /device:TPU:32 before, /device:TPU:2 now
where the time goes in v1:
time: 192 us; the launch traced here: 191 us
  waiting for transfers between devices  63.4 us (33%)
  Pallas kernels  53.4 us (28%)
  starting transfers between devices  33 us (17%)
  blocking collectives  27.7 us (14%)
  local copies, waits for them, and re-layouts  13.5 us (7%)
    ppermute x6, waiting for transfers between devices, moved(): lax.ppermute(x, axis, [(i - step, i) for i in devices if i - step in devi...  43.6 us
    pallas_call x1, Pallas kernels, lift_points(): pl.pallas_call(functools.partial(lift_kernel, last), out_shape=shapes, in...  41.2 us
    all_to_all x2, blocking collectives, exchange(): return lax.all_to_all(x, axis, split_axis=0, concat_axis=0, tiled=True)  27.7 us
    all_to_all x2, waiting for transfers between devices, exchange(): return lax.all_to_all(x, axis, split_axis=0, concat_axis=0, tiled=True)  19.8 us
    all_to_all x2, starting transfers between devices, exchange(): return lax.all_to_all(x, axis, split_axis=0, concat_axis=0, tiled=True)  18.3 us
    ppermute x6, starting transfers between devices, moved(): lax.ppermute(x, axis, [(i - step, i) for i in devices if i - step in devi...  14.7 us
    unnamed x54, local copies, waits for them, and re-layouts  13.3 us
    pallas_call x5, Pallas kernels, call(): pl.pallas_call(kernel, out_shape=shapes, in_specs=specs, scratch_shapes=l...  12.2 us
  transfers between devices with their start and end apart: 8, of which 7 were waited for; matrix products, arithmetic and copies ran while one was open for 0% of the time, Pallas kernels for 0%

profile of v1, /device:TPU:2, one launch (start us, length us, event | category | flops | bytes accessed | tf_op | source)
XLA Modules:
  0.0 191.3 jit_solution(17412091686140408800)
XLA Ops:
  0.1 0.9 copy-done.9
  1.0 0.9 copy-done.11
  1.9 0.8 copy-done.16
  2.8 0.8 copy-done.19
  7.8 41.2 %lift.2 = (f32[32,64,192]{2,1,0:T(8,128)S(1)}, f32[2,4,64,192]{3,2,1,0:T(8,128)S(1)}, f32[2,10,64,192]{3,2,1,0:T(8,128)S(1)}, f32[32,40,128]{2,1,0:T(8,128)S(1)}, f32[2,32,10,128]{3,2,1,0:T(8,128)S(1)}) custom-call(s32[2]{0:T(128)S(1)} %pad_add_fusion.at, bf16[64,2048]{1,0:T(8,128)(2,1)S(1)} %bitcast.22, f32[3,2048]{1,0:T(4,128)S(1)} %copy-done.19, ...), custom_call_target="tpu_custom_call" | custom-call | tf_op jit(solution)/shard_map/lift/pallas_call | solution.py:284
  49.0 1.3 copy-done.3
  50.4 1.9 %collective-permute-start.1 = (f32[32,10,128]{2,1,0:T(8,128)S(1)}, f32[32,10,128]{2,1,0:T(8,128)S(1)}, u32[]{:S(2)}, u32[]{:S(2)}) collective-permute-start(f32[32,10,128]{2,1,0:T(8,128)S(1)} %get-tuple-element.23), channel_id=1, source_target_pairs={{16,0},{32,16},{48,32},{64,48},{80,64},{96,80},{112,96},{128,112},... | collective-permute-start | bytes 491528 | tf_op jit(solution)/shard_map/ppermute | solution.py:427
  52.3 2.4 %collective-permute-start = (f32[32,10,128]{2,1,0:T(8,128)S(1)}, f32[32,10,128]{2,1,0:T(8,128)S(1)}, u32[]{:S(2)}, u32[]{:S(2)}) collective-permute-start(f32[32,10,128]{2,1,0:T(8,128)S(1)} %get-tuple-element.24), channel_id=1, source_target_pairs={{0,16},{16,32},{32,48},{48,64},{64,80},{80,96},{96,112},{112,128},... | collective-permute-start | bytes 491528 | tf_op jit(solution)/shard_map/ppermute | solution.py:427
  54.7 1.5 collective-permute-done.1.above
  56.2 8.1 %collective-permute-done.below = f32[32,10,128]{2,1,0:T(8,128)S(1)} collective-permute-done((f32[32,10,128]{2,1,0:T(8,128)S(1)}, f32[32,10,128]{2,1,0:T(8,128)S(1)}, u32[]{:S(2)}, u32[]{:S(2)}) %collective-permute-start) | collective-permute-done | bytes 163872 | tf_op jit(solution)/shard_map/ppermute | solution.py:427
  64.3 1.5 join.1
  65.7 10.9 %all-to-all-start = ((f32[16,80,128]{2,1,0:T(8,128)}), f32[16,80,128]{2,1,0:T(8,128)S(1)}, u32[]{:S(2)}, u32[]{:S(2)}) async-start(f32[16,80,128]{2,1,0:T(8,128)} %bitcast.8), calls=%async_computation | async-start | bytes 1310720 | tf_op jit(solution)/shard_map/all_to_all | solution.py:422
  76.8 1.9 %collective-permute-start.3 = (f32[10,64,192]{2,1,0:T(8,128)S(1)}, f32[10,64,192]{2,1,0:T(8,128)S(1)}, u32[]{:S(2)}, u32[]{:S(2)}) collective-permute-start(f32[10,64,192]{2,1,0:T(8,128)S(1)} %get-tuple-element.19), channel_id=1, source_target_pairs={{16,0},{32,16},{48,32},{64,48},{80,64},{96,80},{112,96},{128,112},... | collective-permute-start | bytes 1474568 | tf_op jit(solution)/shard_map/ppermute | solution.py:427
  78.7 2.4 %collective-permute-start.2 = (f32[10,64,192]{2,1,0:T(8,128)S(1)}, f32[10,64,192]{2,1,0:T(8,128)S(1)}, u32[]{:S(2)}, u32[]{:S(2)}) collective-permute-start(f32[10,64,192]{2,1,0:T(8,128)S(1)} %get-tuple-element.20), channel_id=1, source_target_pairs={{0,16},{16,32},{32,48},{48,64},{64,80},{80,96},{96,112},{112,128},... | collective-permute-start | bytes 1474568 | tf_op jit(solution)/shard_map/ppermute | solution.py:427
  81.2 5.7 %collective-permute-done.3.above = f32[10,64,192]{2,1,0:T(8,128)S(1)} collective-permute-done((f32[10,64,192]{2,1,0:T(8,128)S(1)}, f32[10,64,192]{2,1,0:T(8,128)S(1)}, u32[]{:S(2)}, u32[]{:S(2)}) %collective-permute-start.3) | collective-permute-done | bytes 491552 | tf_op jit(solution)/shard_map/ppermute | solution.py:427
  86.8 3.8 %collective-permute-done.2.below = f32[10,64,192]{2,1,0:T(8,128)S(1)} collective-permute-done((f32[10,64,192]{2,1,0:T(8,128)S(1)}, f32[10,64,192]{2,1,0:T(8,128)S(1)}, u32[]{:S(2)}, u32[]{:S(2)}) %collective-permute-start.2) | collective-permute-done | bytes 491552 | tf_op jit(solution)/shard_map/ppermute | solution.py:427
  90.7 18.7 %all-to-all-done.r = f32[16,80,128]{2,1,0:T(8,128)S(1)} async-done(((f32[16,80,128]{2,1,0:T(8,128)}), f32[16,80,128]{2,1,0:T(8,128)S(1)}, u32[]{:S(2)}, u32[]{:S(2)}) %all-to-all-start) | async-done | bytes 655392 | tf_op jit(solution)/shard_map/all_to_all | solution.py:422
  109.4 1.0 copy-done.6
  110.4 1.4 forward_y.1
  111.8 0.8 copy-done
  112.6 16.3 %all_to_all.20.r = f32[32,8,128]{2,1,0:T(8,128)S(1)} all-to-all(f32[32,8,128]{2,1,0:T(8,128)S(1)} %get-tuple-element.16), channel_id=1, replica_groups=mesh['bin'=32,'pen'=16] {'bin'}, dimensions={0} | all-to-all | bytes 262144 | tf_op jit(solution)/shard_map/all_to_all | solution.py:422
  128.9 1.4 mix_x.1
  130.3 11.4 %all_to_all.21.r = f32[32,8,128]{2,1,0:T(8,128)S(1)} all-to-all(f32[32,8,128]{2,1,0:T(8,128)S(1)} %mix_x.1), channel_id=1, replica_groups=mesh['bin'=32,'pen'=16] {'bin'}, dimensions={0} | all-to-all | bytes 262144 | tf_op jit(solution)/shard_map/all_to_all | solution.py:422
  141.7 1.1 inverse_y.1
  142.8 0.8 copy-done.2
  143.6 7.4 %all-to-all-start.3 = ((f32[16,64,128]{2,1,0:T(8,128)}), f32[16,64,128]{2,1,0:T(8,128)}, u32[]{:S(2)}, u32[]{:S(2)}) async-start(f32[16,64,128]{2,1,0:T(8,128)} %copy-done.2), calls=%async_computation.3 | async-start | bytes 1048576 | tf_op jit(solution)/shard_map/all_to_all | solution.py:422
  151.0 1.3 collective-permute-start.5
  152.3 4.7 %collective-permute-start.4 = (f32[4,64,192]{2,1,0:T(8,128)S(1)}, f32[4,64,192]{2,1,0:T(8,128)S(1)}, u32[]{:S(2)}, u32[]{:S(2)}) collective-permute-start(f32[4,64,192]{2,1,0:T(8,128)S(1)} %get-tuple-element.22), channel_id=1, source_target_pairs={{0,1},{1,2},{2,3},{3,4},{4,5},{5,6},{6,7},{7,8},{8,9},{9,10},{10,1... | collective-permute-start | bytes 589832 | tf_op jit(solution)/shard_map/ppermute | solution.py:427
  157.0 24.6 %collective-permute-done.5.right = f32[4,64,192]{2,1,0:T(8,128)S(1)} collective-permute-done((f32[4,64,192]{2,1,0:T(8,128)S(1)}, f32[4,64,192]{2,1,0:T(8,128)S(1)}, u32[]{:S(2)}, u32[]{:S(2)}) %collective-permute-start.5) | collective-permute-done | bytes 196640 | tf_op jit(solution)/shard_map/ppermute | solution.py:427
  182.3 1.2 all-to-all-done.3
  183.5 0.9 copy-done.8
  184.4 6.9 %finish.1 = bf16[4,8,64,192]{3,2,1,0:T(8,128)(2,1)} custom-call(s32[2]{0:T(128)S(1)} %pad_add_fusion.at, f32[32,32,128]{2,1,0:T(8,128)} %bitcast.11.zb, f32[64,192]{1,0:T(8,128)S(1)} %copy-done.15, f32[32,64,192]{2,1,0:T(8,128)} %copy-done.3, f32[2,10,64,192]{3,2,1,0:T(8,128)S(1)} %get-tuple-element.15.xsides, ...), custom_call_target="tpu_custom_call" | custom-call | tf_op jit(solution)/shard_map/finish/pallas_call | solution.py:407
  (50 shorter events, 5.2 us)
Async XLA Ops:
  0.1 0.9 copy-start.9
  1.0 0.9 copy-start.11
  1.9 0.8 copy-start.16
  2.8 0.8 copy-start.19
  3.5 0.8 copy-start.20
  4.3 0.7 copy-start.21
  5.0 0.7 copy-start.22
  49.0 1.4 copy-start.3
  50.3 15.4 %copy-start.5 = (f32[2,4,64,192]{3,2,1,0:T(8,128)}, f32[2,4,64,192]{3,2,1,0:T(8,128)S(1)}, u32[]{:S(2)}) copy-start(f32[2,4,64,192]{3,2,1,0:T(8,128)S(1)} %get-tuple-element.14.ysides) | copy-start | bytes 1179652
  50.4 5.8 %collective-permute-start.1 = (f32[32,10,128]{2,1,0:T(8,128)S(1)}, f32[32,10,128]{2,1,0:T(8,128)S(1)}, u32[]{:S(2)}, u32[]{:S(2)}) collective-permute-start(f32[32,10,128]{2,1,0:T(8,128)S(1)} %get-tuple-element.23), channel_id=1, source_target_pairs={{16,0},{32,16},{48,32},{64,48},{80,64},{96,80},{112,96},{128,112},... | collective-permute-start | bytes 491528 | tf_op jit(solution)/shard_map/ppermute | solution.py:427
  52.3 12.0 %collective-permute-start = (f32[32,10,128]{2,1,0:T(8,128)S(1)}, f32[32,10,128]{2,1,0:T(8,128)S(1)}, u32[]{:S(2)}, u32[]{:S(2)}) collective-permute-start(f32[32,10,128]{2,1,0:T(8,128)S(1)} %get-tuple-element.24), channel_id=1, source_target_pairs={{0,16},{16,32},{32,48},{48,64},{64,80},{80,96},{96,112},{112,128},... | collective-permute-start | bytes 491528 | tf_op jit(solution)/shard_map/ppermute | solution.py:427
  65.7 43.6 %all-to-all-start = ((f32[16,80,128]{2,1,0:T(8,128)}), f32[16,80,128]{2,1,0:T(8,128)S(1)}, u32[]{:S(2)}, u32[]{:S(2)}) async-start(f32[16,80,128]{2,1,0:T(8,128)} %bitcast.8), calls=%async_computation | async-start | bytes 1310720 | tf_op jit(solution)/shard_map/all_to_all | solution.py:422
  76.7 32.7 %copy-start.12 = (f32[256,128]{1,0:T(8,128)S(1)}, f32[256,128]{1,0:T(8,128)}, u32[]{:S(2)}) copy-start(f32[256,128]{1,0:T(8,128)} %constant.25.clone.side) | copy-start | bytes 393220
  76.7 32.7 %copy-start.18 = (f32[64,128]{1,0:T(8,128)S(1)}, f32[64,128]{1,0:T(8,128)}, u32[]{:S(2)}) copy-start(f32[64,128]{1,0:T(8,128)} %constant.24.clone.main) | copy-start | bytes 98308
  76.8 10.0 %collective-permute-start.3 = (f32[10,64,192]{2,1,0:T(8,128)S(1)}, f32[10,64,192]{2,1,0:T(8,128)S(1)}, u32[]{:S(2)}, u32[]{:S(2)}) collective-permute-start(f32[10,64,192]{2,1,0:T(8,128)S(1)} %get-tuple-element.19), channel_id=1, source_target_pairs={{16,0},{32,16},{48,32},{64,48},{80,64},{96,80},{112,96},{128,112},... | collective-permute-start | bytes 1474568 | tf_op jit(solution)/shard_map/ppermute | solution.py:427
  78.7 11.9 %collective-permute-start.2 = (f32[10,64,192]{2,1,0:T(8,128)S(1)}, f32[10,64,192]{2,1,0:T(8,128)S(1)}, u32[]{:S(2)}, u32[]{:S(2)}) collective-permute-start(f32[10,64,192]{2,1,0:T(8,128)S(1)} %get-tuple-element.20), channel_id=1, source_target_pairs={{0,16},{16,32},{32,48},{48,64},{64,80},{80,96},{96,112},{112,128},... | collective-permute-start | bytes 1474568 | tf_op jit(solution)/shard_map/ppermute | solution.py:427
  109.4 1.0 copy-start.6
  110.4 18.5 %copy-start.4 = (bf16[32,1,2,64,128]{4,3,2,1,0:T(8,128)(2,1)S(1)}, bf16[32,1,2,64,128]{4,3,2,1,0:T(8,128)(2,1)}, u32[]{:S(2)}) copy-start(bf16[32,1,2,64,128]{4,3,2,1,0:T(8,128)(2,1)} %w.1) | copy-start | bytes 3145732
  110.4 18.5 %copy-start.10 = (f32[512,64]{1,0:T(8,128)S(1)}, f32[512,64]{1,0:T(8,128)}, u32[]{:S(2)}) copy-start(f32[512,64]{1,0:T(8,128)} %constant.27.clone.inv) | copy-start | bytes 393220
  110.4 18.5 %copy-start.14 = (f32[128,256]{1,0:T(8,128)S(1)}, f32[128,256]{1,0:T(8,128)}, u32[]{:S(2)}) copy-start(f32[128,256]{1,0:T(8,128)} %constant.26.clone.fwd) | copy-start | bytes 393220
  111.8 0.8 copy-start
  112.6 29.1 %copy-start.13 = (f32[256,32]{1,0:T(8,128)S(1)}, f32[256,32]{1,0:T(8,128)}, u32[]{:S(2)}) copy-start(f32[256,32]{1,0:T(8,128)} %constant.28.clone.inv) | copy-start | bytes 98308
  130.3 20.7 %copy-start.1 = (f32[2,4,64,192]{3,2,1,0:T(8,128)S(1)}, f32[2,4,64,192]{3,2,1,0:T(8,128)}, u32[]{:S(2)}) copy-start(f32[2,4,64,192]{3,2,1,0:T(8,128)} %copy-done) | copy-start | bytes 1179652
  141.7 41.8 %copy-start.15 = (f32[64,192]{1,0:T(8,128)S(1)}, f32[64,192]{1,0:T(8,128)}, u32[]{:S(2)}) copy-start(f32[64,192]{1,0:T(8,128)} %constant.29.clone.tab) | copy-start | bytes 147460
  141.7 41.8 %copy-start.17 = (f32[64,64]{1,0:T(8,128)S(1)}, f32[64,64]{1,0:T(8,128)}, u32[]{:S(2)}) copy-start(f32[64,64]{1,0:T(8,128)} %skip.1) | copy-start | bytes 49156
  141.7 41.8 %copy-start.26 = (f32[64]{0:T(128)S(1)}, f32[64]{0:T(128)}, u32[]{:S(2)}) copy-start(f32[64]{0:T(128)} %param.30) | copy-start | bytes 772
  142.8 0.8 copy-start.2
  143.6 39.9 %all-to-all-start.3 = ((f32[16,64,128]{2,1,0:T(8,128)}), f32[16,64,128]{2,1,0:T(8,128)}, u32[]{:S(2)}, u32[]{:S(2)}) async-start(f32[16,64,128]{2,1,0:T(8,128)} %copy-done.2), calls=%async_computation.3 | async-start | bytes 1048576 | tf_op jit(solution)/shard_map/all_to_all | solution.py:422
  151.0 30.6 %collective-permute-start.5 = (f32[4,64,192]{2,1,0:T(8,128)S(1)}, f32[4,64,192]{2,1,0:T(8,128)S(1)}, u32[]{:S(2)}, u32[]{:S(2)}) collective-permute-start(f32[4,64,192]{2,1,0:T(8,128)S(1)} %get-tuple-element.21), channel_id=1, source_target_pairs={{1,0},{2,1},{3,2},{4,3},{5,4},{6,5},{7,6},{8,7},{9,8},{10,9},{11,1... | collective-permute-start | bytes 589832 | tf_op jit(solution)/shard_map/ppermute | solution.py:427
  152.3 29.3 %collective-permute-start.4 = (f32[4,64,192]{2,1,0:T(8,128)S(1)}, f32[4,64,192]{2,1,0:T(8,128)S(1)}, u32[]{:S(2)}, u32[]{:S(2)}) collective-permute-start(f32[4,64,192]{2,1,0:T(8,128)S(1)} %get-tuple-element.22), channel_id=1, source_target_pairs={{0,1},{1,2},{2,3},{3,4},{4,5},{5,6},{6,7},{7,8},{8,9},{9,10},{10,1... | collective-permute-start | bytes 589832 | tf_op jit(solution)/shard_map/ppermute | solution.py:427
  181.6 0.7 copy-start.7
  183.5 1.0 copy-start.8
  (3 other events, 2.0 us)

commit v2 on v1

v2 whole, which is shorter than its diff:
```python
import functools
import math

import jax
import jax.numpy as jnp
import numpy as np
from jax import lax
from jax.experimental import pallas as pl
from jax.experimental.pallas import tpu as pltpu
from jax.sharding import PartitionSpec as P

NZ = 192
CX = 4
CY = 8
PTS = 2048
CH = 64
MODES = 32
CHUNK = 256
SUB = 128
HALVES = 2 * CH

F32 = jnp.float32
BF16 = jnp.bfloat16
HIGH = lax.Precision.HIGH
LIMIT = pltpu.CompilerParams(vmem_limit_bytes=32 * 1024 * 1024)

NN = (((1,), (0,)), ((), ()))
NT = (((1,), (1,)), ((), ()))
TN = (((0,), (0,)), ((), ()))


def mm(a, b, dims=NN, precision=None):
    return lax.dot_general(a, b, dims, precision=precision, preferred_element_type=F32)


def gelu(x):
    inner = x * (0.7978845608028654 + 0.035677408136300125 * (x * x))
    half = 0.5 * x
    return half + half * jnp.tanh(inner)


def swap(x):
    return pltpu.roll(x, CH, 1)


def sign_row(shape):
    lane = lax.broadcasted_iota(jnp.int32, shape, 1)
    return jnp.where(lane < CH, 1.0, -1.0).astype(F32)


def tables(length, signed):
    mode = np.arange(MODES)
    if signed:
        mode = np.where(mode < MODES // 2, mode, mode - MODES)
    return mode


def angles(rows, length, signed):
    mode = tables(length, signed)
    phase = (np.asarray(rows)[:, None] * mode[None, :]) % length
    angle = phase * (2.0 * math.pi / length)
    scale = 1.0 / math.sqrt(length)
    return np.cos(angle) * scale, np.sin(angle) * scale


def z_forward_table():
    c, s = angles(np.arange(NZ), NZ, False)
    return np.concatenate([c.T, -s.T], axis=0).astype(np.float32)


def z_inverse_table():
    c, s = angles(np.arange(NZ), NZ, False)
    w = np.where(np.arange(MODES) == 0, 1.0, 2.0)[:, None]
    return np.concatenate([c.T * w, -s.T * w], axis=0).astype(np.float32)


def y_forward_tables(pens):
    length = CY * pens
    c, s = angles(np.arange(length), length, True)
    main = np.concatenate([c.T, s.T], axis=0)
    side = np.zeros((CX, 2, MODES, pens, CX, 2))
    for q in range(pens):
        for h in range(2):
            y = min(max(q * CY - 1 + h * (CY + 1), 0), length - 1)
            for x in range(CX):
                side[x, 0, :, q, x, h] = c[y]
                side[x, 1, :, q, x, h] = s[y]
    side = side.reshape(CX * 2 * MODES, pens * CX * 2)
    return main.astype(np.float32), side.astype(np.float32)


def y_inverse_table(pens):
    length = CY * pens
    c, s = angles(np.arange(length), length, True)
    return np.concatenate([c, s], axis=0).astype(np.float32)


def x_tables(bins):
    length = CX * bins
    c, s = angles(np.arange(length), length, True)
    fwd = np.zeros((2, 2, MODES, bins, 2, CX))
    inv = np.zeros((2, bins, 2, CX, 2, MODES))
    for k in range(2):
        fwd[0, k, :, :, k, :] = c.T.reshape(MODES, bins, CX)
        fwd[1, k, :, :, k, :] = s.T.reshape(MODES, bins, CX)
        inv[0, :, k, :, k, :] = c.reshape(bins, CX, MODES)
        inv[1, :, k, :, k, :] = s.reshape(bins, CX, MODES)
    fwd = fwd.reshape(4 * MODES, bins * 2 * CX)
    inv = inv.reshape(2 * bins * 2 * CX, 2 * MODES)
    return fwd.astype(np.float32), inv.astype(np.float32)


def pieces(x):
    hi = x.astype(BF16).astype(F32)
    rest = x - hi
    mid = rest.astype(BF16).astype(F32)
    return hi, mid, rest - mid


def home_plane(order):
    return jnp.where(order == 0, 0, jnp.where(order == 1, CX - 1, order - 1))


def add_chunk(last, at, step, plane0, data, rankb, taps, quad, lift_t, mess, keys, grid):
    base = step * CHUNK
    lanes = lax.broadcasted_iota(jnp.int32, (PTS, 128), 1) + base
    perm = jnp.concatenate(
        [jnp.where(rankb[...] == lanes + j * 128, 1.0, 0.0).astype(BF16)
         for j in range(CHUNK // 128)], axis=1)
    t = mm(data[...], perm)
    hzs = t[73:74]
    cols = t[74:75]
    spans = [(jnp.min(cols[:, j * SUB:(j + 1) * SUB]).astype(jnp.int32),
              jnp.max(cols[:, j * SUB:(j + 1) * SUB]).astype(jnp.int32) + 1)
             for j in range(CHUNK // SUB)]
    key = 256.0 * cols
    key = jnp.concatenate(
        [key + jnp.maximum(hzs - 1.0, 0.0), key + hzs, key + jnp.minimum(hzs + 1.0, NZ - 1.0),
         jnp.zeros((5, CHUNK), F32)], axis=0)
    key = jnp.transpose(key)
    for dz in range(3):
        keys[dz] = jnp.broadcast_to(key[:, dz:dz + 1], (CHUNK, NZ))

    values = mm(lift_t[...], t[0:64].astype(BF16))
    ox = t[64:65] + t[65:66] + t[66:67]
    oy = t[67:68] + t[68:69] + t[69:70]
    oz = t[70:71] + t[71:72] + t[72:73]
    coli = cols.astype(jnp.int32)
    gx = home_plane(lax.shift_right_logical(coli, 3)) + at[0] * CX
    gy = jnp.bitwise_and(coli, 7) + at[1] * CY
    k_x, k_y, k_z, k_b = taps[0], taps[1], taps[2], taps[3]

    def ends(g, end):
        return (jnp.where(g > 0, -1.0, 0.0), None, jnp.where(g < end, 1.0, 0.0))

    base_pre = k_x * ox + k_y * oy + k_z * oz + k_b
    ex = ends(gx, last[0])
    ey = ends(gy, last[1])
    ez = ends(hzs, NZ - 1.0)
    pend = []

    def flush():
        while len(pend) < 4:
            pend.append((None, jnp.zeros((CH, CHUNK), BF16)))
        kern = mm(quad[...], jnp.concatenate([h for _, h in pend], axis=0))
        for j, (where, _) in enumerate(pend):
            if where is None:
                continue
            dx, dy, dz = where
            k = dx * 9 + dy * 3 + dz
            m = kern[j * CH:(j + 1) * CH] * (values * t[80 + k:81 + k])
            hi = m.astype(BF16)
            lo = (m - hi.astype(F32)).astype(BF16)
            r = (dx * 3 + dy) * CH
            for s in range(CHUNK // SUB):
                cut = slice(s * SUB, (s + 1) * SUB)
                mess[s, r:r + CH, dz * SUB:(dz + 1) * SUB] = hi[:, cut]
                mess[s, r:r + CH, (3 + dz) * SUB:(4 + dz) * SUB] = lo[:, cut]
        pend.clear()

    for dx in range(3):
        pre_x = base_pre if ex[dx] is None else base_pre + ex[dx] * k_x
        for dy in range(3):
            pre_y = pre_x if ey[dy] is None else pre_x + ey[dy] * k_y
            for dz in range(3):
                pre = pre_y if ez[dz] is None else pre_y + ez[dz] * k_z
                pend.append(((dx, dy, dz), gelu(pre).astype(BF16)))
                if len(pend) == 4:
                    flush()
    flush()

    lane = lax.broadcasted_iota(jnp.int32, (SUB, NZ), 1).astype(F32)
    for s in range(CHUNK // SUB):
        def column(c, _):
            goal = lane + 256.0 * c.astype(F32)
            hot = jnp.concatenate(
                [jnp.where(keys[dz, s * SUB:(s + 1) * SUB] == goal, 1.0, 0.0).astype(BF16)
                 for dz in range(3)], axis=0)
            acc = mm(mess[s], jnp.concatenate([hot, hot], axis=0))
            cx = home_plane(lax.shift_right_logical(c, 3)) - plane0
            cy = jnp.bitwise_and(c, 7)
            for dx in range(3):
                for dy in range(3):
                    r = (dx * 3 + dy) * CH
                    grid[cx + dx, cy + dy] += acc[r:r + CH]
            return 0

        lax.fori_loop(spans[s][0], spans[s][1], column, 0)


def sides_kernel(last, at, feat_h, pos_h, home_h, nbr_h, deg_h, lift_h, first_h, bias_h, second_h,
                 grid, low, high, data, rankb, taps, quad, lift_t, count,
                 pos, home, nbr, deg, lift, first, bias, second, mess, keys, sems):
    pairs = [(home_h, home), (pos_h, pos), (nbr_h, nbr), (deg_h, deg),
             (feat_h, data.at[0:64]), (lift_h, lift), (first_h, first), (bias_h, bias),
             (second_h, second)]
    copies = [pltpu.make_async_copy(a, b, sems.at[i]) for i, (a, b) in enumerate(pairs)]
    for c in copies:
        c.start()
    grid[...] = jnp.zeros_like(grid)
    tri = jnp.where(
        lax.broadcasted_iota(jnp.int32, (CHUNK, CHUNK), 0)
        < lax.broadcasted_iota(jnp.int32, (CHUNK, CHUNK), 1), 1.0, 0.0).astype(BF16)
    for c in copies:
        c.wait()
    hx = home[0:1, :]
    hy = home[1:2, :]
    hz = home[2:3, :]
    order = jnp.where(hx == 0, 0, jnp.where(hx == CX - 1, 1, hx + 1))
    col = order * CY + hy
    count[0] = jnp.sum(jnp.where(order < 2, 1.0, 0.0)).astype(jnp.int32)

    ids = lax.broadcasted_iota(jnp.int32, (CX * CY, PTS), 0)
    carry = jnp.sum(jnp.where(col < ids, 1.0, 0.0), axis=1, keepdims=True)
    for blk in range(PTS // CHUNK):
        part = slice(blk * CHUNK, (blk + 1) * CHUNK)
        hot = jnp.where(col[:, part] == ids[:, part], 1.0, 0.0)
        ahead = mm(hot.astype(BF16), tri) + carry
        rank = jnp.sum(hot * ahead, axis=0, keepdims=True)
        rank = jnp.transpose(jnp.broadcast_to(rank, (8, CHUNK)))
        rankb[part, :] = jnp.broadcast_to(rank[:, 0:1], (CHUNK, 128)).astype(jnp.int32)
        carry = carry + jnp.sum(hot, axis=1, keepdims=True)

    slot = lax.broadcasted_iota(jnp.int32, (16, PTS), 0)
    bits = jnp.sum(
        jnp.where(slot < deg[...], jnp.left_shift(1, nbr[...]), 0), axis=0, keepdims=True)
    code = lax.broadcasted_iota(jnp.int32, (32, PTS), 0)
    live = jnp.bitwise_and(jnp.right_shift(bits, code), 1).astype(F32)
    off_x = (hx + at[0] * CX).astype(F32) + 0.5 - pos[0:1, :]
    off_y = (hy + at[1] * CY).astype(F32) + 0.5 - pos[1:2, :]
    off_z = hz.astype(F32) + 0.5 - pos[2:3, :]
    rows = [*pieces(off_x), *pieces(off_y), *pieces(off_z), hz.astype(F32), col.astype(F32),
            jnp.zeros((5, PTS), F32)]
    data[64:80, :] = jnp.concatenate(rows, axis=0).astype(BF16)
    data[80:112, :] = live.astype(BF16)

    flat = jnp.concatenate([first[...], bias[...], jnp.zeros((4, CH), F32)], axis=0)
    flat = jnp.concatenate([flat, jnp.zeros((8, 128 - CH), F32)], axis=1)
    flat = jnp.transpose(flat)
    for j in range(4):
        taps[j] = jnp.broadcast_to(flat[0:CH, j:j + 1], (CH, CHUNK))
    zero = jnp.zeros((CH, CH), F32)
    sec_t = jnp.transpose(second[...].astype(F32))
    quad[...] = jnp.concatenate(
        [jnp.concatenate([sec_t if i == j else zero for j in range(4)], axis=1)
         for i in range(4)], axis=0).astype(BF16)
    lift_t[...] = jnp.transpose(lift[...].astype(F32)).astype(BF16)

    def chunk(step, _):
        add_chunk(last, at, step, 0, data, rankb, taps, quad, lift_t, mess, keys, grid)
        return 0

    lax.fori_loop(0, (count[0] + CHUNK - 1) // CHUNK, chunk, 0)
    low[...] = grid[0]
    high[...] = grid[CX + 1]


def middle_kernel(last, at, count, data, rankb, taps, quad, lift_t, grid, mess, keys):
    grid[...] = jnp.zeros_like(grid)

    def chunk(step, _):
        add_chunk(last, at, step, 1, data, rankb, taps, quad, lift_t, mess, keys, grid)
        return 0

    lax.fori_loop((count[0] + CHUNK - 1) // CHUNK, PTS // CHUNK, chunk, 0)


def lift_points(at, last, feat, pos, home, nbr, deg, lift, first, bias, second):
    vmem = pl.BlockSpec(memory_space=pltpu.VMEM)
    smem = pl.BlockSpec(memory_space=pltpu.SMEM)
    work = [
        pltpu.VMEM((CHUNK // SUB, 9 * CH, 6 * SUB), BF16),
        pltpu.VMEM((3, CHUNK, NZ), F32),
    ]
    inputs = (feat, pos, home, nbr, deg, lift, first, bias, second)
    grid, low, high, *prepared, count = pl.pallas_call(
        functools.partial(sides_kernel, last),
        out_shape=[
            shape(CX + 2, CY + 2, CH, NZ),
            shape(CY + 2, CH, NZ),
            shape(CY + 2, CH, NZ),
            jax.ShapeDtypeStruct((112, PTS), BF16),
            jax.ShapeDtypeStruct((PTS, 128), jnp.int32),
            shape(4, CH, CHUNK),
            jax.ShapeDtypeStruct((4 * CH, 4 * CH), BF16),
            jax.ShapeDtypeStruct((CH, CH), BF16),
            jax.ShapeDtypeStruct((1,), jnp.int32),
        ],
        in_specs=[smem] + [pl.BlockSpec(memory_space=pltpu.HBM)] * len(inputs),
        out_specs=[vmem] * 8 + [smem],
        scratch_shapes=[pltpu.VMEM(x.shape, x.dtype) for x in inputs[1:]] + work
        + [pltpu.SemaphoreType.DMA((len(inputs),))],
        compiler_params=LIMIT,
        name="lift_sides",
    )(at, *inputs)
    middle = pl.pallas_call(
        functools.partial(middle_kernel, last),
        out_shape=shape(CX, CY + 2, CH, NZ),
        in_specs=[smem, smem] + [vmem] * 5,
        scratch_shapes=work,
        compiler_params=LIMIT,
        name="lift_middle",
    )(at, count, *prepared)
    return grid, low, high, middle


def latent_kernel(last, at, tabz, sides, middle, below, above, spec, own, yedge):
    low = at[0] == 0
    top = at[0] == last
    lane = lax.broadcasted_iota(jnp.int32, (MODES, HALVES), 1)
    table = tabz[...]
    for x in range(CX):
        for yp in range((CY + 2) // 2):
            cells = []
            for y in (2 * yp, 2 * yp + 1):
                l = sides[x + 1, y] + middle[x, y]
                if x == 0:
                    l = l + jnp.where(low, sides[0, y], below[y])
                if x == CX - 1:
                    l = l + jnp.where(top, sides[CX + 1, y], above[y])
                cells.append(l)
            d = mm(table, jnp.concatenate(cells, axis=0), NT, HIGH)
            re, im = d[0:MODES], d[MODES:]
            out = (jnp.where(lane < CH, re, swap(im)), jnp.where(lane < CH, swap(re), im))
            for j in range(2):
                y = 2 * yp + j
                if y in (0, CY + 1):
                    h = 0 if y == 0 else 1
                    spec[:, CX * CY + x * 2 + h, :] = out[j]
                    yedge[h, x] = cells[j]
                else:
                    spec[:, x * CY + y - 1, :] = out[j]
                    own[x * CY + y - 1] = cells[j]


def y_kernel(r, main, side, yedge, out, yedge_out):
    sgn = sign_row((MODES, HALVES))
    n = CX * CY
    pens = r.shape[0]
    for kz in range(2):
        o = kz * (n + 2 * CX)
        halo = mm(side[...], r[:, o + n:o + n + 2 * CX, :].reshape(pens * 2 * CX, HALVES), NN, HIGH)
        for x in range(CX):
            rows = r[:, o + x * CY:o + (x + 1) * CY, :].reshape(pens * CY, HALVES)
            ab = mm(main[...], rows, NN, HIGH) + halo[x * 2 * MODES:(x + 1) * 2 * MODES]
            out[:, kz * CX + x, :] = ab[:MODES] + swap(ab[MODES:]) * sgn
    yedge_out[...] = yedge[...]


def x_kernel(r, fwd, inv, w, out, lhs, res):
    rows = r.shape[0] * r.shape[1]
    modes = 2 * MODES
    sgn = sign_row((modes, HALVES))
    ab = mm(fwd[...], r[...].reshape(rows, HALVES), NN, HIGH)
    x = ab[:modes] + swap(ab[modes:]) * sgn
    parts = [*pieces(x), *pieces(swap(x))]
    lhs[...] = jnp.zeros_like(lhs)
    for j, p in enumerate(parts):
        lhs[:, j, :] = p
    for k in range(2):
        for j in range(MODES):
            m = k * MODES + j
            res[m] = mm(lhs[m][:, 0:CH].astype(BF16), w[j, 0, k])
    re = res[:, 0, :] + res[:, 1, :] + res[:, 2, :]
    im = res[:, 3, :] + res[:, 4, :] + res[:, 5, :]
    mixed = re - swap(im) * sgn
    ab = mm(inv[...], mixed, NN, HIGH)
    a, b = ab[:rows], ab[rows:]
    y = a - swap(b) * sign_row((rows, HALVES))
    out[...] = y.reshape(out.shape)


def y_back_kernel(r, inv, left, right, out):
    rows = inv.shape[0] // 2
    sgn = sign_row((rows, HALVES))
    for i in range(2 * CX):
        ab = mm(inv[...], r[:, i, :], NN, HIGH)
        y = ab[:rows] - swap(ab[rows:]) * sgn
        out[:, i * CY:(i + 1) * CY, :] = y.reshape(rows // CY, CY, HALVES)


def final_kernel(last, at, zb, tab, own, yedge, left, right, skip, bias, out):
    first_pen = at[1] == 0
    last_pen = at[1] == last
    lane = lax.broadcasted_iota(jnp.int32, (MODES, HALVES), 1)
    zero = jnp.zeros((CH, CH), F32)
    skip_t = jnp.transpose(skip[...])
    pair = jnp.concatenate(
        [jnp.concatenate([skip_t, zero], axis=1), jnp.concatenate([zero, skip_t], axis=1)], axis=0)
    col = jnp.concatenate([bias[...], bias[...]], axis=1)
    col = jnp.transpose(jnp.broadcast_to(col, (8, HALVES)))
    col = jnp.broadcast_to(col[:, 0:1], (HALVES, NZ))
    for x in range(CX):
        for yp in range(CY // 2):
            i = x * CY + 2 * yp
            u = zb[:, i, :]
            v = zb[:, i + 1, :]
            s = jnp.concatenate(
                [jnp.where(lane < CH, u, swap(v)), jnp.where(lane < CH, swap(u), v)], axis=0)
            spectral = mm(s, tab[...], TN, HIGH)
            lat = []
            for j in range(2):
                y = 2 * yp + j
                l = own[i + j]
                if y == 0:
                    l = l + jnp.where(first_pen, yedge[0, x], left[x])
                if y == CY - 1:
                    l = l + jnp.where(last_pen, yedge[1, x], right[x])
                lat.append(l)
            total = spectral + mm(pair, jnp.concatenate(lat, axis=0), NN, HIGH) + col
            out[x, 2 * yp:2 * yp + 2] = gelu(total).astype(BF16).reshape(2, CH, NZ)


def call(kernel, shapes, args, scratch=(), smem=False, name=None, unread=0):
    specs = [pl.BlockSpec(memory_space=pltpu.VMEM)] * len(args)
    if smem:
        specs[0] = pl.BlockSpec(memory_space=pltpu.SMEM)
    for j in range(unread):
        specs[-1 - j] = pl.BlockSpec(memory_space=pl.ANY)
    return pl.pallas_call(
        kernel,
        out_shape=shapes,
        in_specs=specs,
        scratch_shapes=list(scratch),
        compiler_params=LIMIT,
        name=name,
    )(*args)


def shape(*dims):
    return jax.ShapeDtypeStruct(dims, F32)


def exchange(x, axis):
    return lax.all_to_all(x, axis, split_axis=0, concat_axis=0, tiled=True)


def moved(x, axis, step):
    devices = range(lax.axis_size(axis))
    return lax.ppermute(x, axis, [(i - step, i) for i in devices if i - step in devices])


def per_device(features, positions, home_cells, neighbours, degrees, lift_input, kernel_first,
               kernel_bias, kernel_second, spectral_weights, skip_weights, skip_bias):
    bins = lax.axis_size("bin")
    pens = lax.axis_size("pen")
    at = jnp.stack([lax.axis_index("bin"), lax.axis_index("pen")]).astype(jnp.int32)
    sides, low, high, middle = lift_points(
        at, (bins * CX - 1, pens * CY - 1), features.T, positions, home_cells, neighbours.T,
        degrees[None, :], lift_input, kernel_first, kernel_bias[None, :], kernel_second)
    below = moved(high, "bin", 1)
    above = moved(low, "bin", -1)
    spec, own, yedge = call(
        functools.partial(latent_kernel, bins - 1),
        [shape(MODES, CX * (CY + 2), HALVES), shape(CX * CY, CH, NZ), shape(2, CX, CH, NZ)],
        (at, jnp.asarray(z_forward_table()), sides, middle, below, above),
        smem=True, name="latent_z")
    rows = 2 * CX * (CY + 2)
    r = exchange(spec.reshape(pens, rows, HALVES), "pen")
    main, side = y_forward_tables(pens)
    r, yedge = call(y_kernel, [shape(MODES, 2 * CX, HALVES), shape(2, CX, CH, NZ)],
                    (r, jnp.asarray(main), jnp.asarray(side), yedge), name="forward_y")
    left = moved(yedge[1], "pen", 1)
    right = moved(yedge[0], "pen", -1)
    r = exchange(r, "bin")
    fwd, inv = x_tables(bins)
    r = call(x_kernel, shape(MODES, 2 * CX, HALVES),
             (r, jnp.asarray(fwd), jnp.asarray(inv), spectral_weights),
             scratch=[pltpu.VMEM((2 * MODES, 8, HALVES), F32)] * 2, name="mix_x")
    r = exchange(r, "bin")
    r = call(y_back_kernel, shape(pens, 2 * CX * CY, HALVES),
             (r, jnp.asarray(y_inverse_table(pens)), left, right), unread=2, name="inverse_y")
    r = exchange(r, "pen")
    out = call(
        functools.partial(final_kernel, pens - 1),
        jax.ShapeDtypeStruct((CX, CY, CH, NZ), BF16),
        (at, r.reshape(MODES, CX * CY, HALVES), jnp.asarray(z_inverse_table()), own,
         yedge, left, right, skip_weights, skip_bias[None, :]),
        smem=True, name="finish")
    return out.transpose(0, 1, 3, 2)


def solution(mesh):
    in_specs = (
        P(("bin", "pen"), None),
        P(None, ("bin", "pen")),
        P(None, ("bin", "pen")),
        P(("bin", "pen"), None),
        P(("bin", "pen")),
        P(),
        P(),
        P(),
        P(),
        P(None, "bin", "pen", None, None),
        P(),
        P(),
    )
    out_specs = P("bin", "pen", None, None)
    return jax.shard_map(
        per_device, mesh=mesh, in_specs=in_specs, out_specs=out_specs, check_vma=False
    )
```

time: 192 us -> 181 us (0.943)
  the two profiles are of different devices: /device:TPU:2 before, /device:TPU:32 now
where the time goes in v2:
time: 181 us; the launch traced here: 180 us
  blocking collectives  84.9 us (47%)
  Pallas kernels  46.2 us (26%)
  starting transfers between devices  28.9 us (16%)
  local copies, waits for them, and re-layouts  10.8 us (6%)
  waiting for transfers between devices  8.88 us (5%)
    all_to_all x2, blocking collectives, exchange(): return lax.all_to_all(x, axis, split_axis=0, concat_axis=0, tiled=True)  84.9 us
    pallas_call x1, Pallas kernels, lift_points(): pl.pallas_call(functools.partial(sides_kernel, last), out_shape=[shape(CX...  19 us
    pallas_call x1, Pallas kernels, lift_points(): pl.pallas_call(functools.partial(middle_kernel, last), out_shape=shape(CX...  17 us
    all_to_all x2, starting transfers between devices, exchange(): return lax.all_to_all(x, axis, split_axis=0, concat_axis=0, tiled=True)  16.4 us
    ppermute x4, starting transfers between devices, moved(): lax.ppermute(x, axis, [(i - step, i) for i in devices if i - step in devi...  12.5 us
    pallas_call x5, Pallas kernels, call(): pl.pallas_call(kernel, out_shape=shapes, in_specs=specs, scratch_shapes=l...  10.1 us
    unnamed x38, local copies, waits for them, and re-layouts  9.9 us
    all_to_all x2, waiting for transfers between devices, exchange(): return lax.all_to_all(x, axis, split_axis=0, concat_axis=0, tiled=True)  8.87 us
  transfers between devices with their start and end apart: 6, of which 2 were waited for; matrix products, arithmetic and copies ran while one was open for 0% of the time, Pallas kernels for 11%

profile of v2, /device:TPU:32, one launch (start us, length us, event | category | flops | bytes accessed | tf_op | source)
XLA Modules:
  0.0 179.9 jit_solution(4299858470153425217)
XLA Ops:
  0.0 0.1 pad_add_fusion.at
  0.1 0.9 copy-done.1
  1.0 0.9 copy-done.4
  1.9 0.8 copy-done.10
  2.7 0.8 copy-done.11
  3.5 0.7 copy-done.13
  4.2 0.7 copy-done.14
  4.9 0.7 copy-done.15
  5.6 0.7 copy-done.16
  6.3 0.7 copy-done.17
  6.9 19.0 %lift_sides.1 = (f32[6,10,64,192]{3,2,1,0:T(8,128)S(1)}, f32[10,64,192]{2,1,0:T(8,128)S(1)}, f32[10,64,192]{2,1,0:T(8,128)S(1)}, bf16[112,2048]{1,0:T(8,128)(2,1...) custom-call(s32[2]{0:T(128)S(1)} %pad_add_fusion.at, ...), custom_call_target="tpu_custom_call" | custom-call | tf_op jit(solution)/shard_map/lift_sides/pallas_call | solution.py:296
  25.9 5.4 %collective-permute-start = (f32[10,64,192]{2,1,0:T(8,128)S(1)}, f32[10,64,192]{2,1,0:T(8,128)S(1)}, u32[]{:S(2)}, u32[]{:S(2)}) collective-permute-start(f32[10,64,192]{2,1,0:T(8,128)S(1)} %get-tuple-element.26), channel_id=1, source_target_pairs={{0,16},{16,32},{32,48},{48,64},{64,80},{80,96},{96,112},{112,128},... | collective-permute-start | bytes 1474568 | tf_op jit(solution)/shard_map/ppermute | solution.py:460
  31.3 1.3 collective-permute-start.1
  32.6 17.0 %lift_middle.1.middle = f32[4,10,64,192]{3,2,1,0:T(8,128)S(1)} custom-call(s32[2]{0:T(128)S(1)} %pad_add_fusion.at, s32[1]{0:T(128)} %get-tuple-element.20.count, bf16[112,2048]{1,0:T(8,128)(2,1)S(1)} %get-tuple-element.21.data, s32[2048,128]{1,0:T(8,128)S(1)} %get-tuple-element.22.rankb, f32[4,64,256]{2,1,0:T(8,128)S(1)} %get-tuple-element.23.taps, ...), custom_call_target="tpu_custom_call" | custom-call | tf_op jit(solution)/shard_map/lift_middle/pallas_call | solution.py:316
  49.7 0.0 copy-start.6
  49.7 2.4 %latent_z.1 = (f32[32,40,128]{2,1,0:T(8,128)S(1)}, f32[32,64,192]{2,1,0:T(8,128)S(1)}, f32[2,4,64,192]{3,2,1,0:T(8,128)S(1)}) custom-call(s32[2]{0:T(128)S(1)} %pad_add_fusion.at, f32[64,192]{1,0:T(8,128)S(1)} %copy-done.8, f32[6,10,64,192]{3,2,1,0:T(8,128)S(1)} %get-tuple-element.19.sides, f32[4,10,64,192]{3,2,1,0:T(8,128)S(1)} %lift_middle.1.middle, ...), custom_call_target="tpu_custom_call" | custom-call | tf_op jit(solution)/shard_map/latent_z/pallas_call | solution.py:440
  52.1 49.8 %all_to_all.20.r = f32[16,80,128]{2,1,0:T(8,128)S(1)} all-to-all(f32[16,80,128]{2,1,0:T(8,128)S(1)} %bitcast.15), channel_id=1, replica_groups=mesh['bin'=32,'pen'=16] {'pen'}, dimensions={0} | all-to-all | bytes 1310720 | tf_op jit(solution)/shard_map/all_to_all | solution.py:455
  101.9 1.2 forward_y.1
  103.1 9.9 %all-to-all-start.1 = ((f32[32,8,128]{2,1,0:T(8,128)}), f32[32,8,128]{2,1,0:T(8,128)S(1)}, u32[]{:S(2)}, u32[]{:S(2)}) async-start(f32[32,8,128]{2,1,0:T(8,128)} %get-tuple-element.30), calls=%async_computation.1 | async-start | bytes 262144 | tf_op jit(solution)/shard_map/all_to_all | solution.py:455
  113.1 0.8 slice_bitcast_fusion
  113.9 1.9 %collective-permute-start.3 = (f32[4,64,192]{2,1,0:T(8,128)}, f32[4,64,192]{2,1,0:T(8,128)S(1)}, u32[]{:S(2)}, u32[]{:S(2)}) collective-permute-start(f32[4,64,192]{2,1,0:T(8,128)} %get-tuple-element.33), channel_id=1, source_target_pairs={{1,0},{2,1},{3,2},{4,3},{5,4},{6,5},{7,6},{8,7},{9,8},{10,9},{11,1... | collective-permute-start | bytes 589832 | tf_op jit(solution)/shard_map/ppermute | solution.py:460
  115.8 3.9 %collective-permute-start.2 = (f32[4,64,192]{2,1,0:T(8,128)}, f32[4,64,192]{2,1,0:T(8,128)S(1)}, u32[]{:S(2)}, u32[]{:S(2)}) collective-permute-start(f32[4,64,192]{2,1,0:T(8,128)} %get-tuple-element.34), channel_id=1, source_target_pairs={{0,1},{1,2},{2,3},{3,4},{4,5},{5,6},{6,7},{7,8},{8,9},{9,10},{10,1... | collective-permute-start | bytes 589832 | tf_op jit(solution)/shard_map/ppermute | solution.py:460
  119.8 1.1 all-to-all-done.1.r
  120.9 1.2 copy-done
  122.1 0.9 copy-done.5
  123.0 1.9 %mix_x.1 = f32[32,8,128]{2,1,0:T(8,128)} custom-call(f32[32,8,128]{2,1,0:T(8,128)S(1)} %all-to-all-done.1.r, f32[128,256]{1,0:T(8,128)S(1)} %copy-done.5, f32[512,64]{1,0:T(8,128)S(1)} %copy-done.2, bf16[32,1,2,64,128]{4,3,2,1,0:T(8,128)(2,1)S(1)} %copy-done), custom_call_target="tpu_custom_call" | custom-call | tf_op jit(solution)/shard_map/mix_x/pallas_call | solution.py:440
  124.9 6.4 %all-to-all-start.2 = ((f32[32,8,128]{2,1,0:T(8,128)}), f32[32,8,128]{2,1,0:T(8,128)S(1)}, u32[]{:S(2)}, u32[]{:S(2)}) async-start(f32[32,8,128]{2,1,0:T(8,128)} %mix_x.1), calls=%async_computation.2 | async-start | bytes 262144 | tf_op jit(solution)/shard_map/all_to_all | solution.py:455
  131.4 7.8 %all-to-all-done.2.r = f32[32,8,128]{2,1,0:T(8,128)S(1)} async-done(((f32[32,8,128]{2,1,0:T(8,128)}), f32[32,8,128]{2,1,0:T(8,128)S(1)}, u32[]{:S(2)}, u32[]{:S(2)}) %all-to-all-start.2) | async-done | bytes 131104 | tf_op jit(solution)/shard_map/all_to_all | solution.py:455
  139.1 0.9 copy-done.3
  140.0 0.7 inverse_y.1
  140.7 35.1 %all_to_all.21 = f32[16,64,128]{2,1,0:T(8,128)S(1)} all-to-all(f32[16,64,128]{2,1,0:T(8,128)S(1)} %inverse_y.1), channel_id=1, replica_groups=mesh['bin'=32,'pen'=16] {'pen'}, dimensions={0} | all-to-all | bytes 1048576 | tf_op jit(solution)/shard_map/all_to_all | solution.py:455
  175.8 4.1 %finish.1 = bf16[4,8,64,192]{3,2,1,0:T(8,128)(2,1)} custom-call(s32[2]{0:T(128)S(1)} %pad_add_fusion.at, f32[32,32,128]{2,1,0:T(8,128)S(1)} %bitcast.14, f32[64,192]{1,0:T(8,128)S(1)} %copy-done.7, f32[32,64,192]{2,1,0:T(8,128)S(1)} %get-tuple-element.32.own, f32[2,4,64,192]{3,2,1,0:T(8,128)S(1)} %get-tuple-element.31.yedge, ...), custom_call_target="tpu_custom_call" | custom-call | tf_op jit(solution)/shard_map/finish/pallas_call | solution.py:440
  (29 shorter events, 0.1 us)
Async XLA Ops:
  0.1 0.9 copy-start.1
  1.0 0.9 copy-start.4
  1.9 0.8 copy-start.10
  2.7 0.8 copy-start.11
  3.4 0.7 copy-start.13
  4.2 0.7 copy-start.14
  4.9 0.7 copy-start.15
  5.6 0.7 copy-start.16
  6.3 0.7 copy-start.17
  6.9 42.8 %copy-start.8 = (f32[64,192]{1,0:T(8,128)S(1)}, f32[64,192]{1,0:T(8,128)}, u32[]{:S(2)}) copy-start(f32[64,192]{1,0:T(8,128)} %constant.23.clone.tabz) | copy-start | bytes 147460
  25.9 23.7 %collective-permute-start = (f32[10,64,192]{2,1,0:T(8,128)S(1)}, f32[10,64,192]{2,1,0:T(8,128)S(1)}, u32[]{:S(2)}, u32[]{:S(2)}) collective-permute-start(f32[10,64,192]{2,1,0:T(8,128)S(1)} %get-tuple-element.26), channel_id=1, source_target_pairs={{0,16},{16,32},{32,48},{48,64},{64,80},{80,96},{96,112},{112,128},... | collective-permute-start | bytes 1474568 | tf_op jit(solution)/shard_map/ppermute | solution.py:460
  31.3 18.4 %collective-permute-start.1 = (f32[10,64,192]{2,1,0:T(8,128)S(1)}, f32[10,64,192]{2,1,0:T(8,128)S(1)}, u32[]{:S(2)}, u32[]{:S(2)}) collective-permute-start(f32[10,64,192]{2,1,0:T(8,128)S(1)} %get-tuple-element.27), channel_id=1, source_target_pairs={{16,0},{32,16},{48,32},{64,48},{80,64},{96,80},{112,96},{128,112},... | collective-permute-start | bytes 1474568 | tf_op jit(solution)/shard_map/ppermute | solution.py:460
  49.7 52.2 %copy-start.6 = (f32[256,128]{1,0:T(8,128)S(1)}, f32[256,128]{1,0:T(8,128)}, u32[]{:S(2)}) copy-start(f32[256,128]{1,0:T(8,128)} %constant.25.clone.side) | copy-start | bytes 393220
  49.7 52.2 %copy-start.12 = (f32[64,128]{1,0:T(8,128)S(1)}, f32[64,128]{1,0:T(8,128)}, u32[]{:S(2)}) copy-start(f32[64,128]{1,0:T(8,128)} %constant.24.clone.main) | copy-start | bytes 98308
  52.1 68.8 %copy-start.2 = (f32[512,64]{1,0:T(8,128)S(1)}, f32[512,64]{1,0:T(8,128)}, u32[]{:S(2)}) copy-start(f32[512,64]{1,0:T(8,128)} %constant.27.clone.inv) | copy-start | bytes 393220
  103.1 17.7 %all-to-all-start.1 = ((f32[32,8,128]{2,1,0:T(8,128)}), f32[32,8,128]{2,1,0:T(8,128)S(1)}, u32[]{:S(2)}, u32[]{:S(2)}) async-start(f32[32,8,128]{2,1,0:T(8,128)} %get-tuple-element.30), calls=%async_computation.1 | async-start | bytes 262144 | tf_op jit(solution)/shard_map/all_to_all | solution.py:455
  113.0 62.8 %copy-start.18 = (f32[64]{0:T(128)S(1)}, f32[64]{0:T(128)}, u32[]{:S(2)}) copy-start(f32[64]{0:T(128)} %param.30) | copy-start | bytes 772
  113.9 17.4 %collective-permute-start.3 = (f32[4,64,192]{2,1,0:T(8,128)}, f32[4,64,192]{2,1,0:T(8,128)S(1)}, u32[]{:S(2)}, u32[]{:S(2)}) collective-permute-start(f32[4,64,192]{2,1,0:T(8,128)} %get-tuple-element.33), channel_id=1, source_target_pairs={{1,0},{2,1},{3,2},{4,3},{5,4},{6,5},{7,6},{8,7},{9,8},{10,9},{11,1... | collective-permute-start | bytes 589832 | tf_op jit(solution)/shard_map/ppermute | solution.py:460
  115.8 15.5 %collective-permute-start.2 = (f32[4,64,192]{2,1,0:T(8,128)}, f32[4,64,192]{2,1,0:T(8,128)S(1)}, u32[]{:S(2)}, u32[]{:S(2)}) collective-permute-start(f32[4,64,192]{2,1,0:T(8,128)} %get-tuple-element.34), channel_id=1, source_target_pairs={{0,1},{1,2},{2,3},{3,4},{4,5},{5,6},{6,7},{7,8},{8,9},{9,10},{10,1... | collective-permute-start | bytes 589832 | tf_op jit(solution)/shard_map/ppermute | solution.py:460
  120.8 1.2 copy-start
  122.1 0.9 copy-start.5
  124.9 50.9 %copy-start.7 = (f32[64,192]{1,0:T(8,128)S(1)}, f32[64,192]{1,0:T(8,128)}, u32[]{:S(2)}) copy-start(f32[64,192]{1,0:T(8,128)} %constant.29.clone.tab) | copy-start | bytes 147460
  124.9 50.9 %copy-start.9 = (f32[64,64]{1,0:T(8,128)S(1)}, f32[64,64]{1,0:T(8,128)}, u32[]{:S(2)}) copy-start(f32[64,64]{1,0:T(8,128)} %skip.1) | copy-start | bytes 49156
  124.9 14.2 %all-to-all-start.2 = ((f32[32,8,128]{2,1,0:T(8,128)}), f32[32,8,128]{2,1,0:T(8,128)S(1)}, u32[]{:S(2)}, u32[]{:S(2)}) async-start(f32[32,8,128]{2,1,0:T(8,128)} %mix_x.1), calls=%async_computation.2 | async-start | bytes 262144 | tf_op jit(solution)/shard_map/all_to_all | solution.py:455
  139.1 0.9 copy-start.3

commit v3 on v2

--- a/solution.py
+++ b/solution.py
@@ -17,12 +17,13 @@
 MODES = 32
 CHUNK = 256
 SUB = 128
+FIRST = 5
 HALVES = 2 * CH
 
 F32 = jnp.float32
 BF16 = jnp.bfloat16
 HIGH = lax.Precision.HIGH
-LIMIT = pltpu.CompilerParams(vmem_limit_bytes=32 * 1024 * 1024)
+LIMIT = pltpu.CompilerParams(vmem_limit_bytes=24 * 1024 * 1024)
 
 NN = (((1,), (0,)), ((), ()))
 NT = (((1,), (1,)), ((), ()))
@@ -74,19 +75,10 @@
     return np.concatenate([c.T * w, -s.T * w], axis=0).astype(np.float32)
 
 
-def y_forward_tables(pens):
+def y_forward_table(pens):
     length = CY * pens
     c, s = angles(np.arange(length), length, True)
-    main = np.concatenate([c.T, s.T], axis=0)
-    side = np.zeros((CX, 2, MODES, pens, CX, 2))
-    for q in range(pens):
-        for h in range(2):
-            y = min(max(q * CY - 1 + h * (CY + 1), 0), length - 1)
-            for x in range(CX):
-                side[x, 0, :, q, x, h] = c[y]
-                side[x, 1, :, q, x, h] = s[y]
-    side = side.reshape(CX * 2 * MODES, pens * CX * 2)
-    return main.astype(np.float32), side.astype(np.float32)
+    return np.concatenate([c.T, s.T], axis=0).astype(np.float32)
 
 
 def y_inverse_table(pens):
@@ -170,12 +162,10 @@
             k = dx * 9 + dy * 3 + dz
             m = kern[j * CH:(j + 1) * CH] * (values * t[80 + k:81 + k])
             hi = m.astype(BF16)
-            lo = (m - hi.astype(F32)).astype(BF16)
             r = (dx * 3 + dy) * CH
             for s in range(CHUNK // SUB):
                 cut = slice(s * SUB, (s + 1) * SUB)
                 mess[s, r:r + CH, dz * SUB:(dz + 1) * SUB] = hi[:, cut]
-                mess[s, r:r + CH, (3 + dz) * SUB:(4 + dz) * SUB] = lo[:, cut]
         pend.clear()
 
     for dx in range(3):
@@ -190,22 +180,29 @@
     flush()
 
     lane = lax.broadcasted_iota(jnp.int32, (SUB, NZ), 1).astype(F32)
-    for s in range(CHUNK // SUB):
-        def column(c, _):
-            goal = lane + 256.0 * c.astype(F32)
+    longest = spans[0][1] - spans[0][0]
+    for begin, end in spans[1:]:
+        longest = jnp.maximum(longest, end - begin)
+
+    def column(j, _):
+        results = []
+        for s, (begin, end) in enumerate(spans):
+            c = jnp.minimum(begin + j, end - 1)
+            goal = lane + jnp.where(begin + j < end, 256.0 * c.astype(F32), -1.0e6)
             hot = jnp.concatenate(
                 [jnp.where(keys[dz, s * SUB:(s + 1) * SUB] == goal, 1.0, 0.0).astype(BF16)
                  for dz in range(3)], axis=0)
-            acc = mm(mess[s], jnp.concatenate([hot, hot], axis=0))
+            results.append((c, mm(mess[s], hot)))
+        for c, acc in results:
             cx = home_plane(lax.shift_right_logical(c, 3)) - plane0
             cy = jnp.bitwise_and(c, 7)
             for dx in range(3):
                 for dy in range(3):
                     r = (dx * 3 + dy) * CH
                     grid[cx + dx, cy + dy] += acc[r:r + CH]
-            return 0
-
-        lax.fori_loop(spans[s][0], spans[s][1], column, 0)
+        return 0
+
+    lax.fori_loop(0, longest, column, 0)
 
 
 def sides_kernel(last, at, feat_h, pos_h, home_h, nbr_h, deg_h, lift_h, first_h, bias_h, second_h,
@@ -228,7 +225,9 @@
     hz = home[2:3, :]
     order = jnp.where(hx == 0, 0, jnp.where(hx == CX - 1, 1, hx + 1))
     col = order * CY + hy
-    count[0] = jnp.sum(jnp.where(order < 2, 1.0, 0.0)).astype(jnp.int32)
+    outer = jnp.sum(jnp.where(order < 2, 1.0, 0.0)).astype(jnp.int32)
+    split = jnp.maximum((outer + CHUNK - 1) // CHUNK, FIRST)
+    count[0] = split
 
     ids = lax.broadcasted_iota(jnp.int32, (CX * CY, PTS), 0)
     carry = jnp.sum(jnp.where(col < ids, 1.0, 0.0), axis=1, keepdims=True)
@@ -270,7 +269,7 @@
         add_chunk(last, at, step, 0, data, rankb, taps, quad, lift_t, mess, keys, grid)
         return 0
 
-    lax.fori_loop(0, (count[0] + CHUNK - 1) // CHUNK, chunk, 0)
+    lax.fori_loop(0, split, chunk, 0)
     low[...] = grid[0]
     high[...] = grid[CX + 1]
 
@@ -282,14 +281,14 @@
         add_chunk(last, at, step, 1, data, rankb, taps, quad, lift_t, mess, keys, grid)
         return 0
 
-    lax.fori_loop((count[0] + CHUNK - 1) // CHUNK, PTS // CHUNK, chunk, 0)
+    lax.fori_loop(count[0], PTS // CHUNK, chunk, 0)
 
 
 def lift_points(at, last, feat, pos, home, nbr, deg, lift, first, bias, second):
     vmem = pl.BlockSpec(memory_space=pltpu.VMEM)
     smem = pl.BlockSpec(memory_space=pltpu.SMEM)
     work = [
-        pltpu.VMEM((CHUNK // SUB, 9 * CH, 6 * SUB), BF16),
+        pltpu.VMEM((CHUNK // SUB, 9 * CH, 3 * SUB), BF16),
         pltpu.VMEM((3, CHUNK, NZ), F32),
     ]
     inputs = (feat, pos, home, nbr, deg, lift, first, bias, second)
@@ -324,47 +323,65 @@
     return grid, low, high, middle
 
 
-def latent_kernel(last, at, tabz, sides, middle, below, above, spec, own, yedge):
+def latent_kernel(last, at, sides, middle, below, above, own, low_y, high_y):
     low = at[0] == 0
     top = at[0] == last
+    for x in range(CX):
+        for y in range(CY + 2):
+            l = sides[x + 1, y] + middle[x, y]
+            if x == 0:
+                l = l + jnp.where(low, sides[0, y], below[y])
+            if x == CX - 1:
+                l = l + jnp.where(top, sides[CX + 1, y], above[y])
+            if y == 0:
+                low_y[x] = l
+            elif y == CY + 1:
+                high_y[x] = l
+            else:
+                own[x * CY + y - 1] = l
+
+
+def z_modes(table, pair):
     lane = lax.broadcasted_iota(jnp.int32, (MODES, HALVES), 1)
+    d = mm(table, pair, NT, HIGH)
+    re, im = d[0:MODES], d[MODES:]
+    return jnp.where(lane < CH, re, swap(im)), jnp.where(lane < CH, swap(re), im)
+
+
+def inner_kernel(tabz, own, spec):
     table = tabz[...]
     for x in range(CX):
-        for yp in range((CY + 2) // 2):
-            cells = []
-            for y in (2 * yp, 2 * yp + 1):
-                l = sides[x + 1, y] + middle[x, y]
-                if x == 0:
-                    l = l + jnp.where(low, sides[0, y], below[y])
-                if x == CX - 1:
-                    l = l + jnp.where(top, sides[CX + 1, y], above[y])
-                cells.append(l)
-            d = mm(table, jnp.concatenate(cells, axis=0), NT, HIGH)
-            re, im = d[0:MODES], d[MODES:]
-            out = (jnp.where(lane < CH, re, swap(im)), jnp.where(lane < CH, swap(re), im))
-            for j in range(2):
-                y = 2 * yp + j
-                if y in (0, CY + 1):
-                    h = 0 if y == 0 else 1
-                    spec[:, CX * CY + x * 2 + h, :] = out[j]
-                    yedge[h, x] = cells[j]
-                else:
-                    spec[:, x * CY + y - 1, :] = out[j]
-                    own[x * CY + y - 1] = cells[j]
-
-
-def y_kernel(r, main, side, yedge, out, yedge_out):
+        for y in range(1, CY - 1, 2):
+            i = x * CY + y
+            u, v = z_modes(table, own[i:i + 2].reshape(2 * CH, NZ))
+            spec[:, i, :] = u
+            spec[:, i + 1, :] = v
+        spec[:, x * CY, :] = jnp.zeros((MODES, HALVES), F32)
+        spec[:, x * CY + CY - 1, :] = jnp.zeros((MODES, HALVES), F32)
+
+
+def outer_kernel(last, at, tabz, own, part, low_y, high_y, left, right, spec, ends):
+    first_pen = at[1] == 0
+    last_pen = at[1] == last
+    table = tabz[...]
+    spec[...] = part[...]
+    for x in range(CX):
+        a = own[x * CY] + jnp.where(first_pen, low_y[x], left[x])
+        b = own[x * CY + CY - 1] + jnp.where(last_pen, high_y[x], right[x])
+        u, v = z_modes(table, jnp.concatenate([a, b], axis=0))
+        spec[:, x * CY, :] = u
+        spec[:, x * CY + CY - 1, :] = v
+        ends[0, x] = a
+        ends[1, x] = b
+
+
+def y_kernel(r, main, out):
     sgn = sign_row((MODES, HALVES))
-    n = CX * CY
     pens = r.shape[0]
-    for kz in range(2):
-        o = kz * (n + 2 * CX)
-        halo = mm(side[...], r[:, o + n:o + n + 2 * CX, :].reshape(pens * 2 * CX, HALVES), NN, HIGH)
-        for x in range(CX):
-            rows = r[:, o + x * CY:o + (x + 1) * CY, :].reshape(pens * CY, HALVES)
-            ab = mm(main[...], rows, NN, HIGH) + halo[x * 2 * MODES:(x + 1) * 2 * MODES]
-            out[:, kz * CX + x, :] = ab[:MODES] + swap(ab[MODES:]) * sgn
-    yedge_out[...] = yedge[...]
+    for i in range(2 * CX):
+        rows = r[:, i * CY:(i + 1) * CY, :].reshape(pens * CY, HALVES)
+        ab = mm(main[...], rows, NN, HIGH)
+        out[:, i, :] = ab[:MODES] + swap(ab[MODES:]) * sgn
 
 
 def x_kernel(r, fwd, inv, w, out, lhs, res):
@@ -390,7 +407,7 @@
     out[...] = y.reshape(out.shape)
 
 
-def y_back_kernel(r, inv, left, right, out):
+def y_back_kernel(r, inv, out):
     rows = inv.shape[0] // 2
     sgn = sign_row((rows, HALVES))
     for i in range(2 * CX):
@@ -399,9 +416,7 @@
         out[:, i * CY:(i + 1) * CY, :] = y.reshape(rows // CY, CY, HALVES)
 
 
-def final_kernel(last, at, zb, tab, own, yedge, left, right, skip, bias, out):
-    first_pen = at[1] == 0
-    last_pen = at[1] == last
+def final_kernel(zb, tab, own, ends, skip, bias, out):
     lane = lax.broadcasted_iota(jnp.int32, (MODES, HALVES), 1)
     zero = jnp.zeros((CH, CH), F32)
     skip_t = jnp.transpose(skip[...])
@@ -421,22 +436,15 @@
             lat = []
             for j in range(2):
                 y = 2 * yp + j
-                l = own[i + j]
-                if y == 0:
-                    l = l + jnp.where(first_pen, yedge[0, x], left[x])
-                if y == CY - 1:
-                    l = l + jnp.where(last_pen, yedge[1, x], right[x])
-                lat.append(l)
+                lat.append(ends[0, x] if y == 0 else ends[1, x] if y == CY - 1 else own[i + j])
             total = spectral + mm(pair, jnp.concatenate(lat, axis=0), NN, HIGH) + col
             out[x, 2 * yp:2 * yp + 2] = gelu(total).astype(BF16).reshape(2, CH, NZ)
 
 
-def call(kernel, shapes, args, scratch=(), smem=False, name=None, unread=0):
+def call(kernel, shapes, args, scratch=(), smem=False, name=None):
     specs = [pl.BlockSpec(memory_space=pltpu.VMEM)] * len(args)
     if smem:
         specs[0] = pl.BlockSpec(memory_space=pltpu.SMEM)
-    for j in range(unread):
-        specs[-1 - j] = pl.BlockSpec(memory_space=pl.ANY)
     return pl.pallas_call(
         kernel,
         out_shape=shapes,
@@ -470,18 +478,20 @@
         degrees[None, :], lift_input, kernel_first, kernel_bias[None, :], kernel_second)
     below = moved(high, "bin", 1)
     above = moved(low, "bin", -1)
-    spec, own, yedge = call(
-        functools.partial(latent_kernel, bins - 1),
-        [shape(MODES, CX * (CY + 2), HALVES), shape(CX * CY, CH, NZ), shape(2, CX, CH, NZ)],
-        (at, jnp.asarray(z_forward_table()), sides, middle, below, above),
-        smem=True, name="latent_z")
-    rows = 2 * CX * (CY + 2)
-    r = exchange(spec.reshape(pens, rows, HALVES), "pen")
-    main, side = y_forward_tables(pens)
-    r, yedge = call(y_kernel, [shape(MODES, 2 * CX, HALVES), shape(2, CX, CH, NZ)],
-                    (r, jnp.asarray(main), jnp.asarray(side), yedge), name="forward_y")
-    left = moved(yedge[1], "pen", 1)
-    right = moved(yedge[0], "pen", -1)
+    half = shape(CX, CH, NZ)
+    own, low_y, high_y = call(
+        functools.partial(latent_kernel, bins - 1), [shape(CX * CY, CH, NZ), half, half],
+        (at, sides, middle, below, above), smem=True, name="latent")
+    left = moved(high_y, "pen", 1)
+    right = moved(low_y, "pen", -1)
+    table = jnp.asarray(z_forward_table())
+    spec = call(inner_kernel, shape(MODES, CX * CY, HALVES), (table, own), name="forward_z")
+    spec, ends = call(
+        functools.partial(outer_kernel, pens - 1), [shape(*spec.shape), shape(2, CX, CH, NZ)],
+        (at, table, own, spec, low_y, high_y, left, right), smem=True, name="forward_z_ends")
+    r = exchange(spec.reshape(pens, 2 * CX * CY, HALVES), "pen")
+    r = call(y_kernel, shape(MODES, 2 * CX, HALVES), (r, jnp.asarray(y_forward_table(pens))),
+             name="forward_y")
     r = exchange(r, "bin")
     fwd, inv = x_tables(bins)
     r = call(x_kernel, shape(MODES, 2 * CX, HALVES),
@@ -489,14 +499,12 @@
              scratch=[pltpu.VMEM((2 * MODES, 8, HALVES), F32)] * 2, name="mix_x")
     r = exchange(r, "bin")
     r = call(y_back_kernel, shape(pens, 2 * CX * CY, HALVES),
-             (r, jnp.asarray(y_inverse_table(pens)), left, right), unread=2, name="inverse_y")
+             (r, jnp.asarray(y_inverse_table(pens))), name="inverse_y")
     r = exchange(r, "pen")
     out = call(
-        functools.partial(final_kernel, pens - 1),
-        jax.ShapeDtypeStruct((CX, CY, CH, NZ), BF16),
-        (at, r.reshape(MODES, CX * CY, HALVES), jnp.asarray(z_inverse_table()), own,
-         yedge, left, right, skip_weights, skip_bias[None, :]),
-        smem=True, name="finish")
+        final_kernel, jax.ShapeDtypeStruct((CX, CY, CH, NZ), BF16),
+        (r.reshape(MODES, CX * CY, HALVES), jnp.asarray(z_inverse_table()), own, ends,
+         skip_weights, skip_bias[None, :]), name="finish")
     return out.transpose(0, 1, 3, 2)
 
 

time: 181 us -> 170 us (0.939)
  blocking collectives: 84.9 us -> 104 us
  starting transfers between devices: 28.9 us -> 11.4 us
  Pallas kernels: 46.2 us -> 38.5 us
  local copies, waits for them, and re-layouts: 10.8 us -> 6.89 us
    all_to_all x2 -> x4, blocking collectives: 84.9 us -> 104 us  [exchange(): return lax.all_to_all(x, axis, split_axis=0, concat_axis=0, tiled=True)]
    all_to_all x2 -> x0, starting transfers between devices: 16.4 us -> none  [exchange(): return lax.all_to_all(x, axis, split_axis=0, concat_axis=0, tiled=True)]
    all_to_all x2 -> x0, waiting for transfers between devices: 8.87 us -> none  [exchange(): return lax.all_to_all(x, axis, split_axis=0, concat_axis=0, tiled=True)]
    ppermute x4, waiting for transfers between devices: 0.01 us -> 7.77 us  [moved(): lax.ppermute(x, axis, [(i - step, i) for i in devices if i - step in devi...]
    pallas_call x1, Pallas kernels: 17 us -> 11.1 us  [lift_points(): pl.pallas_call(functools.partial(middle_kernel, last), out_shape=shape(CX...]
    unnamed x38 -> x36, local copies, waits for them, and re-layouts: 9.9 us -> 6.89 us
    pallas_call x5 -> x7, Pallas kernels: 10.1 us -> 8.99 us  [call(): pl.pallas_call(kernel, out_shape=shapes, in_specs=specs, scratch_shapes=l...]
  transfers between devices with their start and end apart: 6 -> 4, of which waited for: 2 -> 2; matrix products, arithmetic and copies ran while one was open for 0% -> 0% of each run, Pallas kernels for 11% -> 7%
where the time goes in v3:
time: 170 us; the launch traced here: 169 us
  blocking collectives  104 us (61%)
  Pallas kernels  38.5 us (23%)
  starting transfers between devices  11.4 us (7%)
  waiting for transfers between devices  7.77 us (5%)
  local copies, waits for them, and re-layouts  6.89 us (4%)
    all_to_all x4, blocking collectives, exchange(): return lax.all_to_all(x, axis, split_axis=0, concat_axis=0, tiled=True)  104 us
    pallas_call x1, Pallas kernels, lift_points(): pl.pallas_call(functools.partial(sides_kernel, last), out_shape=[shape(CX...  18.4 us
    ppermute x4, starting transfers between devices, moved(): lax.ppermute(x, axis, [(i - step, i) for i in devices if i - step in devi...  11.4 us
    pallas_call x1, Pallas kernels, lift_points(): pl.pallas_call(functools.partial(middle_kernel, last), out_shape=shape(CX...  11.1 us
    pallas_call x7, Pallas kernels, call(): pl.pallas_call(kernel, out_shape=shapes, in_specs=specs, scratch_shapes=l...  8.99 us
    ppermute x4, waiting for transfers between devices, moved(): lax.ppermute(x, axis, [(i - step, i) for i in devices if i - step in devi...  7.77 us
    unnamed x36, local copies, waits for them, and re-layouts  6.89 us
  transfers between devices with their start and end apart: 4, of which 2 were waited for; matrix products, arithmetic and copies ran while one was open for 0% of the time, Pallas kernels for 7%

profile of v3, /device:TPU:32, one launch (start us, length us, event | category | flops | bytes accessed | tf_op | source)
XLA Modules:
  0.0 168.9 jit_solution(9481630386789091293)
XLA Ops:
  0.0 0.1 pad_add_fusion.at
  0.1 0.9 copy-done.2
  1.0 0.9 copy-done.4
  1.9 0.8 copy-done.9
  2.7 0.8 copy-done.10
  3.5 0.7 copy-done.12
  4.2 0.7 copy-done.13
  4.9 0.7 copy-done.14
  5.6 0.7 copy-done.15
  6.3 0.7 copy-done.17
  6.9 18.4 %lift_sides.1 = (f32[6,10,64,192]{3,2,1,0:T(8,128)S(1)}, f32[10,64,192]{2,1,0:T(8,128)S(1)}, f32[10,64,192]{2,1,0:T(8,128)S(1)}, bf16[112,2048]{1,0:T(8,128)(2,1...) custom-call(s32[2]{0:T(128)S(1)} %pad_add_fusion.at, ...), custom_call_target="tpu_custom_call" | custom-call | tf_op jit(solution)/shard_map/lift_sides/pallas_call | solution.py:295
  25.3 2.9 %collective-permute-start = (f32[10,64,192]{2,1,0:T(8,128)S(1)}, f32[10,64,192]{2,1,0:T(8,128)S(1)}, u32[]{:S(2)}, u32[]{:S(2)}) collective-permute-start(f32[10,64,192]{2,1,0:T(8,128)S(1)} %get-tuple-element.26), channel_id=1, source_target_pairs={{0,16},{16,32},{32,48},{48,64},{64,80},{80,96},{96,112},{112,128},... | collective-permute-start | bytes 1474568 | tf_op jit(solution)/shard_map/ppermute | solution.py:468
  28.2 1.3 collective-permute-start.1
  29.5 11.1 %lift_middle.1.middle = f32[4,10,64,192]{3,2,1,0:T(8,128)S(1)} custom-call(s32[2]{0:T(128)S(1)} %pad_add_fusion.at, s32[1]{0:T(128)} %get-tuple-element.20.count, bf16[112,2048]{1,0:T(8,128)(2,1)S(1)} %get-tuple-element.21.data, s32[2048,128]{1,0:T(8,128)S(1)} %get-tuple-element.22.rankb, f32[4,64,256]{2,1,0:T(8,128)S(1)} %get-tuple-element.23.taps, ...), custom_call_target="tpu_custom_call" | custom-call | tf_op jit(solution)/shard_map/lift_middle/pallas_call | solution.py:315
  40.6 0.0 copy-start.1
  40.6 0.9 latent.1
  41.6 5.3 %collective-permute-start.3 = (f32[4,64,192]{2,1,0:T(8,128)S(1)}, f32[4,64,192]{2,1,0:T(8,128)S(1)}, u32[]{:S(2)}, u32[]{:S(2)}) collective-permute-start(f32[4,64,192]{2,1,0:T(8,128)S(1)} %get-tuple-element.29.low_y), channel_id=1, source_target_pairs={{1,0},{2,1},{3,2},{4,3},{5,4},{6,5},{7,6},{8,7},{9,8},{10,9},{11,1... | collective-permute-start | bytes 589832 | tf_op jit(solution)/shard_map/ppermute | solution.py:468
  46.9 1.9 %collective-permute-start.2 = (f32[4,64,192]{2,1,0:T(8,128)S(1)}, f32[4,64,192]{2,1,0:T(8,128)S(1)}, u32[]{:S(2)}, u32[]{:S(2)}) collective-permute-start(f32[4,64,192]{2,1,0:T(8,128)S(1)} %get-tuple-element.30.high_y), channel_id=1, source_target_pairs={{0,1},{1,2},{2,3},{3,4},{4,5},{5,6},{6,7},{7,8},{8,9},{9,10},{10,1... | collective-permute-start | bytes 589832 | tf_op jit(solution)/shard_map/ppermute | solution.py:468
  48.8 1.2 forward_z.1.part
  50.1 0.0 copy-start.3
  50.1 0.0 copy-start.6
  50.1 3.3 %collective-permute-done.3.right = f32[4,64,192]{2,1,0:T(8,128)S(1)} collective-permute-done((f32[4,64,192]{2,1,0:T(8,128)S(1)}, f32[4,64,192]{2,1,0:T(8,128)S(1)}, u32[]{:S(2)}, u32[]{:S(2)}) %collective-permute-start.3) | collective-permute-done | bytes 196640 | tf_op jit(solution)/shard_map/ppermute | solution.py:468
  53.4 4.4 %collective-permute-done.2.left = f32[4,64,192]{2,1,0:T(8,128)S(1)} collective-permute-done((f32[4,64,192]{2,1,0:T(8,128)S(1)}, f32[4,64,192]{2,1,0:T(8,128)S(1)}, u32[]{:S(2)}, u32[]{:S(2)}) %collective-permute-start.2) | collective-permute-done | bytes 196640 | tf_op jit(solution)/shard_map/ppermute | solution.py:468
  57.8 1.1 forward_z_ends.1
  59.0 40.5 %all_to_all.20.r = f32[16,64,128]{2,1,0:T(8,128)S(1)} all-to-all(f32[16,64,128]{2,1,0:T(8,128)S(1)} %bitcast.11), channel_id=1, replica_groups=mesh['bin'=32,'pen'=16] {'pen'}, dimensions={0} | all-to-all | bytes 1048576 | tf_op jit(solution)/shard_map/all_to_all | solution.py:463
  99.5 0.4 forward_y.1
  99.9 16.1 %all_to_all.21.r = f32[32,8,128]{2,1,0:T(8,128)S(1)} all-to-all(f32[32,8,128]{2,1,0:T(8,128)S(1)} %forward_y.1), channel_id=1, replica_groups=mesh['bin'=32,'pen'=16] {'bin'}, dimensions={0} | all-to-all | bytes 262144 | tf_op jit(solution)/shard_map/all_to_all | solution.py:463
  116.0 1.3 mix_x.1
  117.3 11.3 %all_to_all.22.r = f32[32,8,128]{2,1,0:T(8,128)S(1)} all-to-all(f32[32,8,128]{2,1,0:T(8,128)S(1)} %mix_x.1), channel_id=1, replica_groups=mesh['bin'=32,'pen'=16] {'bin'}, dimensions={0} | all-to-all | bytes 262144 | tf_op jit(solution)/shard_map/all_to_all | solution.py:463
  128.5 0.6 inverse_y.1
  129.2 36.2 %all_to_all.23 = f32[16,64,128]{2,1,0:T(8,128)S(1)} all-to-all(f32[16,64,128]{2,1,0:T(8,128)S(1)} %inverse_y.1), channel_id=1, replica_groups=mesh['bin'=32,'pen'=16] {'pen'}, dimensions={0} | all-to-all | bytes 1048576 | tf_op jit(solution)/shard_map/all_to_all | solution.py:463
  165.4 3.5 %finish.1 = bf16[4,8,64,192]{3,2,1,0:T(8,128)(2,1)} custom-call(f32[32,32,128]{2,1,0:T(8,128)S(1)} %bitcast.10, f32[64,192]{1,0:T(8,128)S(1)} %copy-done.7, f32[32,64,192]{2,1,0:T(8,128)S(1)} %get-tuple-element.28.own, f32[2,4,64,192]{3,2,1,0:T(8,128)S(1)} %get-tuple-element.32.ends, f32[64,64]{1,0:T(8,128)S(1)} %copy-done.8, f32[1,64]{1,0:T(1,128)S(1)} %bitcast.15), custom_call_target="tpu_custom_call" | custom-call | tf_op jit(solution)/shard_map/finish/pallas_call | solution.py:448
  (26 shorter events, 0.1 us)
Async XLA Ops:
  0.1 0.9 copy-start.2
  1.0 0.9 copy-start.4
  1.9 0.8 copy-start.9
  2.7 0.8 copy-start.10
  3.4 0.7 copy-start.12
  4.2 0.7 copy-start.13
  4.9 0.7 copy-start.14
  5.6 0.7 copy-start.15
  6.3 0.7 copy-start.17
  25.3 15.3 %collective-permute-start = (f32[10,64,192]{2,1,0:T(8,128)S(1)}, f32[10,64,192]{2,1,0:T(8,128)S(1)}, u32[]{:S(2)}, u32[]{:S(2)}) collective-permute-start(f32[10,64,192]{2,1,0:T(8,128)S(1)} %get-tuple-element.26), channel_id=1, source_target_pairs={{0,16},{16,32},{32,48},{48,64},{64,80},{80,96},{96,112},{112,128},... | collective-permute-start | bytes 1474568 | tf_op jit(solution)/shard_map/ppermute | solution.py:468
  28.2 12.4 %collective-permute-start.1 = (f32[10,64,192]{2,1,0:T(8,128)S(1)}, f32[10,64,192]{2,1,0:T(8,128)S(1)}, u32[]{:S(2)}, u32[]{:S(2)}) collective-permute-start(f32[10,64,192]{2,1,0:T(8,128)S(1)} %get-tuple-element.27), channel_id=1, source_target_pairs={{16,0},{32,16},{48,32},{64,48},{80,64},{96,80},{112,96},{128,112},... | collective-permute-start | bytes 1474568 | tf_op jit(solution)/shard_map/ppermute | solution.py:468
  40.6 8.2 %copy-start.1 = (f32[64,192]{1,0:T(8,128)S(1)}, f32[64,192]{1,0:T(8,128)}, u32[]{:S(2)}) copy-start(f32[64,192]{1,0:T(8,128)} %constant.21.clone.tabz) | copy-start | bytes 147460
  41.6 11.8 %collective-permute-start.3 = (f32[4,64,192]{2,1,0:T(8,128)S(1)}, f32[4,64,192]{2,1,0:T(8,128)S(1)}, u32[]{:S(2)}, u32[]{:S(2)}) collective-permute-start(f32[4,64,192]{2,1,0:T(8,128)S(1)} %get-tuple-element.29.low_y), channel_id=1, source_target_pairs={{1,0},{2,1},{3,2},{4,3},{5,4},{6,5},{7,6},{8,7},{9,8},{10,9},{11,1... | collective-permute-start | bytes 589832 | tf_op jit(solution)/shard_map/ppermute | solution.py:468
  46.9 10.9 %collective-permute-start.2 = (f32[4,64,192]{2,1,0:T(8,128)S(1)}, f32[4,64,192]{2,1,0:T(8,128)S(1)}, u32[]{:S(2)}, u32[]{:S(2)}) collective-permute-start(f32[4,64,192]{2,1,0:T(8,128)S(1)} %get-tuple-element.30.high_y), channel_id=1, source_target_pairs={{0,1},{1,2},{2,3},{3,4},{4,5},{5,6},{6,7},{7,8},{8,9},{9,10},{10,1... | collective-permute-start | bytes 589832 | tf_op jit(solution)/shard_map/ppermute | solution.py:468
  50.0 49.4 %copy-start.11 = (f32[64,128]{1,0:T(8,128)S(1)}, f32[64,128]{1,0:T(8,128)}, u32[]{:S(2)}) copy-start(f32[64,128]{1,0:T(8,128)} %constant.22.clone.main) | copy-start | bytes 98308
  50.0 65.9 %copy-start = (bf16[32,1,2,64,128]{4,3,2,1,0:T(8,128)(2,1)S(1)}, bf16[32,1,2,64,128]{4,3,2,1,0:T(8,128)(2,1)}, u32[]{:S(2)}) copy-start(bf16[32,1,2,64,128]{4,3,2,1,0:T(8,128)(2,1)} %w.1) | copy-start | bytes 3145732
  50.1 65.9 %copy-start.3 = (f32[512,64]{1,0:T(8,128)S(1)}, f32[512,64]{1,0:T(8,128)}, u32[]{:S(2)}) copy-start(f32[512,64]{1,0:T(8,128)} %constant.24.clone.inv) | copy-start | bytes 393220
  50.1 65.9 %copy-start.6 = (f32[128,256]{1,0:T(8,128)S(1)}, f32[128,256]{1,0:T(8,128)}, u32[]{:S(2)}) copy-start(f32[128,256]{1,0:T(8,128)} %constant.23.clone.fwd) | copy-start | bytes 393220
  58.9 69.6 %copy-start.5 = (f32[256,32]{1,0:T(8,128)S(1)}, f32[256,32]{1,0:T(8,128)}, u32[]{:S(2)}) copy-start(f32[256,32]{1,0:T(8,128)} %constant.25.clone.inv) | copy-start | bytes 98308
  99.5 65.9 %copy-start.7 = (f32[64,192]{1,0:T(8,128)S(1)}, f32[64,192]{1,0:T(8,128)}, u32[]{:S(2)}) copy-start(f32[64,192]{1,0:T(8,128)} %constant.26.clone.tab) | copy-start | bytes 147460
  99.5 65.9 %copy-start.8 = (f32[64,64]{1,0:T(8,128)S(1)}, f32[64,64]{1,0:T(8,128)}, u32[]{:S(2)}) copy-start(f32[64,64]{1,0:T(8,128)} %skip.1) | copy-start | bytes 49156
  99.5 65.9 %copy-start.16 = (f32[64]{0:T(128)S(1)}, f32[64]{0:T(128)}, u32[]{:S(2)}) copy-start(f32[64]{0:T(128)} %param.29) | copy-start | bytes 772

commit v4 on v3

--- a/solution.py
+++ b/solution.py
@@ -17,6 +17,7 @@
 MODES = 32
 CHUNK = 256
 SUB = 128
+LARGE = 512
 FIRST = 5
 HALVES = 2 * CH
 
@@ -113,25 +114,24 @@
     return jnp.where(order == 0, 0, jnp.where(order == 1, CX - 1, order - 1))
 
 
-def add_chunk(last, at, step, plane0, data, rankb, taps, quad, lift_t, mess, keys, grid):
-    base = step * CHUNK
+def add_chunk(last, at, base, size, plane0, data, rankb, taps, quad, lift_t, mess, keys, grid):
     lanes = lax.broadcasted_iota(jnp.int32, (PTS, 128), 1) + base
     perm = jnp.concatenate(
         [jnp.where(rankb[...] == lanes + j * 128, 1.0, 0.0).astype(BF16)
-         for j in range(CHUNK // 128)], axis=1)
+         for j in range(size // 128)], axis=1)
     t = mm(data[...], perm)
     hzs = t[73:74]
     cols = t[74:75]
     spans = [(jnp.min(cols[:, j * SUB:(j + 1) * SUB]).astype(jnp.int32),
               jnp.max(cols[:, j * SUB:(j + 1) * SUB]).astype(jnp.int32) + 1)
-             for j in range(CHUNK // SUB)]
+             for j in range(size // SUB)]
     key = 256.0 * cols
     key = jnp.concatenate(
         [key + jnp.maximum(hzs - 1.0, 0.0), key + hzs, key + jnp.minimum(hzs + 1.0, NZ - 1.0),
-         jnp.zeros((5, CHUNK), F32)], axis=0)
+         jnp.zeros((5, size), F32)], axis=0)
     key = jnp.transpose(key)
     for dz in range(3):
-        keys[dz] = jnp.broadcast_to(key[:, dz:dz + 1], (CHUNK, NZ))
+        keys[dz, 0:size] = jnp.broadcast_to(key[:, dz:dz + 1], (size, NZ))
 
     values = mm(lift_t[...], t[0:64].astype(BF16))
     ox = t[64:65] + t[65:66] + t[66:67]
@@ -140,7 +140,7 @@
     coli = cols.astype(jnp.int32)
     gx = home_plane(lax.shift_right_logical(coli, 3)) + at[0] * CX
     gy = jnp.bitwise_and(coli, 7) + at[1] * CY
-    k_x, k_y, k_z, k_b = taps[0], taps[1], taps[2], taps[3]
+    k_x, k_y, k_z, k_b = (taps[j, :, 0:size] for j in range(4))
 
     def ends(g, end):
         return (jnp.where(g > 0, -1.0, 0.0), None, jnp.where(g < end, 1.0, 0.0))
@@ -153,7 +153,7 @@
 
     def flush():
         while len(pend) < 4:
-            pend.append((None, jnp.zeros((CH, CHUNK), BF16)))
+            pend.append((None, jnp.zeros((CH, size), BF16)))
         kern = mm(quad[...], jnp.concatenate([h for _, h in pend], axis=0))
         for j, (where, _) in enumerate(pend):
             if where is None:
@@ -163,7 +163,7 @@
             m = kern[j * CH:(j + 1) * CH] * (values * t[80 + k:81 + k])
             hi = m.astype(BF16)
             r = (dx * 3 + dy) * CH
-            for s in range(CHUNK // SUB):
+            for s in range(size // SUB):
                 cut = slice(s * SUB, (s + 1) * SUB)
                 mess[s, r:r + CH, dz * SUB:(dz + 1) * SUB] = hi[:, cut]
         pend.clear()
@@ -192,14 +192,13 @@
             hot = jnp.concatenate(
                 [jnp.where(keys[dz, s * SUB:(s + 1) * SUB] == goal, 1.0, 0.0).astype(BF16)
                  for dz in range(3)], axis=0)
-            results.append((c, mm(mess[s], hot)))
+            results.append((c, [mm(mess[s, q * 3 * CH:(q + 1) * 3 * CH], hot) for q in range(3)]))
         for c, acc in results:
             cx = home_plane(lax.shift_right_logical(c, 3)) - plane0
             cy = jnp.bitwise_and(c, 7)
             for dx in range(3):
                 for dy in range(3):
-                    r = (dx * 3 + dy) * CH
-                    grid[cx + dx, cy + dy] += acc[r:r + CH]
+                    grid[cx + dx, cy + dy] += acc[dx][dy * CH:(dy + 1) * CH]
         return 0
 
     lax.fori_loop(0, longest, column, 0)
@@ -257,7 +256,7 @@
     flat = jnp.concatenate([flat, jnp.zeros((8, 128 - CH), F32)], axis=1)
     flat = jnp.transpose(flat)
     for j in range(4):
-        taps[j] = jnp.broadcast_to(flat[0:CH, j:j + 1], (CH, CHUNK))
+        taps[j] = jnp.broadcast_to(flat[0:CH, j:j + 1], (CH, LARGE))
     zero = jnp.zeros((CH, CH), F32)
     sec_t = jnp.transpose(second[...].astype(F32))
     quad[...] = jnp.concatenate(
@@ -265,11 +264,14 @@
          for i in range(4)], axis=0).astype(BF16)
     lift_t[...] = jnp.transpose(lift[...].astype(F32)).astype(BF16)
 
-    def chunk(step, _):
-        add_chunk(last, at, step, 0, data, rankb, taps, quad, lift_t, mess, keys, grid)
+    def chunk(size, first, step, _):
+        add_chunk(last, at, first + step * size, size, 0, data, rankb, taps, quad, lift_t, mess,
+                  keys, grid)
         return 0
 
-    lax.fori_loop(0, split, chunk, 0)
+    large = split // 2
+    lax.fori_loop(0, large, functools.partial(chunk, LARGE, 0), 0)
+    lax.fori_loop(0, split - 2 * large, functools.partial(chunk, CHUNK, large * LARGE), 0)
     low[...] = grid[0]
     high[...] = grid[CX + 1]
 
@@ -277,21 +279,28 @@
 def middle_kernel(last, at, count, data, rankb, taps, quad, lift_t, grid, mess, keys):
     grid[...] = jnp.zeros_like(grid)
 
-    def chunk(step, _):
-        add_chunk(last, at, step, 1, data, rankb, taps, quad, lift_t, mess, keys, grid)
+    def chunk(size, first, step, _):
+        add_chunk(last, at, first + step * size, size, 1, data, rankb, taps, quad, lift_t, mess,
+                  keys, grid)
         return 0
 
-    lax.fori_loop(count[0], PTS // CHUNK, chunk, 0)
+    split = count[0]
+    odd = jnp.bitwise_and(split, 1)
+    large = (PTS // CHUNK - split) // 2
+    lax.fori_loop(0, odd, functools.partial(chunk, CHUNK, split * CHUNK), 0)
+    lax.fori_loop(0, large, functools.partial(chunk, LARGE, (split + odd) * CHUNK), 0)
 
 
 def lift_points(at, last, feat, pos, home, nbr, deg, lift, first, bias, second):
     vmem = pl.BlockSpec(memory_space=pltpu.VMEM)
     smem = pl.BlockSpec(memory_space=pltpu.SMEM)
     work = [
-        pltpu.VMEM((CHUNK // SUB, 9 * CH, 3 * SUB), BF16),
-        pltpu.VMEM((3, CHUNK, NZ), F32),
+        pltpu.VMEM((LARGE // SUB, 9 * CH, 3 * SUB), BF16),
+        pltpu.VMEM((3, LARGE, NZ), F32),
     ]
-    inputs = (feat, pos, home, nbr, deg, lift, first, bias, second)
+    inputs = tuple(
+        pltpu.with_memory_space_constraint(x, pltpu.HBM)
+        for x in (feat, pos, home, nbr, deg, lift, first, bias, second))
     grid, low, high, *prepared, count = pl.pallas_call(
         functools.partial(sides_kernel, last),
         out_shape=[
@@ -300,7 +309,7 @@
             shape(CY + 2, CH, NZ),
             jax.ShapeDtypeStruct((112, PTS), BF16),
             jax.ShapeDtypeStruct((PTS, 128), jnp.int32),
-            shape(4, CH, CHUNK),
+            shape(4, CH, LARGE),
             jax.ShapeDtypeStruct((4 * CH, 4 * CH), BF16),
             jax.ShapeDtypeStruct((CH, CH), BF16),
             jax.ShapeDtypeStruct((1,), jnp.int32),

time: 170 us -> 160 us (0.941)
  local copies, waits for them, and re-layouts: 6.89 us -> 0.05 us
  Pallas kernels: 38.5 us -> 35 us
    unnamed x36 -> x18, local copies, waits for them, and re-layouts: 6.89 us -> 0.05 us
    pallas_call x1, Pallas kernels: 18.4 us -> 16 us  [lift_points(): pl.pallas_call(functools.partial(sides_kernel, last), out_shape=[shape(CX...]
    ppermute x4, starting transfers between devices: 11.4 us -> 13.1 us  [moved(): lax.ppermute(x, axis, [(i - step, i) for i in devices if i - step in devi...]
where the time goes in v4:
time: 160 us
  blocking collectives  104 us (65%)
  Pallas kernels  35 us (22%)
  starting transfers between devices  13.1 us (8%)
  waiting for transfers between devices  7.11 us (4%)
    all_to_all x4, blocking collectives, exchange(): return lax.all_to_all(x, axis, split_axis=0, concat_axis=0, tiled=True)  104 us
    pallas_call x1, Pallas kernels, lift_points(): pl.pallas_call(functools.partial(sides_kernel, last), out_shape=[shape(CX...  16 us
    ppermute x4, starting transfers between devices, moved(): lax.ppermute(x, axis, [(i - step, i) for i in devices if i - step in devi...  13.1 us
    pallas_call x1, Pallas kernels, lift_points(): pl.pallas_call(functools.partial(middle_kernel, last), out_shape=shape(CX...  10 us
    pallas_call x7, Pallas kernels, call(): pl.pallas_call(kernel, out_shape=shapes, in_specs=specs, scratch_shapes=l...  9 us
    ppermute x4, waiting for transfers between devices, moved(): lax.ppermute(x, axis, [(i - step, i) for i in devices if i - step in devi...  7.11 us
  transfers between devices with their start and end apart: 4, of which 2 were waited for; matrix products, arithmetic and copies ran while one was open for 0% of the time, Pallas kernels for 7%

profile of v4, /device:TPU:32, one launch (start us, length us, event | category | flops | bytes accessed | tf_op | source)
XLA Modules:
  0.0 159.7 jit_solution(6942800955002826007)
XLA Ops:
  0.0 0.1 pad_add_fusion.at
  0.1 16.0 %lift_sides.1 = (f32[6,10,64,192]{3,2,1,0:T(8,128)S(1)}, f32[10,64,192]{2,1,0:T(8,128)S(1)}, f32[10,64,192]{2,1,0:T(8,128)S(1)}, bf16[112,2048]{1,0:T(8,128)(2,1...) custom-call(s32[2]{0:T(128)S(1)} %pad_add_fusion.at, ...), custom_call_target="tpu_custom_call" | custom-call | tf_op jit(solution)/shard_map/lift_sides/pallas_call | solution.py:304
  16.1 2.7 %collective-permute-start = (f32[10,64,192]{2,1,0:T(8,128)S(1)}, f32[10,64,192]{2,1,0:T(8,128)S(1)}, u32[]{:S(2)}, u32[]{:S(2)}) collective-permute-start(f32[10,64,192]{2,1,0:T(8,128)S(1)} %get-tuple-element.26), channel_id=1, source_target_pairs={{0,16},{16,32},{32,48},{48,64},{64,80},{80,96},{96,112},{112,128},... | collective-permute-start | bytes 1474568 | tf_op jit(solution)/shard_map/ppermute | solution.py:477
  18.8 1.3 collective-permute-start.1
  20.1 10.0 %lift_middle.1.middle = f32[4,10,64,192]{3,2,1,0:T(8,128)S(1)} custom-call(s32[2]{0:T(128)S(1)} %pad_add_fusion.at, s32[1]{0:T(128)} %get-tuple-element.20.count, bf16[112,2048]{1,0:T(8,128)(2,1)S(1)} %get-tuple-element.21.data, s32[2048,128]{1,0:T(8,128)S(1)} %get-tuple-element.22.rankb, f32[4,64,512]{2,1,0:T(8,128)S(1)} %get-tuple-element.23.taps, ...), custom_call_target="tpu_custom_call" | custom-call | tf_op jit(solution)/shard_map/lift_middle/pallas_call | solution.py:324
  30.1 0.0 collective-permute-done.below
  30.1 0.0 collective-permute-done.1.above
  30.1 0.0 copy-start.1
  30.1 0.9 latent.1
  31.1 7.1 %collective-permute-start.3 = (f32[4,64,192]{2,1,0:T(8,128)S(1)}, f32[4,64,192]{2,1,0:T(8,128)S(1)}, u32[]{:S(2)}, u32[]{:S(2)}) collective-permute-start(f32[4,64,192]{2,1,0:T(8,128)S(1)} %get-tuple-element.29.low_y), channel_id=1, source_target_pairs={{1,0},{2,1},{3,2},{4,3},{5,4},{6,5},{7,6},{8,7},{9,8},{10,9},{11,1... | collective-permute-start | bytes 589832 | tf_op jit(solution)/shard_map/ppermute | solution.py:477
  38.1 2.1 %collective-permute-start.2 = (f32[4,64,192]{2,1,0:T(8,128)S(1)}, f32[4,64,192]{2,1,0:T(8,128)S(1)}, u32[]{:S(2)}, u32[]{:S(2)}) collective-permute-start(f32[4,64,192]{2,1,0:T(8,128)S(1)} %get-tuple-element.30.high_y), channel_id=1, source_target_pairs={{0,1},{1,2},{2,3},{3,4},{4,5},{5,6},{6,7},{7,8},{8,9},{9,10},{10,1... | collective-permute-start | bytes 589832 | tf_op jit(solution)/shard_map/ppermute | solution.py:477
  40.2 0.0 copy-done.1
  40.3 1.2 forward_z.1.part
  41.5 0.0 copy-start.7
  41.5 0.0 copy-start
  41.5 0.0 copy-start.2
  41.5 0.0 copy-start.4
  41.5 3.0 %collective-permute-done.3.right = f32[4,64,192]{2,1,0:T(8,128)S(1)} collective-permute-done((f32[4,64,192]{2,1,0:T(8,128)S(1)}, f32[4,64,192]{2,1,0:T(8,128)S(1)}, u32[]{:S(2)}, u32[]{:S(2)}) %collective-permute-start.3) | collective-permute-done | bytes 196640 | tf_op jit(solution)/shard_map/ppermute | solution.py:477
  44.5 4.1 %collective-permute-done.2.left = f32[4,64,192]{2,1,0:T(8,128)S(1)} collective-permute-done((f32[4,64,192]{2,1,0:T(8,128)S(1)}, f32[4,64,192]{2,1,0:T(8,128)S(1)}, u32[]{:S(2)}, u32[]{:S(2)}) %collective-permute-start.2) | collective-permute-done | bytes 196640 | tf_op jit(solution)/shard_map/ppermute | solution.py:477
  48.6 1.1 forward_z_ends.1
  49.7 0.0 copy-start.3
  49.7 35.9 %all_to_all.20.r = f32[16,64,128]{2,1,0:T(8,128)S(1)} all-to-all(f32[16,64,128]{2,1,0:T(8,128)S(1)} %bitcast.11), channel_id=1, replica_groups=mesh['bin'=32,'pen'=16] {'pen'}, dimensions={0} | all-to-all | bytes 1048576 | tf_op jit(solution)/shard_map/all_to_all | solution.py:472
  85.6 0.0 copy-done.7
  85.6 0.4 forward_y.1
  86.1 22.0 %all_to_all.21.r = f32[32,8,128]{2,1,0:T(8,128)S(1)} all-to-all(f32[32,8,128]{2,1,0:T(8,128)S(1)} %forward_y.1), channel_id=1, replica_groups=mesh['bin'=32,'pen'=16] {'bin'}, dimensions={0} | all-to-all | bytes 262144 | tf_op jit(solution)/shard_map/all_to_all | solution.py:472
  108.1 0.0 copy-done.4
  108.1 1.3 mix_x.1
  109.3 11.3 %all_to_all.22.r = f32[32,8,128]{2,1,0:T(8,128)S(1)} all-to-all(f32[32,8,128]{2,1,0:T(8,128)S(1)} %mix_x.1), channel_id=1, replica_groups=mesh['bin'=32,'pen'=16] {'bin'}, dimensions={0} | all-to-all | bytes 262144 | tf_op jit(solution)/shard_map/all_to_all | solution.py:472
  120.6 0.6 inverse_y.1
  121.3 34.9 %all_to_all.23 = f32[16,64,128]{2,1,0:T(8,128)S(1)} all-to-all(f32[16,64,128]{2,1,0:T(8,128)S(1)} %inverse_y.1), channel_id=1, replica_groups=mesh['bin'=32,'pen'=16] {'pen'}, dimensions={0} | all-to-all | bytes 1048576 | tf_op jit(solution)/shard_map/all_to_all | solution.py:472
  156.2 0.0 copy-done.8
  156.2 3.5 %finish.1 = bf16[4,8,64,192]{3,2,1,0:T(8,128)(2,1)} custom-call(f32[32,32,128]{2,1,0:T(8,128)S(1)} %bitcast.10, f32[64,192]{1,0:T(8,128)S(1)} %copy-done.5, f32[32,64,192]{2,1,0:T(8,128)S(1)} %get-tuple-element.28.own, f32[2,4,64,192]{3,2,1,0:T(8,128)S(1)} %get-tuple-element.32.ends, f32[64,64]{1,0:T(8,128)S(1)} %copy-done.6, f32[1,64]{1,0:T(1,128)S(1)} %bitcast.12), custom_call_target="tpu_custom_call" | custom-call | tf_op jit(solution)/shard_map/finish/pallas_call | solution.py:457
  (8 shorter events, 0.0 us)
Async XLA Ops:
  16.1 14.0 %collective-permute-start = (f32[10,64,192]{2,1,0:T(8,128)S(1)}, f32[10,64,192]{2,1,0:T(8,128)S(1)}, u32[]{:S(2)}, u32[]{:S(2)}) collective-permute-start(f32[10,64,192]{2,1,0:T(8,128)S(1)} %get-tuple-element.26), channel_id=1, source_target_pairs={{0,16},{16,32},{32,48},{48,64},{64,80},{80,96},{96,112},{112,128},... | collective-permute-start | bytes 1474568 | tf_op jit(solution)/shard_map/ppermute | solution.py:477
  18.8 11.3 %collective-permute-start.1 = (f32[10,64,192]{2,1,0:T(8,128)S(1)}, f32[10,64,192]{2,1,0:T(8,128)S(1)}, u32[]{:S(2)}, u32[]{:S(2)}) collective-permute-start(f32[10,64,192]{2,1,0:T(8,128)S(1)} %get-tuple-element.27), channel_id=1, source_target_pairs={{16,0},{32,16},{48,32},{64,48},{80,64},{96,80},{112,96},{128,112},... | collective-permute-start | bytes 1474568 | tf_op jit(solution)/shard_map/ppermute | solution.py:477
  30.1 10.1 %copy-start.1 = (f32[64,192]{1,0:T(8,128)S(1)}, f32[64,192]{1,0:T(8,128)}, u32[]{:S(2)}) copy-start(f32[64,192]{1,0:T(8,128)} %constant.21.clone.tabz) | copy-start | bytes 147460
  31.1 13.4 %collective-permute-start.3 = (f32[4,64,192]{2,1,0:T(8,128)S(1)}, f32[4,64,192]{2,1,0:T(8,128)S(1)}, u32[]{:S(2)}, u32[]{:S(2)}) collective-permute-start(f32[4,64,192]{2,1,0:T(8,128)S(1)} %get-tuple-element.29.low_y), channel_id=1, source_target_pairs={{1,0},{2,1},{3,2},{4,3},{5,4},{6,5},{7,6},{8,7},{9,8},{10,9},{11,1... | collective-permute-start | bytes 589832 | tf_op jit(solution)/shard_map/ppermute | solution.py:477
  38.1 10.5 %collective-permute-start.2 = (f32[4,64,192]{2,1,0:T(8,128)S(1)}, f32[4,64,192]{2,1,0:T(8,128)S(1)}, u32[]{:S(2)}, u32[]{:S(2)}) collective-permute-start(f32[4,64,192]{2,1,0:T(8,128)S(1)} %get-tuple-element.30.high_y), channel_id=1, source_target_pairs={{0,1},{1,2},{2,3},{3,4},{4,5},{5,6},{6,7},{7,8},{8,9},{9,10},{10,1... | collective-permute-start | bytes 589832 | tf_op jit(solution)/shard_map/ppermute | solution.py:477
  41.5 44.2 %copy-start.7 = (f32[64,128]{1,0:T(8,128)S(1)}, f32[64,128]{1,0:T(8,128)}, u32[]{:S(2)}) copy-start(f32[64,128]{1,0:T(8,128)} %constant.22.clone.main) | copy-start | bytes 98308
  41.5 66.6 %copy-start = (bf16[32,1,2,64,128]{4,3,2,1,0:T(8,128)(2,1)S(1)}, bf16[32,1,2,64,128]{4,3,2,1,0:T(8,128)(2,1)}, u32[]{:S(2)}) copy-start(bf16[32,1,2,64,128]{4,3,2,1,0:T(8,128)(2,1)} %w.1) | copy-start | bytes 3145732
  41.5 66.6 %copy-start.2 = (f32[512,64]{1,0:T(8,128)S(1)}, f32[512,64]{1,0:T(8,128)}, u32[]{:S(2)}) copy-start(f32[512,64]{1,0:T(8,128)} %constant.24.clone.inv) | copy-start | bytes 393220
  41.5 66.6 %copy-start.4 = (f32[128,256]{1,0:T(8,128)S(1)}, f32[128,256]{1,0:T(8,128)}, u32[]{:S(2)}) copy-start(f32[128,256]{1,0:T(8,128)} %constant.23.clone.fwd) | copy-start | bytes 393220
  49.7 70.9 %copy-start.3 = (f32[256,32]{1,0:T(8,128)S(1)}, f32[256,32]{1,0:T(8,128)}, u32[]{:S(2)}) copy-start(f32[256,32]{1,0:T(8,128)} %constant.25.clone.inv) | copy-start | bytes 98308
  85.6 70.6 %copy-start.5 = (f32[64,192]{1,0:T(8,128)S(1)}, f32[64,192]{1,0:T(8,128)}, u32[]{:S(2)}) copy-start(f32[64,192]{1,0:T(8,128)} %constant.26.clone.tab) | copy-start | bytes 147460
  85.6 70.6 %copy-start.6 = (f32[64,64]{1,0:T(8,128)S(1)}, f32[64,64]{1,0:T(8,128)}, u32[]{:S(2)}) copy-start(f32[64,64]{1,0:T(8,128)} %skip.1) | copy-start | bytes 49156
  85.6 70.6 %copy-start.8 = (f32[64]{0:T(128)S(1)}, f32[64]{0:T(128)}, u32[]{:S(2)}) copy-start(f32[64]{0:T(128)} %param.29) | copy-start | bytes 772

commit v5 on v4

--- a/solution.py
+++ b/solution.py
@@ -19,6 +19,7 @@
 SUB = 128
 LARGE = 512
 FIRST = 5
+SECOND = 6
 HALVES = 2 * CH
 
 F32 = jnp.float32
@@ -110,8 +111,28 @@
     return hi, mid, rest - mid
 
 
-def home_plane(order):
-    return jnp.where(order == 0, 0, jnp.where(order == 1, CX - 1, order - 1))
+SIDE = 2 * CY
+BOTH = SIDE + 4
+
+
+def column_rank(hx, hy):
+    side = jnp.where(hx == 0, 0, CY) + hy
+    end = SIDE + (hx - 1) * 2 + jnp.where(hy == 0, 0, 1)
+    core = BOTH + (hx - 1) * (CY - 2) + hy - 1
+    inner = jnp.where((hy == 0) | (hy == CY - 1), end, core)
+    return jnp.where((hx == 0) | (hx == CX - 1), side, inner)
+
+
+def column_x(o):
+    inner = jnp.where(o < BOTH, jnp.where(o < SIDE + 2, 1, 2), jnp.where(o < BOTH + CY - 2, 1, 2))
+    return jnp.where(o < CY, 0, jnp.where(o < SIDE, CX - 1, inner))
+
+
+def column_y(o):
+    side = jnp.where(o < CY, o, o - CY)
+    end = jnp.where((o == SIDE) | (o == SIDE + 2), 0, CY - 1)
+    core = jnp.where(o < BOTH + CY - 2, o - BOTH, o - (BOTH + CY - 2)) + 1
+    return jnp.where(o < SIDE, side, jnp.where(o < BOTH, end, core))
 
 
 def add_chunk(last, at, base, size, plane0, data, rankb, taps, quad, lift_t, mess, keys, grid):
@@ -138,8 +159,8 @@
     oy = t[67:68] + t[68:69] + t[69:70]
     oz = t[70:71] + t[71:72] + t[72:73]
     coli = cols.astype(jnp.int32)
-    gx = home_plane(lax.shift_right_logical(coli, 3)) + at[0] * CX
-    gy = jnp.bitwise_and(coli, 7) + at[1] * CY
+    gx = column_x(coli) + at[0] * CX
+    gy = column_y(coli) + at[1] * CY
     k_x, k_y, k_z, k_b = (taps[j, :, 0:size] for j in range(4))
 
     def ends(g, end):
@@ -194,8 +215,8 @@
                  for dz in range(3)], axis=0)
             results.append((c, [mm(mess[s, q * 3 * CH:(q + 1) * 3 * CH], hot) for q in range(3)]))
         for c, acc in results:
-            cx = home_plane(lax.shift_right_logical(c, 3)) - plane0
-            cy = jnp.bitwise_and(c, 7)
+            cx = column_x(c) - plane0
+            cy = column_y(c)
             for dx in range(3):
                 for dy in range(3):
                     grid[cx + dx, cy + dy] += acc[dx][dy * CH:(dy + 1) * CH]
@@ -205,7 +226,7 @@
 
 
 def sides_kernel(last, at, feat_h, pos_h, home_h, nbr_h, deg_h, lift_h, first_h, bias_h, second_h,
-                 grid, low, high, data, rankb, taps, quad, lift_t, count,
+                 grid, low, high, data, rankb, taps, quad, lift_t, span_a, span_b,
                  pos, home, nbr, deg, lift, first, bias, second, mess, keys, sems):
     pairs = [(home_h, home), (pos_h, pos), (nbr_h, nbr), (deg_h, deg),
              (feat_h, data.at[0:64]), (lift_h, lift), (first_h, first), (bias_h, bias),
@@ -222,11 +243,18 @@
     hx = home[0:1, :]
     hy = home[1:2, :]
     hz = home[2:3, :]
-    order = jnp.where(hx == 0, 0, jnp.where(hx == CX - 1, 1, hx + 1))
-    col = order * CY + hy
-    outer = jnp.sum(jnp.where(order < 2, 1.0, 0.0)).astype(jnp.int32)
-    split = jnp.maximum((outer + CHUNK - 1) // CHUNK, FIRST)
-    count[0] = split
+    col = column_rank(hx, hy)
+
+    def blocks(limit, least):
+        n = jnp.sum(jnp.where(col < limit, 1.0, 0.0)).astype(jnp.int32)
+        return jnp.maximum((n + CHUNK - 1) // CHUNK, least)
+
+    split = blocks(SIDE, FIRST)
+    later = jnp.maximum(blocks(BOTH, SECOND), split)
+    span_a[0] = split
+    span_a[1] = later
+    span_b[0] = later
+    span_b[1] = PTS // CHUNK
 
     ids = lax.broadcasted_iota(jnp.int32, (CX * CY, PTS), 0)
     carry = jnp.sum(jnp.where(col < ids, 1.0, 0.0), axis=1, keepdims=True)
@@ -276,7 +304,7 @@
     high[...] = grid[CX + 1]
 
 
-def middle_kernel(last, at, count, data, rankb, taps, quad, lift_t, grid, mess, keys):
+def middle_kernel(last, at, span, data, rankb, taps, quad, lift_t, grid, mess, keys):
     grid[...] = jnp.zeros_like(grid)
 
     def chunk(size, first, step, _):
@@ -284,9 +312,9 @@
                   keys, grid)
         return 0
 
-    split = count[0]
-    odd = jnp.bitwise_and(split, 1)
-    large = (PTS // CHUNK - split) // 2
+    split = span[0]
+    odd = jnp.bitwise_and(span[1] - split, 1)
+    large = (span[1] - split) // 2
     lax.fori_loop(0, odd, functools.partial(chunk, CHUNK, split * CHUNK), 0)
     lax.fori_loop(0, large, functools.partial(chunk, LARGE, (split + odd) * CHUNK), 0)
 
@@ -301,7 +329,7 @@
     inputs = tuple(
         pltpu.with_memory_space_constraint(x, pltpu.HBM)
         for x in (feat, pos, home, nbr, deg, lift, first, bias, second))
-    grid, low, high, *prepared, count = pl.pallas_call(
+    grid, low, high, *prepared, span_a, span_b = pl.pallas_call(
         functools.partial(sides_kernel, last),
         out_shape=[
             shape(CX + 2, CY + 2, CH, NZ),
@@ -312,42 +340,47 @@
             shape(4, CH, LARGE),
             jax.ShapeDtypeStruct((4 * CH, 4 * CH), BF16),
             jax.ShapeDtypeStruct((CH, CH), BF16),
-            jax.ShapeDtypeStruct((1,), jnp.int32),
+            jax.ShapeDtypeStruct((2,), jnp.int32),
+            jax.ShapeDtypeStruct((2,), jnp.int32),
         ],
         in_specs=[smem] + [pl.BlockSpec(memory_space=pltpu.HBM)] * len(inputs),
-        out_specs=[vmem] * 8 + [smem],
+        out_specs=[vmem] * 8 + [smem, smem],
         scratch_shapes=[pltpu.VMEM(x.shape, x.dtype) for x in inputs[1:]] + work
         + [pltpu.SemaphoreType.DMA((len(inputs),))],
         compiler_params=LIMIT,
         name="lift_sides",
     )(at, *inputs)
-    middle = pl.pallas_call(
+    return grid, low, high, prepared, span_a, span_b
+
+
+def lift_inner(at, last, span, prepared, name):
+    vmem = pl.BlockSpec(memory_space=pltpu.VMEM)
+    smem = pl.BlockSpec(memory_space=pltpu.SMEM)
+    return pl.pallas_call(
         functools.partial(middle_kernel, last),
         out_shape=shape(CX, CY + 2, CH, NZ),
         in_specs=[smem, smem] + [vmem] * 5,
-        scratch_shapes=work,
+        out_specs=vmem,
+        scratch_shapes=[
+            pltpu.VMEM((LARGE // SUB, 9 * CH, 3 * SUB), BF16),
+            pltpu.VMEM((3, LARGE, NZ), F32),
+        ],
         compiler_params=LIMIT,
-        name="lift_middle",
-    )(at, count, *prepared)
-    return grid, low, high, middle
-
-
-def latent_kernel(last, at, sides, middle, below, above, own, low_y, high_y):
+        name=name,
+    )(at, span, *prepared)
+
+
+def ends_kernel(last, at, sides, middle, below, above, low_y, high_y):
     low = at[0] == 0
     top = at[0] == last
-    for x in range(CX):
-        for y in range(CY + 2):
+    for y, out in ((0, low_y), (CY + 1, high_y)):
+        for x in range(CX):
             l = sides[x + 1, y] + middle[x, y]
             if x == 0:
                 l = l + jnp.where(low, sides[0, y], below[y])
             if x == CX - 1:
                 l = l + jnp.where(top, sides[CX + 1, y], above[y])
-            if y == 0:
-                low_y[x] = l
-            elif y == CY + 1:
-                high_y[x] = l
-            else:
-                own[x * CY + y - 1] = l
+            out[x] = l
 
 
 def z_modes(table, pair):
@@ -357,31 +390,31 @@
     return jnp.where(lane < CH, re, swap(im)), jnp.where(lane < CH, swap(re), im)
 
 
-def inner_kernel(tabz, own, spec):
+def latent_kernel(last, at, tabz, sides, middle, rest, below, above, low_y, high_y, left, right,
+                  spec, own):
+    low = at[0] == 0
+    top = at[0] == last[0]
+    first_pen = at[1] == 0
+    last_pen = at[1] == last[1]
     table = tabz[...]
     for x in range(CX):
-        for y in range(1, CY - 1, 2):
-            i = x * CY + y
+        for yp in range(CY // 2):
+            i = x * CY + 2 * yp
+            for j in range(2):
+                y = 2 * yp + j + 1
+                l = sides[x + 1, y] + middle[x, y] + rest[x, y]
+                if x == 0:
+                    l = l + jnp.where(low, sides[0, y], below[y])
+                if x == CX - 1:
+                    l = l + jnp.where(top, sides[CX + 1, y], above[y])
+                if y == 1:
+                    l = l + jnp.where(first_pen, low_y[x], left[x])
+                if y == CY:
+                    l = l + jnp.where(last_pen, high_y[x], right[x])
+                own[i + j] = l
             u, v = z_modes(table, own[i:i + 2].reshape(2 * CH, NZ))
             spec[:, i, :] = u
             spec[:, i + 1, :] = v
-        spec[:, x * CY, :] = jnp.zeros((MODES, HALVES), F32)
-        spec[:, x * CY + CY - 1, :] = jnp.zeros((MODES, HALVES), F32)
-
-
-def outer_kernel(last, at, tabz, own, part, low_y, high_y, left, right, spec, ends):
-    first_pen = at[1] == 0
-    last_pen = at[1] == last
-    table = tabz[...]
-    spec[...] = part[...]
-    for x in range(CX):
-        a = own[x * CY] + jnp.where(first_pen, low_y[x], left[x])
-        b = own[x * CY + CY - 1] + jnp.where(last_pen, high_y[x], right[x])
-        u, v = z_modes(table, jnp.concatenate([a, b], axis=0))
-        spec[:, x * CY, :] = u
-        spec[:, x * CY + CY - 1, :] = v
-        ends[0, x] = a
-        ends[1, x] = b
 
 
 def y_kernel(r, main, out):
@@ -425,7 +458,7 @@
         out[:, i * CY:(i + 1) * CY, :] = y.reshape(rows // CY, CY, HALVES)
 
 
-def final_kernel(zb, tab, own, ends, skip, bias, out):
+def final_kernel(zb, tab, own, skip, bias, out):
     lane = lax.broadcasted_iota(jnp.int32, (MODES, HALVES), 1)
     zero = jnp.zeros((CH, CH), F32)
     skip_t = jnp.transpose(skip[...])
@@ -442,11 +475,8 @@
             s = jnp.concatenate(
                 [jnp.where(lane < CH, u, swap(v)), jnp.where(lane < CH, swap(u), v)], axis=0)
             spectral = mm(s, tab[...], TN, HIGH)
-            lat = []
-            for j in range(2):
-                y = 2 * yp + j
-                lat.append(ends[0, x] if y == 0 else ends[1, x] if y == CY - 1 else own[i + j])
-            total = spectral + mm(pair, jnp.concatenate(lat, axis=0), NN, HIGH) + col
+            lat = own[i:i + 2].reshape(2 * CH, NZ)
+            total = spectral + mm(pair, lat, NN, HIGH) + col
             out[x, 2 * yp:2 * yp + 2] = gelu(total).astype(BF16).reshape(2, CH, NZ)
 
 
@@ -482,22 +512,25 @@
     bins = lax.axis_size("bin")
     pens = lax.axis_size("pen")
     at = jnp.stack([lax.axis_index("bin"), lax.axis_index("pen")]).astype(jnp.int32)
-    sides, low, high, middle = lift_points(
-        at, (bins * CX - 1, pens * CY - 1), features.T, positions, home_cells, neighbours.T,
+    last = (bins * CX - 1, pens * CY - 1)
+    sides, low, high, prepared, span_a, span_b = lift_points(
+        at, last, features.T, positions, home_cells, neighbours.T,
         degrees[None, :], lift_input, kernel_first, kernel_bias[None, :], kernel_second)
     below = moved(high, "bin", 1)
     above = moved(low, "bin", -1)
+    middle = lift_inner(at, last, span_a, prepared, "lift_ends")
     half = shape(CX, CH, NZ)
-    own, low_y, high_y = call(
-        functools.partial(latent_kernel, bins - 1), [shape(CX * CY, CH, NZ), half, half],
-        (at, sides, middle, below, above), smem=True, name="latent")
+    low_y, high_y = call(
+        functools.partial(ends_kernel, bins - 1), [half, half],
+        (at, sides, middle, below, above), smem=True, name="y_ends")
     left = moved(high_y, "pen", 1)
     right = moved(low_y, "pen", -1)
-    table = jnp.asarray(z_forward_table())
-    spec = call(inner_kernel, shape(MODES, CX * CY, HALVES), (table, own), name="forward_z")
-    spec, ends = call(
-        functools.partial(outer_kernel, pens - 1), [shape(*spec.shape), shape(2, CX, CH, NZ)],
-        (at, table, own, spec, low_y, high_y, left, right), smem=True, name="forward_z_ends")
+    rest = lift_inner(at, last, span_b, prepared, "lift_core")
+    spec, own = call(
+        functools.partial(latent_kernel, (bins - 1, pens - 1)),
+        [shape(MODES, CX * CY, HALVES), shape(CX * CY, CH, NZ)],
+        (at, jnp.asarray(z_forward_table()), sides, middle, rest, below, above, low_y, high_y,
+         left, right), smem=True, name="latent_z")
     r = exchange(spec.reshape(pens, 2 * CX * CY, HALVES), "pen")
     r = call(y_kernel, shape(MODES, 2 * CX, HALVES), (r, jnp.asarray(y_forward_table(pens))),
              name="forward_y")
@@ -512,7 +545,7 @@
     r = exchange(r, "pen")
     out = call(
         final_kernel, jax.ShapeDtypeStruct((CX, CY, CH, NZ), BF16),
-        (r.reshape(MODES, CX * CY, HALVES), jnp.asarray(z_inverse_table()), own, ends,
+        (r.reshape(MODES, CX * CY, HALVES), jnp.asarray(z_inverse_table()), own,
          skip_weights, skip_bias[None, :]), name="finish")
     return out.transpose(0, 1, 3, 2)
 

time: 160 us -> 161 us (level)
  blocking collectives: 104 us -> 112 us
  waiting for transfers between devices: 7.11 us -> 0.2 us
    all_to_all x4, blocking collectives: 104 us -> 112 us  [exchange(): return lax.all_to_all(x, axis, split_axis=0, concat_axis=0, tiled=True)]
    ppermute x4, waiting for transfers between devices: 7.11 us -> 0.2 us  [moved(): lax.ppermute(x, axis, [(i - step, i) for i in devices if i - step in devi...]
    pallas_call x1 -> x2, Pallas kernels: 10 us -> 10.4 us  [lift_inner(): pl.pallas_call(functools.partial(middle_kernel, last), out_shape=shape(CX...]
    pallas_call x7 -> x6, Pallas kernels: 9 us -> 8.62 us  [call(): pl.pallas_call(kernel, out_shape=shapes, in_specs=specs, scratch_shapes=l...]
  transfers between devices with their start and end apart: 4 -> 4, of which waited for: 2 -> 1; matrix products, arithmetic and copies ran while one was open for 0% -> 0% of each run, Pallas kernels for 7% -> 6%
where the time goes in v5:
time: 161 us; the launch traced here: 160 us
  blocking collectives  112 us (70%)
  Pallas kernels  35.4 us (22%)
  starting transfers between devices  12.7 us (8%)
    all_to_all x4, blocking collectives, exchange(): return lax.all_to_all(x, axis, split_axis=0, concat_axis=0, tiled=True)  112 us
    pallas_call x1, Pallas kernels, lift_points(): pl.pallas_call(functools.partial(sides_kernel, last), out_shape=[shape(CX...  16.3 us
    ppermute x4, starting transfers between devices, moved(): lax.ppermute(x, axis, [(i - step, i) for i in devices if i - step in devi...  12.7 us
    pallas_call x2, Pallas kernels, lift_inner(): pl.pallas_call(functools.partial(middle_kernel, last), out_shape=shape(CX...  10.4 us
    pallas_call x6, Pallas kernels, call(): pl.pallas_call(kernel, out_shape=shapes, in_specs=specs, scratch_shapes=l...  8.62 us
  transfers between devices with their start and end apart: 4, of which 1 were waited for; matrix products, arithmetic and copies ran while one was open for 0% of the time, Pallas kernels for 6%

profile of v5, /device:TPU:32, one launch (start us, length us, event | category | flops | bytes accessed | tf_op | source)
XLA Modules:
  0.0 160.1 jit_solution(13397589627432964798)
XLA Ops:
  0.0 0.1 pad_add_fusion.at
  0.1 16.3 %lift_sides.1 = (f32[6,10,64,192]{3,2,1,0:T(8,128)S(1)}, f32[10,64,192]{2,1,0:T(8,128)S(1)}, f32[10,64,192]{2,1,0:T(8,128)S(1)}, bf16[112,2048]{1,0:T(8,128)(2,1...) custom-call(s32[2]{0:T(128)S(1)} %pad_add_fusion.at, ...), custom_call_target="tpu_custom_call" | custom-call | tf_op jit(solution)/shard_map/lift_sides/pallas_call | solution.py:332
  16.4 2.6 %collective-permute-start = (f32[10,64,192]{2,1,0:T(8,128)S(1)}, f32[10,64,192]{2,1,0:T(8,128)S(1)}, u32[]{:S(2)}, u32[]{:S(2)}) collective-permute-start(f32[10,64,192]{2,1,0:T(8,128)S(1)} %get-tuple-element.27), channel_id=1, source_target_pairs={{0,16},{16,32},{32,48},{48,64},{64,80},{80,96},{96,112},{112,128},... | collective-permute-start | bytes 1474568 | tf_op jit(solution)/shard_map/ppermute | solution.py:507
  19.0 1.3 collective-permute-start.1
  20.3 3.7 %lift_ends.1.middle = f32[4,10,64,192]{3,2,1,0:T(8,128)S(1)} custom-call(s32[2]{0:T(128)S(1)} %pad_add_fusion.at, s32[2]{0:T(128)S(1)} %get-tuple-element.20.span, bf16[112,2048]{1,0:T(8,128)(2,1)S(1)} %get-tuple-element.21.data, s32[2048,128]{1,0:T(8,128)S(1)} %get-tuple-element.22.rankb, f32[4,64,512]{2,1,0:T(8,128)S(1)} %get-tuple-element.23.taps, ...), custom_call_target="tpu_custom_call" | custom-call | tf_op jit(solution)/shard_map/lift_ends/pallas_call | solution.py:359
  24.1 0.0 collective-permute-done.below
  24.1 0.2 collective-permute-done.1.above
  24.3 0.6 y_ends.1
  24.9 0.0 copy-start.5
  24.9 6.9 %collective-permute-start.3 = (f32[4,64,192]{2,1,0:T(8,128)S(1)}, f32[4,64,192]{2,1,0:T(8,128)S(1)}, u32[]{:S(2)}, u32[]{:S(2)}) collective-permute-start(f32[4,64,192]{2,1,0:T(8,128)S(1)} %get-tuple-element.29.low_y), channel_id=1, source_target_pairs={{1,0},{2,1},{3,2},{4,3},{5,4},{6,5},{7,6},{8,7},{9,8},{10,9},{11,1... | collective-permute-start | bytes 589832 | tf_op jit(solution)/shard_map/ppermute | solution.py:507
  31.8 1.9 %collective-permute-start.2 = (f32[4,64,192]{2,1,0:T(8,128)S(1)}, f32[4,64,192]{2,1,0:T(8,128)S(1)}, u32[]{:S(2)}, u32[]{:S(2)}) collective-permute-start(f32[4,64,192]{2,1,0:T(8,128)S(1)} %get-tuple-element.30.high_y), channel_id=1, source_target_pairs={{0,1},{1,2},{2,3},{3,4},{4,5},{5,6},{6,7},{7,8},{8,9},{9,10},{10,1... | collective-permute-start | bytes 589832 | tf_op jit(solution)/shard_map/ppermute | solution.py:507
  33.7 6.7 %lift_core.1.rest = f32[4,10,64,192]{3,2,1,0:T(8,128)S(1)} custom-call(s32[2]{0:T(128)S(1)} %pad_add_fusion.at, s32[2]{0:T(128)S(1)} %get-tuple-element.26.span, bf16[112,2048]{1,0:T(8,128)(2,1)S(1)} %get-tuple-element.21.data, s32[2048,128]{1,0:T(8,128)S(1)} %get-tuple-element.22.rankb, f32[4,64,512]{2,1,0:T(8,128)S(1)} %get-tuple-element.23.taps, ...), custom_call_target="tpu_custom_call" | custom-call | tf_op jit(solution)/shard_map/lift_core/pallas_call | solution.py:359
  40.4 0.0 copy-start.7
  40.4 0.0 copy-start.1
  40.5 0.0 copy-start.3
  40.5 0.0 collective-permute-done.3.right
  40.5 0.0 collective-permute-done.2.left
  40.5 0.0 copy-done.5
  40.5 2.2 %latent_z.1 = (f32[32,32,128]{2,1,0:T(8,128)S(1)}, f32[32,64,192]{2,1,0:T(8,128)S(1)}) custom-call(s32[2]{0:T(128)S(1)} %pad_add_fusion.at, f32[64,192]{1,0:T(8,128)S(1)} %copy-done.5, f32[6,10,64,192]{3,2,1,0:T(8,128)S(1)} %get-tuple-element.19.sides, f32[4,10,64,192]{3,2,1,0:T(8,128)S(1)} %lift_ends.1.middle, f32[4,10,64,192]{3,2,1,0:T(8,128)S(1)} %lift_core.1.rest, ...), custom_call_target="tpu_custom_call" | custom-call | tf_op jit(solution)/shard_map/latent_z/pallas_call | solution.py:487
  42.7 0.0 copy-start
  42.7 0.0 copy-start.2
  42.7 36.5 %all_to_all.20.r = f32[16,64,128]{2,1,0:T(8,128)S(1)} all-to-all(f32[16,64,128]{2,1,0:T(8,128)S(1)} %bitcast.11), channel_id=1, replica_groups=mesh['bin'=32,'pen'=16] {'pen'}, dimensions={0} | all-to-all | bytes 1048576 | tf_op jit(solution)/shard_map/all_to_all | solution.py:502
  79.3 0.0 copy-done.7
  79.3 0.4 forward_y.1
  79.7 28.3 %all_to_all.21.r = f32[32,8,128]{2,1,0:T(8,128)S(1)} all-to-all(f32[32,8,128]{2,1,0:T(8,128)S(1)} %forward_y.1), channel_id=1, replica_groups=mesh['bin'=32,'pen'=16] {'bin'}, dimensions={0} | all-to-all | bytes 262144 | tf_op jit(solution)/shard_map/all_to_all | solution.py:502
  108.0 0.0 copy-done.1
  108.0 0.0 copy-done.3
  108.0 1.2 mix_x.1
  109.3 11.3 %all_to_all.22.r = f32[32,8,128]{2,1,0:T(8,128)S(1)} all-to-all(f32[32,8,128]{2,1,0:T(8,128)S(1)} %mix_x.1), channel_id=1, replica_groups=mesh['bin'=32,'pen'=16] {'bin'}, dimensions={0} | all-to-all | bytes 262144 | tf_op jit(solution)/shard_map/all_to_all | solution.py:502
  120.6 0.6 inverse_y.1
  121.2 35.4 %all_to_all.23 = f32[16,64,128]{2,1,0:T(8,128)S(1)} all-to-all(f32[16,64,128]{2,1,0:T(8,128)S(1)} %inverse_y.1), channel_id=1, replica_groups=mesh['bin'=32,'pen'=16] {'pen'}, dimensions={0} | all-to-all | bytes 1048576 | tf_op jit(solution)/shard_map/all_to_all | solution.py:502
  156.6 3.5 %finish.1 = bf16[4,8,64,192]{3,2,1,0:T(8,128)(2,1)} custom-call(f32[32,32,128]{2,1,0:T(8,128)S(1)} %bitcast.10, f32[64,192]{1,0:T(8,128)S(1)} %copy-done.4, f32[32,64,192]{2,1,0:T(8,128)S(1)} %get-tuple-element.32.own, f32[64,64]{1,0:T(8,128)S(1)} %copy-done.6, f32[1,64]{1,0:T(1,128)S(1)} %bitcast.12), custom_call_target="tpu_custom_call" | custom-call | tf_op jit(solution)/shard_map/finish/pallas_call | solution.py:487
  (8 shorter events, 0.0 us)
Async XLA Ops:
  16.4 7.6 %collective-permute-start = (f32[10,64,192]{2,1,0:T(8,128)S(1)}, f32[10,64,192]{2,1,0:T(8,128)S(1)}, u32[]{:S(2)}, u32[]{:S(2)}) collective-permute-start(f32[10,64,192]{2,1,0:T(8,128)S(1)} %get-tuple-element.27), channel_id=1, source_target_pairs={{0,16},{16,32},{32,48},{48,64},{64,80},{80,96},{96,112},{112,128},... | collective-permute-start | bytes 1474568 | tf_op jit(solution)/shard_map/ppermute | solution.py:507
  19.0 5.2 %collective-permute-start.1 = (f32[10,64,192]{2,1,0:T(8,128)S(1)}, f32[10,64,192]{2,1,0:T(8,128)S(1)}, u32[]{:S(2)}, u32[]{:S(2)}) collective-permute-start(f32[10,64,192]{2,1,0:T(8,128)S(1)} %get-tuple-element.28), channel_id=1, source_target_pairs={{16,0},{32,16},{48,32},{64,48},{80,64},{96,80},{112,96},{128,112},... | collective-permute-start | bytes 1474568 | tf_op jit(solution)/shard_map/ppermute | solution.py:507
  24.9 15.6 %copy-start.5 = (f32[64,192]{1,0:T(8,128)S(1)}, f32[64,192]{1,0:T(8,128)}, u32[]{:S(2)}) copy-start(f32[64,192]{1,0:T(8,128)} %constant.21.clone.tabz) | copy-start | bytes 147460
  24.9 15.6 %collective-permute-start.3 = (f32[4,64,192]{2,1,0:T(8,128)S(1)}, f32[4,64,192]{2,1,0:T(8,128)S(1)}, u32[]{:S(2)}, u32[]{:S(2)}) collective-permute-start(f32[4,64,192]{2,1,0:T(8,128)S(1)} %get-tuple-element.29.low_y), channel_id=1, source_target_pairs={{1,0},{2,1},{3,2},{4,3},{5,4},{6,5},{7,6},{8,7},{9,8},{10,9},{11,1... | collective-permute-start | bytes 589832 | tf_op jit(solution)/shard_map/ppermute | solution.py:507
  31.8 8.7 %collective-permute-start.2 = (f32[4,64,192]{2,1,0:T(8,128)S(1)}, f32[4,64,192]{2,1,0:T(8,128)S(1)}, u32[]{:S(2)}, u32[]{:S(2)}) collective-permute-start(f32[4,64,192]{2,1,0:T(8,128)S(1)} %get-tuple-element.30.high_y), channel_id=1, source_target_pairs={{0,1},{1,2},{2,3},{3,4},{4,5},{5,6},{6,7},{7,8},{8,9},{9,10},{10,1... | collective-permute-start | bytes 589832 | tf_op jit(solution)/shard_map/ppermute | solution.py:507
  40.4 38.8 %copy-start.7 = (f32[64,128]{1,0:T(8,128)S(1)}, f32[64,128]{1,0:T(8,128)}, u32[]{:S(2)}) copy-start(f32[64,128]{1,0:T(8,128)} %constant.22.clone.main) | copy-start | bytes 98308
  40.4 67.6 %copy-start.1 = (f32[512,64]{1,0:T(8,128)S(1)}, f32[512,64]{1,0:T(8,128)}, u32[]{:S(2)}) copy-start(f32[512,64]{1,0:T(8,128)} %constant.24.clone.inv) | copy-start | bytes 393220
  40.5 67.6 %copy-start.3 = (f32[128,256]{1,0:T(8,128)S(1)}, f32[128,256]{1,0:T(8,128)}, u32[]{:S(2)}) copy-start(f32[128,256]{1,0:T(8,128)} %constant.23.clone.fwd) | copy-start | bytes 393220
  42.7 65.3 %copy-start = (bf16[32,1,2,64,128]{4,3,2,1,0:T(8,128)(2,1)S(1)}, bf16[32,1,2,64,128]{4,3,2,1,0:T(8,128)(2,1)}, u32[]{:S(2)}) copy-start(bf16[32,1,2,64,128]{4,3,2,1,0:T(8,128)(2,1)} %w.1) | copy-start | bytes 3145732
  42.7 77.8 %copy-start.2 = (f32[256,32]{1,0:T(8,128)S(1)}, f32[256,32]{1,0:T(8,128)}, u32[]{:S(2)}) copy-start(f32[256,32]{1,0:T(8,128)} %constant.25.clone.inv) | copy-start | bytes 98308
  79.3 77.4 %copy-start.4 = (f32[64,192]{1,0:T(8,128)S(1)}, f32[64,192]{1,0:T(8,128)}, u32[]{:S(2)}) copy-start(f32[64,192]{1,0:T(8,128)} %constant.26.clone.tab) | copy-start | bytes 147460
  79.3 77.4 %copy-start.6 = (f32[64,64]{1,0:T(8,128)S(1)}, f32[64,64]{1,0:T(8,128)}, u32[]{:S(2)}) copy-start(f32[64,64]{1,0:T(8,128)} %skip.1) | copy-start | bytes 49156
  79.3 77.4 %copy-start.8 = (f32[64]{0:T(128)S(1)}, f32[64]{0:T(128)}, u32[]{:S(2)}) copy-start(f32[64]{0:T(128)} %param.29) | copy-start | bytes 772

commit v6 on v5

--- a/solution.py
+++ b/solution.py
@@ -19,7 +19,7 @@
 SUB = 128
 LARGE = 512
 FIRST = 5
-SECOND = 6
+SECOND = 7
 HALVES = 2 * CH
 
 F32 = jnp.float32
@@ -104,6 +104,19 @@
     return fwd.astype(np.float32), inv.astype(np.float32)
 
 
+def pack(cells):
+    tail = cells[:, 128:NZ]
+    half = CH // 2
+    return jnp.concatenate(
+        [cells[:, 0:128], jnp.concatenate([tail[0:half], tail[half:CH]], axis=1)], axis=0)
+
+
+def unpack(rows):
+    tail = rows[CH:]
+    tail = jnp.concatenate([tail[:, 0:NZ - 128], tail[:, NZ - 128:]], axis=0)
+    return jnp.concatenate([rows[0:CH], tail], axis=1)
+
+
 def pieces(x):
     hi = x.astype(BF16).astype(F32)
     rest = x - hi
@@ -111,6 +124,7 @@
     return hi, mid, rest - mid
 
 
+PACKED = CH * NZ // 128
 SIDE = 2 * CY
 BOTH = SIDE + 4
 
@@ -300,8 +314,9 @@
     large = split // 2
     lax.fori_loop(0, large, functools.partial(chunk, LARGE, 0), 0)
     lax.fori_loop(0, split - 2 * large, functools.partial(chunk, CHUNK, large * LARGE), 0)
-    low[...] = grid[0]
-    high[...] = grid[CX + 1]
+    for y in range(CY + 2):
+        low[y] = pack(grid[0, y])
+        high[y] = pack(grid[CX + 1, y])
 
 
 def middle_kernel(last, at, span, data, rankb, taps, quad, lift_t, grid, mess, keys):
@@ -333,8 +348,8 @@
         functools.partial(sides_kernel, last),
         out_shape=[
             shape(CX + 2, CY + 2, CH, NZ),
-            shape(CY + 2, CH, NZ),
-            shape(CY + 2, CH, NZ),
+            shape(CY + 2, PACKED, 128),
+            shape(CY + 2, PACKED, 128),
             jax.ShapeDtypeStruct((112, PTS), BF16),
             jax.ShapeDtypeStruct((PTS, 128), jnp.int32),
             shape(4, CH, LARGE),
@@ -377,10 +392,10 @@
         for x in range(CX):
             l = sides[x + 1, y] + middle[x, y]
             if x == 0:
-                l = l + jnp.where(low, sides[0, y], below[y])
+                l = l + jnp.where(low, sides[0, y], unpack(below[y]))
             if x == CX - 1:
-                l = l + jnp.where(top, sides[CX + 1, y], above[y])
-            out[x] = l
+                l = l + jnp.where(top, sides[CX + 1, y], unpack(above[y]))
+            out[x] = pack(l)
 
 
 def z_modes(table, pair):
@@ -404,13 +419,13 @@
                 y = 2 * yp + j + 1
                 l = sides[x + 1, y] + middle[x, y] + rest[x, y]
                 if x == 0:
-                    l = l + jnp.where(low, sides[0, y], below[y])
+                    l = l + jnp.where(low, sides[0, y], unpack(below[y]))
                 if x == CX - 1:
-                    l = l + jnp.where(top, sides[CX + 1, y], above[y])
+                    l = l + jnp.where(top, sides[CX + 1, y], unpack(above[y]))
                 if y == 1:
-                    l = l + jnp.where(first_pen, low_y[x], left[x])
+                    l = l + unpack(jnp.where(first_pen, low_y[x], left[x]))
                 if y == CY:
-                    l = l + jnp.where(last_pen, high_y[x], right[x])
+                    l = l + unpack(jnp.where(last_pen, high_y[x], right[x]))
                 own[i + j] = l
             u, v = z_modes(table, own[i:i + 2].reshape(2 * CH, NZ))
             spec[:, i, :] = u
@@ -519,7 +534,7 @@
     below = moved(high, "bin", 1)
     above = moved(low, "bin", -1)
     middle = lift_inner(at, last, span_a, prepared, "lift_ends")
-    half = shape(CX, CH, NZ)
+    half = shape(CX, PACKED, 128)
     low_y, high_y = call(
         functools.partial(ends_kernel, bins - 1), [half, half],
         (at, sides, middle, below, above), smem=True, name="y_ends")

time: 161 us -> 157 us (0.975)
  blocking collectives: 112 us -> 106 us
  waiting for transfers between devices: 0.2 us -> 3.15 us
    all_to_all x4, blocking collectives: 112 us -> 106 us  [exchange(): return lax.all_to_all(x, axis, split_axis=0, concat_axis=0, tiled=True)]
    ppermute x4, waiting for transfers between devices: 0.2 us -> 3.15 us  [moved(): lax.ppermute(x, axis, [(i - step, i) for i in devices if i - step in devi...]
where the time goes in v6:
time: 157 us; the launch traced here: 156 us
  blocking collectives  106 us (68%)
  Pallas kernels  35.4 us (23%)
  starting transfers between devices  11.2 us (7%)
  waiting for transfers between devices  3.15 us (2%)
    all_to_all x4, blocking collectives, exchange(): return lax.all_to_all(x, axis, split_axis=0, concat_axis=0, tiled=True)  106 us
    pallas_call x1, Pallas kernels, lift_points(): pl.pallas_call(functools.partial(sides_kernel, last), out_shape=[shape(CX...  17.2 us
    ppermute x4, starting transfers between devices, moved(): lax.ppermute(x, axis, [(i - step, i) for i in devices if i - step in devi...  11.2 us
    pallas_call x2, Pallas kernels, lift_inner(): pl.pallas_call(functools.partial(middle_kernel, last), out_shape=shape(CX...  9.54 us
    pallas_call x6, Pallas kernels, call(): pl.pallas_call(kernel, out_shape=shapes, in_specs=specs, scratch_shapes=l...  8.71 us
    ppermute x4, waiting for transfers between devices, moved(): lax.ppermute(x, axis, [(i - step, i) for i in devices if i - step in devi...  3.15 us
  transfers between devices with their start and end apart: 4, of which 1 were waited for; matrix products, arithmetic and copies ran while one was open for 0% of the time, Pallas kernels for 6%

profile of v6, /device:TPU:32, one launch (start us, length us, event | category | flops | bytes accessed | tf_op | source)
XLA Modules:
  0.0 156.5 jit_solution(5483169188600787808)
XLA Ops:
  0.0 0.1 pad_add_fusion.at
  0.1 17.2 %lift_sides.1 = (f32[6,10,64,192]{3,2,1,0:T(8,128)S(1)}, f32[10,96,128]{2,1,0:T(8,128)S(1)}, f32[10,96,128]{2,1,0:T(8,128)S(1)}, bf16[112,2048]{1,0:T(8,128)(2,1...) custom-call(s32[2]{0:T(128)S(1)} %pad_add_fusion.at, ...), custom_call_target="tpu_custom_call" | custom-call | tf_op jit(solution)/shard_map/lift_sides/pallas_call | solution.py:347
  17.2 1.4 collective-permute-start
  18.7 1.3 collective-permute-start.1
  20.0 5.7 %lift_ends.1.middle = f32[4,10,64,192]{3,2,1,0:T(8,128)S(1)} custom-call(s32[2]{0:T(128)S(1)} %pad_add_fusion.at, s32[2]{0:T(128)S(1)} %get-tuple-element.20.span, bf16[112,2048]{1,0:T(8,128)(2,1)S(1)} %get-tuple-element.21.data, s32[2048,128]{1,0:T(8,128)S(1)} %get-tuple-element.22.rankb, f32[4,64,512]{2,1,0:T(8,128)S(1)} %get-tuple-element.23.taps, ...), custom_call_target="tpu_custom_call" | custom-call | tf_op jit(solution)/shard_map/lift_ends/pallas_call | solution.py:374
  25.6 0.0 collective-permute-done.below
  25.6 0.0 collective-permute-done.1.above
  25.7 0.7 y_ends.1
  26.4 0.0 copy-start.5
  26.4 6.6 %collective-permute-start.3 = (f32[4,96,128]{2,1,0:T(8,128)S(1)}, f32[4,96,128]{2,1,0:T(8,128)S(1)}, u32[]{:S(2)}, u32[]{:S(2)}) collective-permute-start(f32[4,96,128]{2,1,0:T(8,128)S(1)} %get-tuple-element.29.low_y), channel_id=1, source_target_pairs={{1,0},{2,1},{3,2},{4,3},{5,4},{6,5},{7,6},{8,7},{9,8},{10,9},{11,1... | collective-permute-start | bytes 589832 | tf_op jit(solution)/shard_map/ppermute | solution.py:522
  33.0 1.9 %collective-permute-start.2 = (f32[4,96,128]{2,1,0:T(8,128)S(1)}, f32[4,96,128]{2,1,0:T(8,128)S(1)}, u32[]{:S(2)}, u32[]{:S(2)}) collective-permute-start(f32[4,96,128]{2,1,0:T(8,128)S(1)} %get-tuple-element.30.high_y), channel_id=1, source_target_pairs={{0,1},{1,2},{2,3},{3,4},{4,5},{5,6},{6,7},{7,8},{8,9},{9,10},{10,1... | collective-permute-start | bytes 589832 | tf_op jit(solution)/shard_map/ppermute | solution.py:522
  34.9 3.9 %lift_core.1.rest = f32[4,10,64,192]{3,2,1,0:T(8,128)S(1)} custom-call(s32[2]{0:T(128)S(1)} %pad_add_fusion.at, s32[2]{0:T(128)S(1)} %get-tuple-element.26.span, bf16[112,2048]{1,0:T(8,128)(2,1)S(1)} %get-tuple-element.21.data, s32[2048,128]{1,0:T(8,128)S(1)} %get-tuple-element.22.rankb, f32[4,64,512]{2,1,0:T(8,128)S(1)} %get-tuple-element.23.taps, ...), custom_call_target="tpu_custom_call" | custom-call | tf_op jit(solution)/shard_map/lift_core/pallas_call | solution.py:374
  38.8 0.0 copy-start.7
  38.8 0.0 copy-start.1
  38.8 0.0 copy-start.3
  38.8 0.0 collective-permute-done.3.right
  38.8 3.1 %collective-permute-done.2.left = f32[4,96,128]{2,1,0:T(8,128)S(1)} collective-permute-done((f32[4,96,128]{2,1,0:T(8,128)S(1)}, f32[4,96,128]{2,1,0:T(8,128)S(1)}, u32[]{:S(2)}, u32[]{:S(2)}) %collective-permute-start.2) | collective-permute-done | bytes 196640 | tf_op jit(solution)/shard_map/ppermute | solution.py:522
  42.0 0.0 copy-done.5
  42.0 2.2 %latent_z.1 = (f32[32,32,128]{2,1,0:T(8,128)S(1)}, f32[32,64,192]{2,1,0:T(8,128)S(1)}) custom-call(s32[2]{0:T(128)S(1)} %pad_add_fusion.at, f32[64,192]{1,0:T(8,128)S(1)} %copy-done.5, f32[6,10,64,192]{3,2,1,0:T(8,128)S(1)} %get-tuple-element.19.sides, f32[4,10,64,192]{3,2,1,0:T(8,128)S(1)} %lift_ends.1.middle, f32[4,10,64,192]{3,2,1,0:T(8,128)S(1)} %lift_core.1.rest, ...), custom_call_target="tpu_custom_call" | custom-call | tf_op jit(solution)/shard_map/latent_z/pallas_call | solution.py:502
  44.2 0.0 copy-start
  44.2 0.0 copy-start.2
  44.2 38.6 %all_to_all.20.r = f32[16,64,128]{2,1,0:T(8,128)S(1)} all-to-all(f32[16,64,128]{2,1,0:T(8,128)S(1)} %bitcast.11), channel_id=1, replica_groups=mesh['bin'=32,'pen'=16] {'pen'}, dimensions={0} | all-to-all | bytes 1048576 | tf_op jit(solution)/shard_map/all_to_all | solution.py:517
  82.8 0.0 copy-done.7
  82.8 0.4 forward_y.1
  83.2 21.5 %all_to_all.21.r = f32[32,8,128]{2,1,0:T(8,128)S(1)} all-to-all(f32[32,8,128]{2,1,0:T(8,128)S(1)} %forward_y.1), channel_id=1, replica_groups=mesh['bin'=32,'pen'=16] {'bin'}, dimensions={0} | all-to-all | bytes 262144 | tf_op jit(solution)/shard_map/all_to_all | solution.py:517
  104.7 0.0 copy-done.3
  104.7 1.2 mix_x.1
  106.0 11.3 %all_to_all.22.r = f32[32,8,128]{2,1,0:T(8,128)S(1)} all-to-all(f32[32,8,128]{2,1,0:T(8,128)S(1)} %mix_x.1), channel_id=1, replica_groups=mesh['bin'=32,'pen'=16] {'bin'}, dimensions={0} | all-to-all | bytes 262144 | tf_op jit(solution)/shard_map/all_to_all | solution.py:517
  117.3 0.0 copy-done.2
  117.3 0.7 inverse_y.1
  117.9 35.1 %all_to_all.23 = f32[16,64,128]{2,1,0:T(8,128)S(1)} all-to-all(f32[16,64,128]{2,1,0:T(8,128)S(1)} %inverse_y.1), channel_id=1, replica_groups=mesh['bin'=32,'pen'=16] {'pen'}, dimensions={0} | all-to-all | bytes 1048576 | tf_op jit(solution)/shard_map/all_to_all | solution.py:517
  153.0 3.5 %finish.1 = bf16[4,8,64,192]{3,2,1,0:T(8,128)(2,1)} custom-call(f32[32,32,128]{2,1,0:T(8,128)S(1)} %bitcast.10, f32[64,192]{1,0:T(8,128)S(1)} %copy-done.4, f32[32,64,192]{2,1,0:T(8,128)S(1)} %get-tuple-element.32.own, f32[64,64]{1,0:T(8,128)S(1)} %copy-done.6, f32[1,64]{1,0:T(1,128)S(1)} %bitcast.12), custom_call_target="tpu_custom_call" | custom-call | tf_op jit(solution)/shard_map/finish/pallas_call | solution.py:502
  (8 shorter events, 0.0 us)
Async XLA Ops:
  17.2 8.4 %collective-permute-start = (f32[10,96,128]{2,1,0:T(8,128)S(1)}, f32[10,96,128]{2,1,0:T(8,128)S(1)}, u32[]{:S(2)}, u32[]{:S(2)}) collective-permute-start(f32[10,96,128]{2,1,0:T(8,128)S(1)} %get-tuple-element.27), channel_id=1, source_target_pairs={{0,16},{16,32},{32,48},{48,64},{64,80},{80,96},{96,112},{112,128},... | collective-permute-start | bytes 1474568 | tf_op jit(solution)/shard_map/ppermute | solution.py:522
  18.7 7.0 %collective-permute-start.1 = (f32[10,96,128]{2,1,0:T(8,128)S(1)}, f32[10,96,128]{2,1,0:T(8,128)S(1)}, u32[]{:S(2)}, u32[]{:S(2)}) collective-permute-start(f32[10,96,128]{2,1,0:T(8,128)S(1)} %get-tuple-element.28), channel_id=1, source_target_pairs={{16,0},{32,16},{48,32},{64,48},{80,64},{96,80},{112,96},{128,112},... | collective-permute-start | bytes 1474568 | tf_op jit(solution)/shard_map/ppermute | solution.py:522
  26.4 15.6 %copy-start.5 = (f32[64,192]{1,0:T(8,128)S(1)}, f32[64,192]{1,0:T(8,128)}, u32[]{:S(2)}) copy-start(f32[64,192]{1,0:T(8,128)} %constant.21.clone.tabz) | copy-start | bytes 147460
  26.4 12.5 %collective-permute-start.3 = (f32[4,96,128]{2,1,0:T(8,128)S(1)}, f32[4,96,128]{2,1,0:T(8,128)S(1)}, u32[]{:S(2)}, u32[]{:S(2)}) collective-permute-start(f32[4,96,128]{2,1,0:T(8,128)S(1)} %get-tuple-element.29.low_y), channel_id=1, source_target_pairs={{1,0},{2,1},{3,2},{4,3},{5,4},{6,5},{7,6},{8,7},{9,8},{10,9},{11,1... | collective-permute-start | bytes 589832 | tf_op jit(solution)/shard_map/ppermute | solution.py:522
  33.0 9.0 %collective-permute-start.2 = (f32[4,96,128]{2,1,0:T(8,128)S(1)}, f32[4,96,128]{2,1,0:T(8,128)S(1)}, u32[]{:S(2)}, u32[]{:S(2)}) collective-permute-start(f32[4,96,128]{2,1,0:T(8,128)S(1)} %get-tuple-element.30.high_y), channel_id=1, source_target_pairs={{0,1},{1,2},{2,3},{3,4},{4,5},{5,6},{6,7},{7,8},{8,9},{9,10},{10,1... | collective-permute-start | bytes 589832 | tf_op jit(solution)/shard_map/ppermute | solution.py:522
  38.8 44.0 %copy-start.7 = (f32[64,128]{1,0:T(8,128)S(1)}, f32[64,128]{1,0:T(8,128)}, u32[]{:S(2)}) copy-start(f32[64,128]{1,0:T(8,128)} %constant.22.clone.main) | copy-start | bytes 98308
  38.8 65.9 %copy-start.1 = (f32[512,64]{1,0:T(8,128)S(1)}, f32[512,64]{1,0:T(8,128)}, u32[]{:S(2)}) copy-start(f32[512,64]{1,0:T(8,128)} %constant.24.clone.inv) | copy-start | bytes 393220
  38.8 65.9 %copy-start.3 = (f32[128,256]{1,0:T(8,128)S(1)}, f32[128,256]{1,0:T(8,128)}, u32[]{:S(2)}) copy-start(f32[128,256]{1,0:T(8,128)} %constant.23.clone.fwd) | copy-start | bytes 393220
  44.2 60.5 %copy-start = (bf16[32,1,2,64,128]{4,3,2,1,0:T(8,128)(2,1)S(1)}, bf16[32,1,2,64,128]{4,3,2,1,0:T(8,128)(2,1)}, u32[]{:S(2)}) copy-start(bf16[32,1,2,64,128]{4,3,2,1,0:T(8,128)(2,1)} %w.1) | copy-start | bytes 3145732
  44.2 73.0 %copy-start.2 = (f32[256,32]{1,0:T(8,128)S(1)}, f32[256,32]{1,0:T(8,128)}, u32[]{:S(2)}) copy-start(f32[256,32]{1,0:T(8,128)} %constant.25.clone.inv) | copy-start | bytes 98308
  82.8 70.2 %copy-start.4 = (f32[64,192]{1,0:T(8,128)S(1)}, f32[64,192]{1,0:T(8,128)}, u32[]{:S(2)}) copy-start(f32[64,192]{1,0:T(8,128)} %constant.26.clone.tab) | copy-start | bytes 147460
  82.8 70.2 %copy-start.6 = (f32[64,64]{1,0:T(8,128)S(1)}, f32[64,64]{1,0:T(8,128)}, u32[]{:S(2)}) copy-start(f32[64,64]{1,0:T(8,128)} %skip.1) | copy-start | bytes 49156
  82.8 70.2 %copy-start.8 = (f32[64]{0:T(128)S(1)}, f32[64]{0:T(128)}, u32[]{:S(2)}) copy-start(f32[64]{0:T(128)} %param.29) | copy-start | bytes 772

commit v7 on v6

--- a/solution.py
+++ b/solution.py
@@ -40,6 +40,10 @@
     inner = x * (0.7978845608028654 + 0.035677408136300125 * (x * x))
     half = 0.5 * x
     return half + half * jnp.tanh(inner)
+
+
+def twice_gelu(x):
+    return x + x * jnp.tanh(x * (0.7978845608028654 + 0.035677408136300125 * (x * x)))
 
 
 def swap(x):
@@ -209,7 +213,7 @@
             pre_y = pre_x if ey[dy] is None else pre_x + ey[dy] * k_y
             for dz in range(3):
                 pre = pre_y if ez[dz] is None else pre_y + ez[dz] * k_z
-                pend.append(((dx, dy, dz), gelu(pre).astype(BF16)))
+                pend.append(((dx, dy, dz), twice_gelu(pre).astype(BF16)))
                 if len(pend) == 4:
                     flush()
     flush()
@@ -252,8 +256,7 @@
     tri = jnp.where(
         lax.broadcasted_iota(jnp.int32, (CHUNK, CHUNK), 0)
         < lax.broadcasted_iota(jnp.int32, (CHUNK, CHUNK), 1), 1.0, 0.0).astype(BF16)
-    for c in copies:
-        c.wait()
+    copies[0].wait()
     hx = home[0:1, :]
     hy = home[1:2, :]
     hz = home[2:3, :]
@@ -281,6 +284,8 @@
         rankb[part, :] = jnp.broadcast_to(rank[:, 0:1], (CHUNK, 128)).astype(jnp.int32)
         carry = carry + jnp.sum(hot, axis=1, keepdims=True)
 
+    for c in copies[1:]:
+        c.wait()
     slot = lax.broadcasted_iota(jnp.int32, (16, PTS), 0)
     bits = jnp.sum(
         jnp.where(slot < deg[...], jnp.left_shift(1, nbr[...]), 0), axis=0, keepdims=True)
@@ -300,7 +305,7 @@
     for j in range(4):
         taps[j] = jnp.broadcast_to(flat[0:CH, j:j + 1], (CH, LARGE))
     zero = jnp.zeros((CH, CH), F32)
-    sec_t = jnp.transpose(second[...].astype(F32))
+    sec_t = jnp.transpose(0.5 * second[...].astype(F32))
     quad[...] = jnp.concatenate(
         [jnp.concatenate([sec_t if i == j else zero for j in range(4)], axis=1)
          for i in range(4)], axis=0).astype(BF16)
@@ -473,7 +478,7 @@
         out[:, i * CY:(i + 1) * CY, :] = y.reshape(rows // CY, CY, HALVES)
 
 
-def final_kernel(zb, tab, own, skip, bias, out):
+def final_kernel(zb, tab, own, skip, bias, out, rows, sems):
     lane = lax.broadcasted_iota(jnp.int32, (MODES, HALVES), 1)
     zero = jnp.zeros((CH, CH), F32)
     skip_t = jnp.transpose(skip[...])
@@ -482,6 +487,7 @@
     col = jnp.concatenate([bias[...], bias[...]], axis=1)
     col = jnp.transpose(jnp.broadcast_to(col, (8, HALVES)))
     col = jnp.broadcast_to(col[:, 0:1], (HALVES, NZ))
+    copies = []
     for x in range(CX):
         for yp in range(CY // 2):
             i = x * CY + 2 * yp
@@ -489,10 +495,27 @@
             v = zb[:, i + 1, :]
             s = jnp.concatenate(
                 [jnp.where(lane < CH, u, swap(v)), jnp.where(lane < CH, swap(u), v)], axis=0)
-            spectral = mm(s, tab[...], TN, HIGH)
             lat = own[i:i + 2].reshape(2 * CH, NZ)
-            total = spectral + mm(pair, lat, NN, HIGH) + col
-            out[x, 2 * yp:2 * yp + 2] = gelu(total).astype(BF16).reshape(2, CH, NZ)
+            left = jnp.concatenate([jnp.transpose(s), pair], axis=1)
+            total = mm(left, jnp.concatenate([tab[...], lat], axis=0), NN, HIGH) + col
+            rows[x, 2 * yp:2 * yp + 2] = gelu(total).astype(BF16).reshape(2, CH, NZ)
+        copies.append(pltpu.make_async_copy(rows.at[x], out.at[x], sems.at[x]))
+        copies[-1].start()
+    for c in copies:
+        c.wait()
+
+
+def finish(zb, own, skip, bias):
+    cells = jax.ShapeDtypeStruct((CX, CY, CH, NZ), BF16)
+    return pl.pallas_call(
+        final_kernel,
+        out_shape=cells,
+        in_specs=[pl.BlockSpec(memory_space=pltpu.VMEM)] * 5,
+        out_specs=pl.BlockSpec(memory_space=pltpu.HBM),
+        scratch_shapes=[pltpu.VMEM(cells.shape, BF16), pltpu.SemaphoreType.DMA((CX,))],
+        compiler_params=LIMIT,
+        name="finish",
+    )(zb, jnp.asarray(z_inverse_table()), own, skip, bias)
 
 
 def call(kernel, shapes, args, scratch=(), smem=False, name=None):
@@ -558,10 +581,7 @@
     r = call(y_back_kernel, shape(pens, 2 * CX * CY, HALVES),
              (r, jnp.asarray(y_inverse_table(pens))), name="inverse_y")
     r = exchange(r, "pen")
-    out = call(
-        final_kernel, jax.ShapeDtypeStruct((CX, CY, CH, NZ), BF16),
-        (r.reshape(MODES, CX * CY, HALVES), jnp.asarray(z_inverse_table()), own,
-         skip_weights, skip_bias[None, :]), name="finish")
+    out = finish(r.reshape(MODES, CX * CY, HALVES), own, skip_weights, skip_bias[None, :])
     return out.transpose(0, 1, 3, 2)
 
 

time: 157 us -> 156 us (level)
  Pallas kernels: 35.4 us -> 33.2 us
  starting transfers between devices: 11.2 us -> 12.9 us
    pallas_call x6 -> x5, Pallas kernels: 8.71 us -> 5.25 us  [call(): pl.pallas_call(kernel, out_shape=shapes, in_specs=specs, scratch_shapes=l...]
    pallas_call x0 -> x1, Pallas kernels: none -> 3.12 us  [finish(): pl.pallas_call(final_kernel, out_shape=cells, in_specs=[pl.BlockSpec(memo...]
    ppermute x4, starting transfers between devices: 11.2 us -> 12.9 us  [moved(): lax.ppermute(x, axis, [(i - step, i) for i in devices if i - step in devi...]
where the time goes in v7:
time: 156 us
  blocking collectives  105 us (67%)
  Pallas kernels  33.2 us (21%)
  starting transfers between devices  12.9 us (8%)
  waiting for transfers between devices  3.83 us (2%)
    all_to_all x4, blocking collectives, exchange(): return lax.all_to_all(x, axis, split_axis=0, concat_axis=0, tiled=True)  105 us
    pallas_call x1, Pallas kernels, lift_points(): pl.pallas_call(functools.partial(sides_kernel, last), out_shape=[shape(CX...  15.6 us
    ppermute x4, starting transfers between devices, moved(): lax.ppermute(x, axis, [(i - step, i) for i in devices if i - step in devi...  12.9 us
    pallas_call x2, Pallas kernels, lift_inner(): pl.pallas_call(functools.partial(middle_kernel, last), out_shape=shape(CX...  9.2 us
    pallas_call x5, Pallas kernels, call(): pl.pallas_call(kernel, out_shape=shapes, in_specs=specs, scratch_shapes=l...  5.25 us
    ppermute x4, waiting for transfers between devices, moved(): lax.ppermute(x, axis, [(i - step, i) for i in devices if i - step in devi...  3.83 us
    pallas_call x1, Pallas kernels, finish(): pl.pallas_call(final_kernel, out_shape=cells, in_specs=[pl.BlockSpec(memo...  3.12 us
  transfers between devices with their start and end apart: 4, of which 1 were waited for; matrix products, arithmetic and copies ran while one was open for 0% of the time, Pallas kernels for 6%

profile of v7, /device:TPU:32, one launch (start us, length us, event | category | flops | bytes accessed | tf_op | source)
XLA Modules:
  0.0 155.9 jit_solution(15030180239341896676)
XLA Ops:
  0.0 0.1 pad_add_fusion.at
  0.1 15.6 %lift_sides.1 = (f32[6,10,64,192]{3,2,1,0:T(8,128)S(1)}, f32[10,96,128]{2,1,0:T(8,128)S(1)}, f32[10,96,128]{2,1,0:T(8,128)S(1)}, bf16[112,2048]{1,0:T(8,128)(2,1...) custom-call(s32[2]{0:T(128)S(1)} %pad_add_fusion.at, ...), custom_call_target="tpu_custom_call" | custom-call | tf_op jit(solution)/shard_map/lift_sides/pallas_call | solution.py:352
  15.7 1.8 %collective-permute-start = (f32[10,96,128]{2,1,0:T(8,128)S(1)}, f32[10,96,128]{2,1,0:T(8,128)S(1)}, u32[]{:S(2)}, u32[]{:S(2)}) collective-permute-start(f32[10,96,128]{2,1,0:T(8,128)S(1)} %get-tuple-element.27), channel_id=1, source_target_pairs={{0,16},{16,32},{32,48},{48,64},{64,80},{80,96},{96,112},{112,128},... | collective-permute-start | bytes 1474568 | tf_op jit(solution)/shard_map/ppermute | solution.py:545
  17.5 1.3 collective-permute-start.1
  18.8 5.4 %lift_ends.1.middle = f32[4,10,64,192]{3,2,1,0:T(8,128)S(1)} custom-call(s32[2]{0:T(128)S(1)} %pad_add_fusion.at, s32[2]{0:T(128)S(1)} %get-tuple-element.20.span, bf16[112,2048]{1,0:T(8,128)(2,1)S(1)} %get-tuple-element.21.data, s32[2048,128]{1,0:T(8,128)S(1)} %get-tuple-element.22.rankb, f32[4,64,512]{2,1,0:T(8,128)S(1)} %get-tuple-element.23.taps, ...), custom_call_target="tpu_custom_call" | custom-call | tf_op jit(solution)/shard_map/lift_ends/pallas_call | solution.py:379
  24.3 0.0 collective-permute-done.below
  24.3 0.0 collective-permute-done.1.above
  24.3 0.7 y_ends.1
  25.0 0.0 copy-start.5
  25.0 7.9 %collective-permute-start.3 = (f32[4,96,128]{2,1,0:T(8,128)S(1)}, f32[4,96,128]{2,1,0:T(8,128)S(1)}, u32[]{:S(2)}, u32[]{:S(2)}) collective-permute-start(f32[4,96,128]{2,1,0:T(8,128)S(1)} %get-tuple-element.29.low_y), channel_id=1, source_target_pairs={{1,0},{2,1},{3,2},{4,3},{5,4},{6,5},{7,6},{8,7},{9,8},{10,9},{11,1... | collective-permute-start | bytes 589832 | tf_op jit(solution)/shard_map/ppermute | solution.py:545
  32.9 1.9 %collective-permute-start.2 = (f32[4,96,128]{2,1,0:T(8,128)S(1)}, f32[4,96,128]{2,1,0:T(8,128)S(1)}, u32[]{:S(2)}, u32[]{:S(2)}) collective-permute-start(f32[4,96,128]{2,1,0:T(8,128)S(1)} %get-tuple-element.30.high_y), channel_id=1, source_target_pairs={{0,1},{1,2},{2,3},{3,4},{4,5},{5,6},{6,7},{7,8},{8,9},{9,10},{10,1... | collective-permute-start | bytes 589832 | tf_op jit(solution)/shard_map/ppermute | solution.py:545
  34.8 3.8 %lift_core.1.rest = f32[4,10,64,192]{3,2,1,0:T(8,128)S(1)} custom-call(s32[2]{0:T(128)S(1)} %pad_add_fusion.at, s32[2]{0:T(128)S(1)} %get-tuple-element.26.span, bf16[112,2048]{1,0:T(8,128)(2,1)S(1)} %get-tuple-element.21.data, s32[2048,128]{1,0:T(8,128)S(1)} %get-tuple-element.22.rankb, f32[4,64,512]{2,1,0:T(8,128)S(1)} %get-tuple-element.23.taps, ...), custom_call_target="tpu_custom_call" | custom-call | tf_op jit(solution)/shard_map/lift_core/pallas_call | solution.py:379
  38.6 0.0 copy-start.7
  38.6 0.0 copy-start.1
  38.6 0.0 copy-start.3
  38.6 0.0 collective-permute-done.3.right
  38.6 3.8 %collective-permute-done.2.left = f32[4,96,128]{2,1,0:T(8,128)S(1)} collective-permute-done((f32[4,96,128]{2,1,0:T(8,128)S(1)}, f32[4,96,128]{2,1,0:T(8,128)S(1)}, u32[]{:S(2)}, u32[]{:S(2)}) %collective-permute-start.2) | collective-permute-done | bytes 196640 | tf_op jit(solution)/shard_map/ppermute | solution.py:545
  42.5 0.0 copy-done.5
  42.5 2.2 %latent_z.1 = (f32[32,32,128]{2,1,0:T(8,128)S(1)}, f32[32,64,192]{2,1,0:T(8,128)S(1)}) custom-call(s32[2]{0:T(128)S(1)} %pad_add_fusion.at, f32[64,192]{1,0:T(8,128)S(1)} %copy-done.5, f32[6,10,64,192]{3,2,1,0:T(8,128)S(1)} %get-tuple-element.19.sides, f32[4,10,64,192]{3,2,1,0:T(8,128)S(1)} %lift_ends.1.middle, f32[4,10,64,192]{3,2,1,0:T(8,128)S(1)} %lift_core.1.rest, ...), custom_call_target="tpu_custom_call" | custom-call | tf_op jit(solution)/shard_map/latent_z/pallas_call | solution.py:525
  44.7 0.0 copy-start
  44.7 0.0 copy-start.2
  44.7 35.4 %all_to_all.20.r = f32[16,64,128]{2,1,0:T(8,128)S(1)} all-to-all(f32[16,64,128]{2,1,0:T(8,128)S(1)} %bitcast.11), channel_id=1, replica_groups=mesh['bin'=32,'pen'=16] {'pen'}, dimensions={0} | all-to-all | bytes 1048576 | tf_op jit(solution)/shard_map/all_to_all | solution.py:540
  80.1 0.0 copy-done.7
  80.1 0.4 forward_y.1
  80.5 23.4 %all_to_all.21.r = f32[32,8,128]{2,1,0:T(8,128)S(1)} all-to-all(f32[32,8,128]{2,1,0:T(8,128)S(1)} %forward_y.1), channel_id=1, replica_groups=mesh['bin'=32,'pen'=16] {'bin'}, dimensions={0} | all-to-all | bytes 262144 | tf_op jit(solution)/shard_map/all_to_all | solution.py:540
  103.9 0.0 copy-done.1
  103.9 1.2 mix_x.1
  105.2 11.3 %all_to_all.22.r = f32[32,8,128]{2,1,0:T(8,128)S(1)} all-to-all(f32[32,8,128]{2,1,0:T(8,128)S(1)} %mix_x.1), channel_id=1, replica_groups=mesh['bin'=32,'pen'=16] {'bin'}, dimensions={0} | all-to-all | bytes 262144 | tf_op jit(solution)/shard_map/all_to_all | solution.py:540
  116.5 0.7 inverse_y.1
  117.1 35.4 %all_to_all.23 = f32[16,64,128]{2,1,0:T(8,128)S(1)} all-to-all(f32[16,64,128]{2,1,0:T(8,128)S(1)} %inverse_y.1), channel_id=1, replica_groups=mesh['bin'=32,'pen'=16] {'pen'}, dimensions={0} | all-to-all | bytes 1048576 | tf_op jit(solution)/shard_map/all_to_all | solution.py:540
  152.6 0.0 copy-done.6
  152.6 3.1 %finish.1 = bf16[4,8,64,192]{3,2,1,0:T(8,128)(2,1)} custom-call(f32[32,32,128]{2,1,0:T(8,128)S(1)} %bitcast.10, f32[64,192]{1,0:T(8,128)S(1)} %copy-done.4, f32[32,64,192]{2,1,0:T(8,128)S(1)} %get-tuple-element.32.own, f32[64,64]{1,0:T(8,128)S(1)} %copy-done.6, f32[1,64]{1,0:T(1,128)S(1)} %bitcast.12), custom_call_target="tpu_custom_call" | custom-call | tf_op jit(solution)/shard_map/finish/pallas_call | solution.py:510
  (8 shorter events, 0.0 us)
Async XLA Ops:
  15.7 8.5 %collective-permute-start = (f32[10,96,128]{2,1,0:T(8,128)S(1)}, f32[10,96,128]{2,1,0:T(8,128)S(1)}, u32[]{:S(2)}, u32[]{:S(2)}) collective-permute-start(f32[10,96,128]{2,1,0:T(8,128)S(1)} %get-tuple-element.27), channel_id=1, source_target_pairs={{0,16},{16,32},{32,48},{48,64},{64,80},{80,96},{96,112},{112,128},... | collective-permute-start | bytes 1474568 | tf_op jit(solution)/shard_map/ppermute | solution.py:545
  17.5 6.8 %collective-permute-start.1 = (f32[10,96,128]{2,1,0:T(8,128)S(1)}, f32[10,96,128]{2,1,0:T(8,128)S(1)}, u32[]{:S(2)}, u32[]{:S(2)}) collective-permute-start(f32[10,96,128]{2,1,0:T(8,128)S(1)} %get-tuple-element.28), channel_id=1, source_target_pairs={{16,0},{32,16},{48,32},{64,48},{80,64},{96,80},{112,96},{128,112},... | collective-permute-start | bytes 1474568 | tf_op jit(solution)/shard_map/ppermute | solution.py:545
  25.0 17.5 %copy-start.5 = (f32[64,192]{1,0:T(8,128)S(1)}, f32[64,192]{1,0:T(8,128)}, u32[]{:S(2)}) copy-start(f32[64,192]{1,0:T(8,128)} %constant.21.clone.tabz) | copy-start | bytes 147460
  25.0 13.6 %collective-permute-start.3 = (f32[4,96,128]{2,1,0:T(8,128)S(1)}, f32[4,96,128]{2,1,0:T(8,128)S(1)}, u32[]{:S(2)}, u32[]{:S(2)}) collective-permute-start(f32[4,96,128]{2,1,0:T(8,128)S(1)} %get-tuple-element.29.low_y), channel_id=1, source_target_pairs={{1,0},{2,1},{3,2},{4,3},{5,4},{6,5},{7,6},{8,7},{9,8},{10,9},{11,1... | collective-permute-start | bytes 589832 | tf_op jit(solution)/shard_map/ppermute | solution.py:545
  32.9 9.6 %collective-permute-start.2 = (f32[4,96,128]{2,1,0:T(8,128)S(1)}, f32[4,96,128]{2,1,0:T(8,128)S(1)}, u32[]{:S(2)}, u32[]{:S(2)}) collective-permute-start(f32[4,96,128]{2,1,0:T(8,128)S(1)} %get-tuple-element.30.high_y), channel_id=1, source_target_pairs={{0,1},{1,2},{2,3},{3,4},{4,5},{5,6},{6,7},{7,8},{8,9},{9,10},{10,1... | collective-permute-start | bytes 589832 | tf_op jit(solution)/shard_map/ppermute | solution.py:545
  38.6 41.5 %copy-start.7 = (f32[64,128]{1,0:T(8,128)S(1)}, f32[64,128]{1,0:T(8,128)}, u32[]{:S(2)}) copy-start(f32[64,128]{1,0:T(8,128)} %constant.22.clone.main) | copy-start | bytes 98308
  38.6 65.3 %copy-start.1 = (f32[512,64]{1,0:T(8,128)S(1)}, f32[512,64]{1,0:T(8,128)}, u32[]{:S(2)}) copy-start(f32[512,64]{1,0:T(8,128)} %constant.24.clone.inv) | copy-start | bytes 393220
  38.6 65.3 %copy-start.3 = (f32[128,256]{1,0:T(8,128)S(1)}, f32[128,256]{1,0:T(8,128)}, u32[]{:S(2)}) copy-start(f32[128,256]{1,0:T(8,128)} %constant.23.clone.fwd) | copy-start | bytes 393220
  44.7 59.2 %copy-start = (bf16[32,1,2,64,128]{4,3,2,1,0:T(8,128)(2,1)S(1)}, bf16[32,1,2,64,128]{4,3,2,1,0:T(8,128)(2,1)}, u32[]{:S(2)}) copy-start(bf16[32,1,2,64,128]{4,3,2,1,0:T(8,128)(2,1)} %w.1) | copy-start | bytes 3145732
  44.7 71.8 %copy-start.2 = (f32[256,32]{1,0:T(8,128)S(1)}, f32[256,32]{1,0:T(8,128)}, u32[]{:S(2)}) copy-start(f32[256,32]{1,0:T(8,128)} %constant.25.clone.inv) | copy-start | bytes 98308
  80.1 72.5 %copy-start.4 = (f32[64,192]{1,0:T(8,128)S(1)}, f32[64,192]{1,0:T(8,128)}, u32[]{:S(2)}) copy-start(f32[64,192]{1,0:T(8,128)} %constant.26.clone.tab) | copy-start | bytes 147460
  80.1 72.5 %copy-start.6 = (f32[64,64]{1,0:T(8,128)S(1)}, f32[64,64]{1,0:T(8,128)}, u32[]{:S(2)}) copy-start(f32[64,64]{1,0:T(8,128)} %skip.1) | copy-start | bytes 49156
  80.1 72.5 %copy-start.8 = (f32[64]{0:T(128)S(1)}, f32[64]{0:T(128)}, u32[]{:S(2)}) copy-start(f32[64]{0:T(128)} %param.29) | copy-start | bytes 772

commit v8 on v7

--- a/solution.py
+++ b/solution.py
@@ -324,8 +324,22 @@
         high[y] = pack(grid[CX + 1, y])
 
 
-def middle_kernel(last, at, span, data, rankb, taps, quad, lift_t, grid, mess, keys):
-    grid[...] = jnp.zeros_like(grid)
+def middle_kernel(last, at, span, data, rankb, taps, quad, lift_t, *refs):
+    *halo, grid, mess, keys = refs
+    if halo:
+        sides, middle, below, above = halo
+        low = at[0] == 0
+        top = at[0] * CX + CX - 1 == last[0]
+        for x in range(CX):
+            for y in range(1, CY + 1):
+                l = sides[x + 1, y] + middle[x, y]
+                if x == 0:
+                    l = l + jnp.where(low, sides[0, y], unpack(below[y]))
+                if x == CX - 1:
+                    l = l + jnp.where(top, sides[CX + 1, y], unpack(above[y]))
+                grid[x, y] = l
+    else:
+        grid[...] = jnp.zeros_like(grid)
 
     def chunk(size, first, step, _):
         add_chunk(last, at, first + step * size, size, 1, data, rankb, taps, quad, lift_t, mess,
@@ -373,13 +387,13 @@
     return grid, low, high, prepared, span_a, span_b
 
 
-def lift_inner(at, last, span, prepared, name):
+def lift_inner(at, last, span, prepared, name, halo=()):
     vmem = pl.BlockSpec(memory_space=pltpu.VMEM)
     smem = pl.BlockSpec(memory_space=pltpu.SMEM)
     return pl.pallas_call(
         functools.partial(middle_kernel, last),
         out_shape=shape(CX, CY + 2, CH, NZ),
-        in_specs=[smem, smem] + [vmem] * 5,
+        in_specs=[smem, smem] + [vmem] * (5 + len(halo)),
         out_specs=vmem,
         scratch_shapes=[
             pltpu.VMEM((LARGE // SUB, 9 * CH, 3 * SUB), BF16),
@@ -387,7 +401,7 @@
         ],
         compiler_params=LIMIT,
         name=name,
-    )(at, span, *prepared)
+    )(at, span, *prepared, *halo)
 
 
 def ends_kernel(last, at, sides, middle, below, above, low_y, high_y):
@@ -410,23 +424,16 @@
     return jnp.where(lane < CH, re, swap(im)), jnp.where(lane < CH, swap(re), im)
 
 
-def latent_kernel(last, at, tabz, sides, middle, rest, below, above, low_y, high_y, left, right,
-                  spec, own):
-    low = at[0] == 0
-    top = at[0] == last[0]
+def latent_kernel(last, at, tabz, rest, low_y, high_y, left, right, spec, own):
     first_pen = at[1] == 0
-    last_pen = at[1] == last[1]
+    last_pen = at[1] == last
     table = tabz[...]
     for x in range(CX):
         for yp in range(CY // 2):
             i = x * CY + 2 * yp
             for j in range(2):
                 y = 2 * yp + j + 1
-                l = sides[x + 1, y] + middle[x, y] + rest[x, y]
-                if x == 0:
-                    l = l + jnp.where(low, sides[0, y], unpack(below[y]))
-                if x == CX - 1:
-                    l = l + jnp.where(top, sides[CX + 1, y], unpack(above[y]))
+                l = rest[x, y]
                 if y == 1:
                     l = l + unpack(jnp.where(first_pen, low_y[x], left[x]))
                 if y == CY:
@@ -563,12 +570,12 @@
         (at, sides, middle, below, above), smem=True, name="y_ends")
     left = moved(high_y, "pen", 1)
     right = moved(low_y, "pen", -1)
-    rest = lift_inner(at, last, span_b, prepared, "lift_core")
+    rest = lift_inner(at, last, span_b, prepared, "lift_core", (sides, middle, below, above))
     spec, own = call(
-        functools.partial(latent_kernel, (bins - 1, pens - 1)),
+        functools.partial(latent_kernel, pens - 1),
         [shape(MODES, CX * CY, HALVES), shape(CX * CY, CH, NZ)],
-        (at, jnp.asarray(z_forward_table()), sides, middle, rest, below, above, low_y, high_y,
-         left, right), smem=True, name="latent_z")
+        (at, jnp.asarray(z_forward_table()), rest, low_y, high_y, left, right),
+        smem=True, name="latent_z")
     r = exchange(spec.reshape(pens, 2 * CX * CY, HALVES), "pen")
     r = call(y_kernel, shape(MODES, 2 * CX, HALVES), (r, jnp.asarray(y_forward_table(pens))),
              name="forward_y")

time: 156 us -> 156 us (level)
  blocking collectives: 105 us -> 110 us
  waiting for transfers between devices: 3.83 us -> 0.47 us
  starting transfers between devices: 12.9 us -> 11.3 us
    all_to_all x4, blocking collectives: 105 us -> 110 us  [exchange(): return lax.all_to_all(x, axis, split_axis=0, concat_axis=0, tiled=True)]
    ppermute x4, waiting for transfers between devices: 3.83 us -> 0.47 us  [moved(): lax.ppermute(x, axis, [(i - step, i) for i in devices if i - step in devi...]
where the time goes in v8:
time: 156 us
  blocking collectives  110 us (71%)
  Pallas kernels  34.3 us (22%)
  starting transfers between devices  11.3 us (7%)
    all_to_all x4, blocking collectives, exchange(): return lax.all_to_all(x, axis, split_axis=0, concat_axis=0, tiled=True)  110 us
    pallas_call x1, Pallas kernels, lift_points(): pl.pallas_call(functools.partial(sides_kernel, last), out_shape=[shape(CX...  16.6 us
    ppermute x4, starting transfers between devices, moved(): lax.ppermute(x, axis, [(i - step, i) for i in devices if i - step in devi...  11.3 us
    pallas_call x2, Pallas kernels, lift_inner(): pl.pallas_call(functools.partial(middle_kernel, last), out_shape=shape(CX...  9.4 us
    pallas_call x5, Pallas kernels, call(): pl.pallas_call(kernel, out_shape=shapes, in_specs=specs, scratch_shapes=l...  5.17 us
    pallas_call x1, Pallas kernels, finish(): pl.pallas_call(final_kernel, out_shape=cells, in_specs=[pl.BlockSpec(memo...  3.17 us
  transfers between devices with their start and end apart: 4, of which 1 were waited for; matrix products, arithmetic and copies ran while one was open for 0% of the time, Pallas kernels for 6%

profile of v8, /device:TPU:32, one launch (start us, length us, event | category | flops | bytes accessed | tf_op | source)
XLA Modules:
  0.0 156.2 jit_solution(17400770265307131833)
XLA Ops:
  0.0 0.1 pad_add_fusion.at
  0.1 16.6 %lift_sides.1 = (f32[6,10,64,192]{3,2,1,0:T(8,128)S(1)}, f32[10,96,128]{2,1,0:T(8,128)S(1)}, f32[10,96,128]{2,1,0:T(8,128)S(1)}, bf16[112,2048]{1,0:T(8,128)(2,1...) custom-call(s32[2]{0:T(128)S(1)} %pad_add_fusion.at, ...), custom_call_target="tpu_custom_call" | custom-call | tf_op jit(solution)/shard_map/lift_sides/pallas_call | solution.py:366
  16.6 1.3 collective-permute-start
  18.0 1.3 collective-permute-start.1
  19.3 5.4 %lift_ends.1.refs_1_.middle = f32[4,10,64,192]{3,2,1,0:T(8,128)S(1)} custom-call(s32[2]{0:T(128)S(1)} %pad_add_fusion.at, s32[2]{0:T(128)S(1)} %get-tuple-element.26.span, bf16[112,2048]{1,0:T(8,128)(2,1)S(1)} %get-tuple-element.20.data, s32[2048,128]{1,0:T(8,128)S(1)} %get-tuple-element.21.rankb, f32[4,64,512]{2,1,0:T(8,128)S(1)} %get-tuple-element.22.taps, ...), custom_call_target="tpu_custom_call" | custom-call | tf_op jit(solution)/shard_map/lift_ends/pallas_call | solution.py:393
  24.7 0.0 collective-permute-done.refs_2_.below
  24.7 0.0 collective-permute-done.1.refs_3_.above
  24.8 0.7 y_ends.1
  25.5 3.5 %collective-permute-start.2 = (f32[4,96,128]{2,1,0:T(8,128)S(1)}, f32[4,96,128]{2,1,0:T(8,128)S(1)}, u32[]{:S(2)}, u32[]{:S(2)}) collective-permute-start(f32[4,96,128]{2,1,0:T(8,128)S(1)} %get-tuple-element.30.high_y), channel_id=1, source_target_pairs={{0,1},{1,2},{2,3},{3,4},{4,5},{5,6},{6,7},{7,8},{8,9},{9,10},{10,1... | collective-permute-start | bytes 589832 | tf_op jit(solution)/shard_map/ppermute | solution.py:552
  28.9 5.3 %collective-permute-start.3 = (f32[4,96,128]{2,1,0:T(8,128)S(1)}, f32[4,96,128]{2,1,0:T(8,128)S(1)}, u32[]{:S(2)}, u32[]{:S(2)}) collective-permute-start(f32[4,96,128]{2,1,0:T(8,128)S(1)} %get-tuple-element.29.low_y), channel_id=1, source_target_pairs={{1,0},{2,1},{3,2},{4,3},{5,4},{6,5},{7,6},{8,7},{9,8},{10,9},{11,1... | collective-permute-start | bytes 589832 | tf_op jit(solution)/shard_map/ppermute | solution.py:552
  34.2 0.0 copy-start.5
  34.2 4.0 %lift_core.1.rest = f32[4,10,64,192]{3,2,1,0:T(8,128)S(1)} custom-call(s32[2]{0:T(128)S(1)} %pad_add_fusion.at, s32[2]{0:T(128)S(1)} %get-tuple-element.19.span, bf16[112,2048]{1,0:T(8,128)(2,1)S(1)} %get-tuple-element.20.data, s32[2048,128]{1,0:T(8,128)S(1)} %get-tuple-element.21.rankb, f32[4,64,512]{2,1,0:T(8,128)S(1)} %get-tuple-element.22.taps, ...), custom_call_target="tpu_custom_call" | custom-call | tf_op jit(solution)/shard_map/lift_core/pallas_call | solution.py:393
  38.2 0.0 copy-start.7
  38.2 0.0 copy-start
  38.2 0.0 copy-start.1
  38.2 0.0 copy-start.3
  38.2 0.0 collective-permute-done.2.left
  38.2 0.5 collective-permute-done.3.right
  38.7 0.0 copy-done.5
  38.7 2.1 %latent_z.1 = (f32[32,32,128]{2,1,0:T(8,128)S(1)}, f32[32,64,192]{2,1,0:T(8,128)S(1)}) custom-call(s32[2]{0:T(128)S(1)} %pad_add_fusion.at, f32[64,192]{1,0:T(8,128)S(1)} %copy-done.5, f32[4,10,64,192]{3,2,1,0:T(8,128)S(1)} %lift_core.1.rest, f32[4,96,128]{2,1,0:T(8,128)S(1)} %get-tuple-element.29.low_y, f32[4,96,128]{2,1,0:T(8,128)S(1)} %get-tuple-element.30.high_y, ...), custom_call_target="tpu_custom_call" | custom-call | tf_op jit(solution)/shard_map/latent_z/pallas_call | solution.py:532
  40.8 0.0 copy-start.2
  40.8 43.7 %all_to_all.20.r = f32[16,64,128]{2,1,0:T(8,128)S(1)} all-to-all(f32[16,64,128]{2,1,0:T(8,128)S(1)} %bitcast.11), channel_id=1, replica_groups=mesh['bin'=32,'pen'=16] {'pen'}, dimensions={0} | all-to-all | bytes 1048576 | tf_op jit(solution)/shard_map/all_to_all | solution.py:547
  84.5 0.0 copy-done.7
  84.5 0.4 forward_y.1
  85.0 18.8 %all_to_all.21.r = f32[32,8,128]{2,1,0:T(8,128)S(1)} all-to-all(f32[32,8,128]{2,1,0:T(8,128)S(1)} %forward_y.1), channel_id=1, replica_groups=mesh['bin'=32,'pen'=16] {'bin'}, dimensions={0} | all-to-all | bytes 262144 | tf_op jit(solution)/shard_map/all_to_all | solution.py:547
  103.8 0.0 copy-done
  103.8 0.0 copy-done.1
  103.8 1.3 mix_x.1
  105.0 11.3 %all_to_all.22.r = f32[32,8,128]{2,1,0:T(8,128)S(1)} all-to-all(f32[32,8,128]{2,1,0:T(8,128)S(1)} %mix_x.1), channel_id=1, replica_groups=mesh['bin'=32,'pen'=16] {'bin'}, dimensions={0} | all-to-all | bytes 262144 | tf_op jit(solution)/shard_map/all_to_all | solution.py:547
  116.3 0.7 inverse_y.1
  117.0 35.9 %all_to_all.23 = f32[16,64,128]{2,1,0:T(8,128)S(1)} all-to-all(f32[16,64,128]{2,1,0:T(8,128)S(1)} %inverse_y.1), channel_id=1, replica_groups=mesh['bin'=32,'pen'=16] {'pen'}, dimensions={0} | all-to-all | bytes 1048576 | tf_op jit(solution)/shard_map/all_to_all | solution.py:547
  152.9 3.2 %finish.1 = bf16[4,8,64,192]{3,2,1,0:T(8,128)(2,1)} custom-call(f32[32,32,128]{2,1,0:T(8,128)S(1)} %bitcast.10, f32[64,192]{1,0:T(8,128)S(1)} %copy-done.4, f32[32,64,192]{2,1,0:T(8,128)S(1)} %get-tuple-element.32.own, f32[64,64]{1,0:T(8,128)S(1)} %copy-done.6, f32[1,64]{1,0:T(1,128)S(1)} %bitcast.12), custom_call_target="tpu_custom_call" | custom-call | tf_op jit(solution)/shard_map/finish/pallas_call | solution.py:517
  (8 shorter events, 0.0 us)
Async XLA Ops:
  16.6 8.1 %collective-permute-start = (f32[10,96,128]{2,1,0:T(8,128)S(1)}, f32[10,96,128]{2,1,0:T(8,128)S(1)}, u32[]{:S(2)}, u32[]{:S(2)}) collective-permute-start(f32[10,96,128]{2,1,0:T(8,128)S(1)} %get-tuple-element.27), channel_id=1, source_target_pairs={{0,16},{16,32},{32,48},{48,64},{64,80},{80,96},{96,112},{112,128},... | collective-permute-start | bytes 1474568 | tf_op jit(solution)/shard_map/ppermute | solution.py:552
  18.0 6.8 %collective-permute-start.1 = (f32[10,96,128]{2,1,0:T(8,128)S(1)}, f32[10,96,128]{2,1,0:T(8,128)S(1)}, u32[]{:S(2)}, u32[]{:S(2)}) collective-permute-start(f32[10,96,128]{2,1,0:T(8,128)S(1)} %get-tuple-element.28), channel_id=1, source_target_pairs={{16,0},{32,16},{48,32},{64,48},{80,64},{96,80},{112,96},{128,112},... | collective-permute-start | bytes 1474568 | tf_op jit(solution)/shard_map/ppermute | solution.py:552
  25.5 12.8 %collective-permute-start.2 = (f32[4,96,128]{2,1,0:T(8,128)S(1)}, f32[4,96,128]{2,1,0:T(8,128)S(1)}, u32[]{:S(2)}, u32[]{:S(2)}) collective-permute-start(f32[4,96,128]{2,1,0:T(8,128)S(1)} %get-tuple-element.30.high_y), channel_id=1, source_target_pairs={{0,1},{1,2},{2,3},{3,4},{4,5},{5,6},{6,7},{7,8},{8,9},{9,10},{10,1... | collective-permute-start | bytes 589832 | tf_op jit(solution)/shard_map/ppermute | solution.py:552
  28.9 9.8 %collective-permute-start.3 = (f32[4,96,128]{2,1,0:T(8,128)S(1)}, f32[4,96,128]{2,1,0:T(8,128)S(1)}, u32[]{:S(2)}, u32[]{:S(2)}) collective-permute-start(f32[4,96,128]{2,1,0:T(8,128)S(1)} %get-tuple-element.29.low_y), channel_id=1, source_target_pairs={{1,0},{2,1},{3,2},{4,3},{5,4},{6,5},{7,6},{8,7},{9,8},{10,9},{11,1... | collective-permute-start | bytes 589832 | tf_op jit(solution)/shard_map/ppermute | solution.py:552
  34.2 4.5 %copy-start.5 = (f32[64,192]{1,0:T(8,128)S(1)}, f32[64,192]{1,0:T(8,128)}, u32[]{:S(2)}) copy-start(f32[64,192]{1,0:T(8,128)} %constant.21.clone.tabz) | copy-start | bytes 147460
  38.2 46.3 %copy-start.7 = (f32[64,128]{1,0:T(8,128)S(1)}, f32[64,128]{1,0:T(8,128)}, u32[]{:S(2)}) copy-start(f32[64,128]{1,0:T(8,128)} %constant.22.clone.main) | copy-start | bytes 98308
  38.2 65.6 %copy-start = (bf16[32,1,2,64,128]{4,3,2,1,0:T(8,128)(2,1)S(1)}, bf16[32,1,2,64,128]{4,3,2,1,0:T(8,128)(2,1)}, u32[]{:S(2)}) copy-start(bf16[32,1,2,64,128]{4,3,2,1,0:T(8,128)(2,1)} %w.1) | copy-start | bytes 3145732
  38.2 65.6 %copy-start.1 = (f32[512,64]{1,0:T(8,128)S(1)}, f32[512,64]{1,0:T(8,128)}, u32[]{:S(2)}) copy-start(f32[512,64]{1,0:T(8,128)} %constant.24.clone.inv) | copy-start | bytes 393220
  38.2 65.6 %copy-start.3 = (f32[128,256]{1,0:T(8,128)S(1)}, f32[128,256]{1,0:T(8,128)}, u32[]{:S(2)}) copy-start(f32[128,256]{1,0:T(8,128)} %constant.23.clone.fwd) | copy-start | bytes 393220
  40.8 75.5 %copy-start.2 = (f32[256,32]{1,0:T(8,128)S(1)}, f32[256,32]{1,0:T(8,128)}, u32[]{:S(2)}) copy-start(f32[256,32]{1,0:T(8,128)} %constant.25.clone.inv) | copy-start | bytes 98308
  84.5 68.4 %copy-start.4 = (f32[64,192]{1,0:T(8,128)S(1)}, f32[64,192]{1,0:T(8,128)}, u32[]{:S(2)}) copy-start(f32[64,192]{1,0:T(8,128)} %constant.26.clone.tab) | copy-start | bytes 147460
  84.5 68.4 %copy-start.6 = (f32[64,64]{1,0:T(8,128)S(1)}, f32[64,64]{1,0:T(8,128)}, u32[]{:S(2)}) copy-start(f32[64,64]{1,0:T(8,128)} %skip.1) | copy-start | bytes 49156
  84.5 68.4 %copy-start.8 = (f32[64]{0:T(128)S(1)}, f32[64]{0:T(128)}, u32[]{:S(2)}) copy-start(f32[64]{0:T(128)} %param.29) | copy-start | bytes 772

commit v9 on v8

--- a/solution.py
+++ b/solution.py
@@ -417,9 +417,8 @@
             out[x] = pack(l)
 
 
-def z_modes(table, pair):
+def z_modes(d):
     lane = lax.broadcasted_iota(jnp.int32, (MODES, HALVES), 1)
-    d = mm(table, pair, NT, HIGH)
     re, im = d[0:MODES], d[MODES:]
     return jnp.where(lane < CH, re, swap(im)), jnp.where(lane < CH, swap(re), im)
 
@@ -429,19 +428,21 @@
     last_pen = at[1] == last
     table = tabz[...]
     for x in range(CX):
-        for yp in range(CY // 2):
-            i = x * CY + 2 * yp
-            for j in range(2):
-                y = 2 * yp + j + 1
+        for yq in range(CY // 4):
+            i = x * CY + 4 * yq
+            for j in range(4):
+                y = 4 * yq + j + 1
                 l = rest[x, y]
                 if y == 1:
                     l = l + unpack(jnp.where(first_pen, low_y[x], left[x]))
                 if y == CY:
                     l = l + unpack(jnp.where(last_pen, high_y[x], right[x]))
                 own[i + j] = l
-            u, v = z_modes(table, own[i:i + 2].reshape(2 * CH, NZ))
-            spec[:, i, :] = u
-            spec[:, i + 1, :] = v
+            d = mm(table, own[i:i + 4].reshape(4 * CH, NZ), NT, HIGH)
+            for j in (0, 2):
+                u, v = z_modes(d[:, j * CH:(j + 2) * CH])
+                spec[:, i + j, :] = u
+                spec[:, i + j + 1, :] = v
 
 
 def y_kernel(r, main, out):

time: 156 us -> 156 us (level)
  transfers between devices with their start and end apart: 4 -> 4, of which waited for: 1 -> 1; matrix products, arithmetic and copies ran while one was open for 0% -> 0% of each run, Pallas kernels for 6% -> 7%
where the time goes in v9:
time: 156 us; the launch traced here: 155 us
  blocking collectives  109 us (70%)
  Pallas kernels  34.8 us (22%)
  starting transfers between devices  10.5 us (7%)
    all_to_all x4, blocking collectives, exchange(): return lax.all_to_all(x, axis, split_axis=0, concat_axis=0, tiled=True)  109 us
    pallas_call x1, Pallas kernels, lift_points(): pl.pallas_call(functools.partial(sides_kernel, last), out_shape=[shape(CX...  16.6 us
    ppermute x4, starting transfers between devices, moved(): lax.ppermute(x, axis, [(i - step, i) for i in devices if i - step in devi...  10.5 us
    pallas_call x2, Pallas kernels, lift_inner(): pl.pallas_call(functools.partial(middle_kernel, last), out_shape=shape(CX...  10.2 us
    pallas_call x5, Pallas kernels, call(): pl.pallas_call(kernel, out_shape=shapes, in_specs=specs, scratch_shapes=l...  4.87 us
    pallas_call x1, Pallas kernels, finish(): pl.pallas_call(final_kernel, out_shape=cells, in_specs=[pl.BlockSpec(memo...  3.17 us
  transfers between devices with their start and end apart: 4, of which 1 were waited for; matrix products, arithmetic and copies ran while one was open for 0% of the time, Pallas kernels for 7%

profile of v9, /device:TPU:32, one launch (start us, length us, event | category | flops | bytes accessed | tf_op | source)
XLA Modules:
  0.0 154.8 jit_solution(10899308712663415920)
XLA Ops:
  0.0 0.1 pad_add_fusion.at
  0.1 16.6 %lift_sides.1 = (f32[6,10,64,192]{3,2,1,0:T(8,128)S(1)}, f32[10,96,128]{2,1,0:T(8,128)S(1)}, f32[10,96,128]{2,1,0:T(8,128)S(1)}, bf16[112,2048]{1,0:T(8,128)(2,1...) custom-call(s32[2]{0:T(128)S(1)} %pad_add_fusion.at, ...), custom_call_target="tpu_custom_call" | custom-call | tf_op jit(solution)/shard_map/lift_sides/pallas_call | solution.py:366
  16.6 2.6 %collective-permute-start = (f32[10,96,128]{2,1,0:T(8,128)S(1)}, f32[10,96,128]{2,1,0:T(8,128)S(1)}, u32[]{:S(2)}, u32[]{:S(2)}) collective-permute-start(f32[10,96,128]{2,1,0:T(8,128)S(1)} %get-tuple-element.27), channel_id=1, source_target_pairs={{0,16},{16,32},{32,48},{48,64},{64,80},{80,96},{96,112},{112,128},... | collective-permute-start | bytes 1474568 | tf_op jit(solution)/shard_map/ppermute | solution.py:553
  19.3 1.3 collective-permute-start.1
  20.6 6.3 %lift_ends.1.refs_1_.middle = f32[4,10,64,192]{3,2,1,0:T(8,128)S(1)} custom-call(s32[2]{0:T(128)S(1)} %pad_add_fusion.at, s32[2]{0:T(128)S(1)} %get-tuple-element.26.span, bf16[112,2048]{1,0:T(8,128)(2,1)S(1)} %get-tuple-element.20.data, s32[2048,128]{1,0:T(8,128)S(1)} %get-tuple-element.21.rankb, f32[4,64,512]{2,1,0:T(8,128)S(1)} %get-tuple-element.22.taps, ...), custom_call_target="tpu_custom_call" | custom-call | tf_op jit(solution)/shard_map/lift_ends/pallas_call | solution.py:393
  26.8 0.0 collective-permute-done.refs_2_.below
  26.9 0.0 collective-permute-done.1.refs_3_.above
  26.9 0.7 y_ends.1
  27.6 3.0 %collective-permute-start.2 = (f32[4,96,128]{2,1,0:T(8,128)S(1)}, f32[4,96,128]{2,1,0:T(8,128)S(1)}, u32[]{:S(2)}, u32[]{:S(2)}) collective-permute-start(f32[4,96,128]{2,1,0:T(8,128)S(1)} %get-tuple-element.30.high_y), channel_id=1, source_target_pairs={{0,1},{1,2},{2,3},{3,4},{4,5},{5,6},{6,7},{7,8},{8,9},{9,10},{10,1... | collective-permute-start | bytes 589832 | tf_op jit(solution)/shard_map/ppermute | solution.py:553
  30.6 3.6 %collective-permute-start.3 = (f32[4,96,128]{2,1,0:T(8,128)S(1)}, f32[4,96,128]{2,1,0:T(8,128)S(1)}, u32[]{:S(2)}, u32[]{:S(2)}) collective-permute-start(f32[4,96,128]{2,1,0:T(8,128)S(1)} %get-tuple-element.29.low_y), channel_id=1, source_target_pairs={{1,0},{2,1},{3,2},{4,3},{5,4},{6,5},{7,6},{8,7},{9,8},{10,9},{11,1... | collective-permute-start | bytes 589832 | tf_op jit(solution)/shard_map/ppermute | solution.py:553
  34.2 0.0 copy-start.5
  34.2 4.0 %lift_core.1.rest = f32[4,10,64,192]{3,2,1,0:T(8,128)S(1)} custom-call(s32[2]{0:T(128)S(1)} %pad_add_fusion.at, s32[2]{0:T(128)S(1)} %get-tuple-element.19.span, bf16[112,2048]{1,0:T(8,128)(2,1)S(1)} %get-tuple-element.20.data, s32[2048,128]{1,0:T(8,128)S(1)} %get-tuple-element.21.rankb, f32[4,64,512]{2,1,0:T(8,128)S(1)} %get-tuple-element.22.taps, ...), custom_call_target="tpu_custom_call" | custom-call | tf_op jit(solution)/shard_map/lift_core/pallas_call | solution.py:393
  38.2 0.0 copy-start.7
  38.2 0.0 copy-start
  38.2 0.0 copy-start.1
  38.2 0.0 copy-start.3
  38.2 0.0 collective-permute-done.2.left
  38.2 0.3 collective-permute-done.3.right
  38.5 0.0 copy-done.5
  38.5 1.8 %latent_z.1 = (f32[32,32,128]{2,1,0:T(8,128)S(1)}, f32[32,64,192]{2,1,0:T(8,128)S(1)}) custom-call(s32[2]{0:T(128)S(1)} %pad_add_fusion.at, f32[64,192]{1,0:T(8,128)S(1)} %copy-done.5, f32[4,10,64,192]{3,2,1,0:T(8,128)S(1)} %lift_core.1.rest, f32[4,96,128]{2,1,0:T(8,128)S(1)} %get-tuple-element.29.low_y, f32[4,96,128]{2,1,0:T(8,128)S(1)} %get-tuple-element.30.high_y, ...), custom_call_target="tpu_custom_call" | custom-call | tf_op jit(solution)/shard_map/latent_z/pallas_call | solution.py:533
  40.3 0.0 copy-start.2
  40.3 39.1 %all_to_all.20.r = f32[16,64,128]{2,1,0:T(8,128)S(1)} all-to-all(f32[16,64,128]{2,1,0:T(8,128)S(1)} %bitcast.11), channel_id=1, replica_groups=mesh['bin'=32,'pen'=16] {'pen'}, dimensions={0} | all-to-all | bytes 1048576 | tf_op jit(solution)/shard_map/all_to_all | solution.py:548
  79.4 0.0 copy-done.7
  79.4 0.4 forward_y.1
  79.9 23.3 %all_to_all.21.r = f32[32,8,128]{2,1,0:T(8,128)S(1)} all-to-all(f32[32,8,128]{2,1,0:T(8,128)S(1)} %forward_y.1), channel_id=1, replica_groups=mesh['bin'=32,'pen'=16] {'bin'}, dimensions={0} | all-to-all | bytes 262144 | tf_op jit(solution)/shard_map/all_to_all | solution.py:548
  103.2 0.0 copy-done
  103.2 0.0 copy-done.1
  103.2 1.3 mix_x.1
  104.5 11.3 %all_to_all.22.r = f32[32,8,128]{2,1,0:T(8,128)S(1)} all-to-all(f32[32,8,128]{2,1,0:T(8,128)S(1)} %mix_x.1), channel_id=1, replica_groups=mesh['bin'=32,'pen'=16] {'bin'}, dimensions={0} | all-to-all | bytes 262144 | tf_op jit(solution)/shard_map/all_to_all | solution.py:548
  115.7 0.7 inverse_y.1
  116.4 35.1 %all_to_all.23 = f32[16,64,128]{2,1,0:T(8,128)S(1)} all-to-all(f32[16,64,128]{2,1,0:T(8,128)S(1)} %inverse_y.1), channel_id=1, replica_groups=mesh['bin'=32,'pen'=16] {'pen'}, dimensions={0} | all-to-all | bytes 1048576 | tf_op jit(solution)/shard_map/all_to_all | solution.py:548
  151.5 3.2 %finish.1 = bf16[4,8,64,192]{3,2,1,0:T(8,128)(2,1)} custom-call(f32[32,32,128]{2,1,0:T(8,128)S(1)} %bitcast.10, f32[64,192]{1,0:T(8,128)S(1)} %copy-done.4, f32[32,64,192]{2,1,0:T(8,128)S(1)} %get-tuple-element.32.own, f32[64,64]{1,0:T(8,128)S(1)} %copy-done.6, f32[1,64]{1,0:T(1,128)S(1)} %bitcast.12), custom_call_target="tpu_custom_call" | custom-call | tf_op jit(solution)/shard_map/finish/pallas_call | solution.py:518
  (8 shorter events, 0.0 us)
Async XLA Ops:
  16.6 10.2 %collective-permute-start = (f32[10,96,128]{2,1,0:T(8,128)S(1)}, f32[10,96,128]{2,1,0:T(8,128)S(1)}, u32[]{:S(2)}, u32[]{:S(2)}) collective-permute-start(f32[10,96,128]{2,1,0:T(8,128)S(1)} %get-tuple-element.27), channel_id=1, source_target_pairs={{0,16},{16,32},{32,48},{48,64},{64,80},{80,96},{96,112},{112,128},... | collective-permute-start | bytes 1474568 | tf_op jit(solution)/shard_map/ppermute | solution.py:553
  19.3 7.6 %collective-permute-start.1 = (f32[10,96,128]{2,1,0:T(8,128)S(1)}, f32[10,96,128]{2,1,0:T(8,128)S(1)}, u32[]{:S(2)}, u32[]{:S(2)}) collective-permute-start(f32[10,96,128]{2,1,0:T(8,128)S(1)} %get-tuple-element.28), channel_id=1, source_target_pairs={{16,0},{32,16},{48,32},{64,48},{80,64},{96,80},{112,96},{128,112},... | collective-permute-start | bytes 1474568 | tf_op jit(solution)/shard_map/ppermute | solution.py:553
  27.6 10.6 %collective-permute-start.2 = (f32[4,96,128]{2,1,0:T(8,128)S(1)}, f32[4,96,128]{2,1,0:T(8,128)S(1)}, u32[]{:S(2)}, u32[]{:S(2)}) collective-permute-start(f32[4,96,128]{2,1,0:T(8,128)S(1)} %get-tuple-element.30.high_y), channel_id=1, source_target_pairs={{0,1},{1,2},{2,3},{3,4},{4,5},{5,6},{6,7},{7,8},{8,9},{9,10},{10,1... | collective-permute-start | bytes 589832 | tf_op jit(solution)/shard_map/ppermute | solution.py:553
  30.6 7.9 %collective-permute-start.3 = (f32[4,96,128]{2,1,0:T(8,128)S(1)}, f32[4,96,128]{2,1,0:T(8,128)S(1)}, u32[]{:S(2)}, u32[]{:S(2)}) collective-permute-start(f32[4,96,128]{2,1,0:T(8,128)S(1)} %get-tuple-element.29.low_y), channel_id=1, source_target_pairs={{1,0},{2,1},{3,2},{4,3},{5,4},{6,5},{7,6},{8,7},{9,8},{10,9},{11,1... | collective-permute-start | bytes 589832 | tf_op jit(solution)/shard_map/ppermute | solution.py:553
  34.2 4.3 %copy-start.5 = (f32[64,192]{1,0:T(8,128)S(1)}, f32[64,192]{1,0:T(8,128)}, u32[]{:S(2)}) copy-start(f32[64,192]{1,0:T(8,128)} %constant.21.clone.tabz) | copy-start | bytes 147460
  38.2 41.3 %copy-start.7 = (f32[64,128]{1,0:T(8,128)S(1)}, f32[64,128]{1,0:T(8,128)}, u32[]{:S(2)}) copy-start(f32[64,128]{1,0:T(8,128)} %constant.22.clone.main) | copy-start | bytes 98308
  38.2 65.0 %copy-start = (bf16[32,1,2,64,128]{4,3,2,1,0:T(8,128)(2,1)S(1)}, bf16[32,1,2,64,128]{4,3,2,1,0:T(8,128)(2,1)}, u32[]{:S(2)}) copy-start(bf16[32,1,2,64,128]{4,3,2,1,0:T(8,128)(2,1)} %w.1) | copy-start | bytes 3145732
  38.2 65.0 %copy-start.1 = (f32[512,64]{1,0:T(8,128)S(1)}, f32[512,64]{1,0:T(8,128)}, u32[]{:S(2)}) copy-start(f32[512,64]{1,0:T(8,128)} %constant.24.clone.inv) | copy-start | bytes 393220
  38.2 65.0 %copy-start.3 = (f32[128,256]{1,0:T(8,128)S(1)}, f32[128,256]{1,0:T(8,128)}, u32[]{:S(2)}) copy-start(f32[128,256]{1,0:T(8,128)} %constant.23.clone.fwd) | copy-start | bytes 393220
  40.3 75.4 %copy-start.2 = (f32[256,32]{1,0:T(8,128)S(1)}, f32[256,32]{1,0:T(8,128)}, u32[]{:S(2)}) copy-start(f32[256,32]{1,0:T(8,128)} %constant.25.clone.inv) | copy-start | bytes 98308
  79.4 72.0 %copy-start.4 = (f32[64,192]{1,0:T(8,128)S(1)}, f32[64,192]{1,0:T(8,128)}, u32[]{:S(2)}) copy-start(f32[64,192]{1,0:T(8,128)} %constant.26.clone.tab) | copy-start | bytes 147460
  79.4 72.0 %copy-start.6 = (f32[64,64]{1,0:T(8,128)S(1)}, f32[64,64]{1,0:T(8,128)}, u32[]{:S(2)}) copy-start(f32[64,64]{1,0:T(8,128)} %skip.1) | copy-start | bytes 49156
  79.4 72.0 %copy-start.8 = (f32[64]{0:T(128)S(1)}, f32[64]{0:T(128)}, u32[]{:S(2)}) copy-start(f32[64]{0:T(128)} %param.29) | copy-start | bytes 772
